TPU v7x, 256 devices: a whole 4x4x8 slice. The times are simulated.
256 devices in a mesh: dp: 16 (over z, y_lo), mp: 16 (over x, y_hi, core).
Axes of the slice: x: 4, y: 4 (y_hi: 2, y_lo: 2; y = y_hi * 2 + y_lo), z: 8, core: 2. Of those that a mesh axis runs over, the one named last changes fastest.
Arguments:
- query_acts: bfloat16 [16, 32, 4096], P('dp', None, 'mp'), may hold values from -6 to 6
- query_grads: bfloat16 [16, 32, 28672], P('dp', None, 'mp'), may hold values from -6 to 6
- train_acts: bfloat16 [16, 32, 4096], P('dp', None, 'mp'), may hold values from -6 to 6
- train_grads: bfloat16 [16, 32, 28672], P('dp', None, 'mp'), may hold values from -6 to 6
- basis_in: bfloat16 [4096, 4096], P('dp', 'mp'), may hold values from -0.09375 to 0.09375
- basis_out: bfloat16 [28672, 28672], P('mp', 'dp'), may hold values from -0.03125 to 0.03125
- eigen: float32 [28672, 4096], P('dp', 'mp'), may hold values from 0.05 to 2
Outputs:
- scores: float32 [16, 16], replicated
All inputs are finite; a program needn't handle non-finite values.
Results may differ from a plain program's by a relative error of at most 0.0049.
Values may be sent and summed in bfloat16 or wider, within the bound.
No kernel may reach another device: no remote copies, remote signals or barrier semaphores. Data moves between devices by JAX's collectives and lax.ppermute only.
A program may use at most 128 MiB of HBM per device.

v0:
```python
import jax
import jax.numpy as jnp
from jax import lax
from jax.sharding import PartitionSpec as P

IN = 4096
OUT = 28672
TS = 32
TQ = 32


damping = 0.1


def shards(query_acts, query_grads, train_acts, train_grads, basis_in, basis_out, eigen):
    n_query, query_len, in_local = query_acts.shape
    n_train, train_len, _ = train_acts.shape
    grad_local = query_grads.shape[2]
    activations = jnp.concatenate(
        [
            query_acts.reshape(n_query * query_len, in_local),
            train_acts.reshape(n_train * train_len, in_local),
        ],
        0,
    )
    gradients = jnp.concatenate(
        [
            query_grads.reshape(n_query * query_len, grad_local),
            train_grads.reshape(n_train * train_len, grad_local),
        ],
        0,
    )
    group_rows = activations.shape[0]
    full_acts = lax.all_gather(activations, "mp", axis=1, tiled=True)
    turned_acts = jnp.dot(
        full_acts,
        lax.all_gather(basis_in, "dp", axis=0, tiled=True),
        preferred_element_type=jnp.float32,
    )
    all_acts = lax.all_gather(turned_acts.astype(jnp.bfloat16), "dp", axis=0, tiled=True)
    partial_grads = jnp.dot(
        lax.all_gather(gradients, "dp", axis=0, tiled=True),
        basis_out,
        preferred_element_type=jnp.float32,
    )
    shares = lax.psum_scatter(partial_grads, "mp", scatter_dimension=1, tiled=True)
    all_grads = lax.all_gather(shares.astype(jnp.bfloat16), "mp", axis=1, tiled=True)
    out_block = all_grads.shape[1]
    groups = all_acts.shape[0] // group_rows
    query_rows = n_query * query_len
    act_groups = all_acts.reshape(groups, group_rows, in_local)
    grad_groups = all_grads.reshape(groups, group_rows, out_block)
    query_act_all = act_groups[:, :query_rows].reshape(
        groups * n_query // 4, 4, query_len, in_local
    )
    query_grad_all = grad_groups[:, :query_rows].reshape(
        groups * n_query // 4, 4, query_len, out_block
    )
    train_act_all = act_groups[:, query_rows:].reshape(
        groups * n_train // 4, 4, train_len, in_local
    )
    train_grad_all = grad_groups[:, query_rows:].reshape(
        groups * n_train // 4, 4, train_len, out_block
    )
    denominator = eigen + damping

    def precondition(paired):
        grad_block, act_block = paired
        outer_sum = jnp.einsum(
            "ntd,nte->nde", grad_block, act_block, preferred_element_type=jnp.float32
        )
        return (outer_sum / denominator).astype(jnp.bfloat16)

    precond = lax.map(precondition, (query_grad_all, query_act_all)).reshape(
        groups * n_query, out_block * in_local
    )

    def score_block(paired):
        grad_block, act_block = paired
        dense = jnp.einsum(
            "std,ste->sde", grad_block, act_block, preferred_element_type=jnp.float32
        ).astype(jnp.bfloat16)
        return jnp.einsum(
            "nk,sk->ns",
            precond,
            dense.reshape(dense.shape[0], out_block * in_local),
            preferred_element_type=jnp.float32,
        )

    blocked = lax.map(score_block, (train_grad_all, train_act_all))
    normalizer = float(TQ * TS * IN * OUT) ** (-0.5)
    partial_scores = (
        jnp.transpose(blocked, (1, 0, 2)).reshape(groups * n_query, groups * n_train) * normalizer
    )
    return lax.psum(partial_scores, ("dp", "mp"))


def solution(mesh):
    placed = (
        P("dp", None, "mp"),
        P("dp", None, "mp"),
        P("dp", None, "mp"),
        P("dp", None, "mp"),
        P("dp", "mp"),
        P("mp", "dp"),
        P("dp", "mp"),
    )
    return jax.shard_map(shards, mesh=mesh, in_specs=placed, out_specs=P(), check_vma=False)
```

profile of v0, /device:TPU:1, one launch (start us, length us, event | category | flops | bytes accessed | tf_op | source)
XLA Modules:
  0.0 594.7 jit_solution(1546297397435642076)
XLA Ops:
  6.5 1.7 pad_maximum_fusion
  8.3 91.9 %all-gather.4.cloned.1.call-done = bf16[1024,1792]{1,0:T(8,128)(2,1)} async-done(((bf16[64,1792]{1,0:T(8,128)(2,1)}), bf16[1024,1792]{1,0:T(8,128)(2,1)}) %all-gather.4.cloned.1.call-update) | async-done | bytes 3670032 | tf_op jit(solution)/shard_map/all_gather | solution.py:42
  100.2 12.3 %fusion.14 = f32[1024,1792]{0,1:T(8,128)} fusion(bf16[1024,1792]{1,0:T(8,128)(2,1)} %all-gather.4.cloned.1.call-done, bf16[1792,1792]{1,0:T(8,128)(2,1)} %param.16), kind=kOutput, calls=%fused_computation.23 | convolution fusion | flops 6576668672 | bytes 17432576 | tf_op jit(solution)/shard_map/dot_general | solution.py:41
  113.4 101.8 %reduce-scatter.2.cloned.1.call-done = f32[1024,112]{0,1:T(8,128)} async-done(((f32[1024,1792]{0,1:T(8,128)}), f32[1024,112]{0,1:T(8,128)}) %reduce-scatter.2.cloned.1.call-update) | async-done | bytes 458768 | tf_op jit(solution)/shard_map/reduce_scatter | solution.py:46
  215.2 1.7 convert_element_type.12
  217.0 24.9 %all_gather.17 = bf16[64,4096]{1,0:T(8,128)(2,1)S(1)} all-gather(bf16[64,256]{1,0:T(8,128)(2,1)S(1)} %pad_maximum_fusion.1), channel_id=1, replica_groups=mesh['dp'=16,'mp'=16] {'mp'}, dimensions={1}, use_global_device_ids=true | all-gather | bytes 557056 | tf_op jit(solution)/shard_map/all_gather | solution.py:34
  241.9 1.5 broadcast_add_fusion
  243.4 37.9 %all-gather.8.cloned.1.call-done = bf16[4096,256]{1,0:T(8,128)(2,1)} async-done(((bf16[256,256]{1,0:T(8,128)(2,1)}), bf16[4096,256]{1,0:T(8,128)(2,1)}) %all-gather.8.cloned.1.call-update) | async-done | bytes 2097168 | tf_op jit(solution)/shard_map/all_gather | solution.py:37
  281.3 2.1 convolution_convert_fusion.1
  283.3 27.7 %all_gather.19 = bf16[1024,256]{1,0:T(8,128)(2,1)S(1)} all-gather(bf16[64,256]{1,0:T(8,128)(2,1)S(1)} %convolution_convert_fusion.1), channel_id=1, replica_groups=mesh['dp'=16,'mp'=16] {'dp'}, dimensions={0}, use_global_device_ids=true | all-gather | bytes 557056 | tf_op jit(solution)/shard_map/all_gather | solution.py:40
  311.0 43.4 %all-gather.6.cloned.1.call-done = bf16[1024,1792]{0,1:T(8,128)(2,1)} async-done(((bf16[1024,112]{0,1:T(8,128)(2,1)}), bf16[1024,1792]{0,1:T(8,128)(2,1)}) %all-gather.6.cloned.1.call-update) | async-done | bytes 3670032 | tf_op jit(solution)/shard_map/all_gather | solution.py:47
  354.5 5.9 copy.11
  360.4 3.6 fusion.12
  363.9 18.7 %while.20 = (s32[]{:T(128)}, bf16[4,4,1792,256]{3,2,1,0:T(8,128)(2,1)}, bf16[4,4,32,1792]{3,2,1,0:T(8,128)(2,1)}, bf16[4,4,32,256]{3,2,1,0:T(8,128)(2,1)S(1)}, f32[1792,256]{1,0:T(8,128)}, /*index=5*/s32[]{:T(128)}) while((s32[]{:T(128)}, bf16[4,4,1792,256]{3,2,1,0:T(8,128)(2,1)}, bf16[4,4,32,1792]{3,2,1,0:T(8,128)(2,1)}, ...), condition=%wide.region_2.3_spmd, body=%wide.region_1.2_spmd.sunk | while | flops 121110528 | bytes 6030917 | solution.py:74
  363.9 4.6 bitcast_dynamic-update-slice_fusion.2
  368.6 4.7 bitcast_dynamic-update-slice_fusion.2
  373.2 4.7 bitcast_dynamic-update-slice_fusion.2
  377.9 4.7 bitcast_dynamic-update-slice_fusion.2
  382.6 15.9 %copy.14 = bf16[2,8,1792,256]{3,1,2,0:T(8,128)(2,1)} copy(bf16[2,8,1792,256]{3,2,1,0:T(8,128)(2,1)} %bitcast.67) | data formatting | bytes 29360128
  398.6 113.1 %while.21 = (s32[]{:T(128)}, f32[4,16,4]{1,2,0:T(4,128)S(1)}, bf16[4,4,32,1792]{3,2,1,0:T(8,128)(2,1)S(1)}, bf16[4,4,32,256]{3,2,1,0:T(8,128)(2,1)S(1)}, bf16[16,458752]{1,0:T(8,128)(2,1)}, /*index=5*/s32[]{:T(128)}) while((s32[]{:T(128)}, f32[4,16,4]{1,2,0:T(4,128)S(1)}, bf16[4,4,32,1792]{3,2,1,0:T(8,128)(2,1)S(1)}, ...), condition=%wide.region_4.5_spmd, body=%wide.region_3.4_spmd.sunk | while | flops 177995776 | bytes 29887560 | solution.py:90
  399.7 15.2 %copy.16 = bf16[1,4,1792,256]{3,1,2,0:T(4,128)(2,1)} copy(bf16[1,4,1792,256]{3,2,1,0:T(8,128)(2,1)S(1)} %fusion.35) | data formatting | bytes 7340032 | tf_op jit(solution)/shard_map/while
  415.0 11.9 %fusion.36 = f32[4,16,4]{1,2,0:T(4,128)S(1)} fusion(f32[4,16,4]{1,2,0:T(4,128)S(1)} %get-tuple-element.172, s32[]{:T(128)} %get-tuple-element.171, bf16[4,458752]{1,0:T(4,128)(2,1)} %bitcast.65, bf16[16,458752]{1,0:T(8,128)(2,1)} %get-tuple-element.181), kind=kOutput, calls=%fused_computation.10.clone.1 | convolution fusion | flops 58720256 | bytes 18352132 | tf_op jit(solution)/shard_map/while/body/eval_jaxpr/nk,sk->ns/dot_general | solution.py:83
  426.8 1.2 fusion.35
  428.0 15.2 %copy.16 = bf16[1,4,1792,256]{3,1,2,0:T(4,128)(2,1)} copy(bf16[1,4,1792,256]{3,2,1,0:T(8,128)(2,1)S(1)} %fusion.35) | data formatting | bytes 7340032 | tf_op jit(solution)/shard_map/while
  443.3 11.9 %fusion.36 = f32[4,16,4]{1,2,0:T(4,128)S(1)} fusion(f32[4,16,4]{1,2,0:T(4,128)S(1)} %get-tuple-element.172, s32[]{:T(128)} %get-tuple-element.171, bf16[4,458752]{1,0:T(4,128)(2,1)} %bitcast.65, bf16[16,458752]{1,0:T(8,128)(2,1)} %get-tuple-element.181), kind=kOutput, calls=%fused_computation.10.clone.1 | convolution fusion | flops 58720256 | bytes 18352132 | tf_op jit(solution)/shard_map/while/body/eval_jaxpr/nk,sk->ns/dot_general | solution.py:83
  455.1 1.2 fusion.35
  456.3 15.2 %copy.16 = bf16[1,4,1792,256]{3,1,2,0:T(4,128)(2,1)} copy(bf16[1,4,1792,256]{3,2,1,0:T(8,128)(2,1)S(1)} %fusion.35) | data formatting | bytes 7340032 | tf_op jit(solution)/shard_map/while
  471.6 11.9 %fusion.36 = f32[4,16,4]{1,2,0:T(4,128)S(1)} fusion(f32[4,16,4]{1,2,0:T(4,128)S(1)} %get-tuple-element.172, s32[]{:T(128)} %get-tuple-element.171, bf16[4,458752]{1,0:T(4,128)(2,1)} %bitcast.65, bf16[16,458752]{1,0:T(8,128)(2,1)} %get-tuple-element.181), kind=kOutput, calls=%fused_computation.10.clone.1 | convolution fusion | flops 58720256 | bytes 18352132 | tf_op jit(solution)/shard_map/while/body/eval_jaxpr/nk,sk->ns/dot_general | solution.py:83
  483.4 1.2 fusion.35
  484.6 15.2 %copy.16 = bf16[1,4,1792,256]{3,1,2,0:T(4,128)(2,1)} copy(bf16[1,4,1792,256]{3,2,1,0:T(8,128)(2,1)S(1)} %fusion.35) | data formatting | bytes 7340032 | tf_op jit(solution)/shard_map/while
  499.8 11.9 %fusion.36 = f32[4,16,4]{1,2,0:T(4,128)S(1)} fusion(f32[4,16,4]{1,2,0:T(4,128)S(1)} %get-tuple-element.172, s32[]{:T(128)} %get-tuple-element.171, bf16[4,458752]{1,0:T(4,128)(2,1)} %bitcast.65, bf16[16,458752]{1,0:T(8,128)(2,1)} %get-tuple-element.181), kind=kOutput, calls=%fused_computation.10.clone.1 | convolution fusion | flops 58720256 | bytes 18352132 | tf_op jit(solution)/shard_map/while/body/eval_jaxpr/nk,sk->ns/dot_general | solution.py:83
  511.7 75.8 %psum.7 = f32[16,16]{0,1:T(8,128)S(1)} all-reduce(f32[16,16]{0,1:T(8,128)S(1)} %bitcast.76), channel_id=1, replica_groups=mesh['dp'=16,'mp'=16] {'dp','mp'}, use_global_device_ids=true, to_apply=%region_5.6 | all-reduce | flops 256 | bytes 2048 | tf_op jit(solution)/shard_map/psum | solution.py:95
  (21 shorter events, 2.7 us)
Async XLA Ops:
  6.5 93.7 %all-gather.4.cloned.1.call-start = ((), (), s32[]{:S(2)}) async-start(), calls=%async_computation.1 | async-start | bytes 3899392 | tf_op jit(solution)/shard_map/all_gather | solution.py:42
  8.2 207.0 %reduce-scatter.2.cloned.1.call-start = ((), (), s32[]{:S(2)}) async-start(), calls=%async_computation.2 | async-start | bytes 7798784 | tf_op jit(solution)/shard_map/reduce_scatter | solution.py:46
  112.6 104.4 %copy-start.1 = (bf16[1,32,256]{2,1,0:T(8,128)(2,1)S(1)}, bf16[1,32,256]{2,1,0:T(8,128)(2,1)}, u32[]{:S(2)}) copy-start(bf16[1,32,256]{2,1,0:T(8,128)(2,1)} %param.13) | copy-start | bytes 49156
  112.6 104.5 %copy-start.2 = (bf16[1,32,256]{2,1,0:T(8,128)(2,1)S(1)}, bf16[1,32,256]{2,1,0:T(8,128)(2,1)}, u32[]{:S(2)}) copy-start(bf16[1,32,256]{2,1,0:T(8,128)(2,1)} %param.11) | copy-start | bytes 49156
  112.6 129.3 %copy-start = (f32[1792,256]{1,0:T(8,128)S(1)}, f32[1792,256]{1,0:T(8,128)}, u32[]{:S(2)}) copy-start(f32[1792,256]{1,0:T(8,128)} %param.17) | copy-start | bytes 5505028
  112.6 168.7 %all-gather.8.cloned.1.call-start = ((), (), s32[]{:S(2)}) async-start(), calls=%async_computation.4 | async-start | bytes 2228224 | tf_op jit(solution)/shard_map/all_gather | solution.py:37
  113.3 241.1 %all-gather.6.cloned.1.call-start = ((), (), s32[]{:S(2)}) async-start(), calls=%async_computation.3 | async-start | bytes 3899392 | tf_op jit(solution)/shard_map/all_gather | solution.py:47
Sparse Core Ops, SparseCore 0:
  9.1 91.0 all-gather.3
  112.7 102.4 reduce-scatter.1
  217.2 64.0 all-gather.7
  284.2 70.2 all-gather.5
where the time goes:
time: 595 us
  waiting for transfers between devices  276 us (46%)
  blocking collectives  128 us (22%)
  local copies, waits for them, and re-layouts  87.1 us (15%)
  matrix products  85.3 us (14%)
  between operations  13.2 us (2%)
    reduce_scatter x1, waiting for transfers between devices, shards(): lax.psum_scatter(partial_grads, 'mp', scatter_dimension=1, tiled=True)  102 us
    all_gather x1, waiting for transfers between devices, shards(): lax.all_gather(gradients, 'dp', axis=0, tiled=True)  91.9 us
    psum x1, blocking collectives, shards(): return lax.psum(partial_scores, ('dp', 'mp'))  75.8 us
    while x4, local copies, waits for them, and re-layouts  60.9 us
    dot_general x4, matrix products, score_block(): jnp.einsum('nk,sk->ns', precond, dense.reshape(dense.shape[0], out_block...  47.5 us
    all_gather x1, waiting for transfers between devices, shards(): lax.all_gather(shares.astype(jnp.bfloat16), 'mp', axis=1, tiled=True)  43.4 us
    all_gather x1, waiting for transfers between devices, shards(): lax.all_gather(basis_in, 'dp', axis=0, tiled=True)  37.9 us
    all_gather x1, blocking collectives, shards(): lax.all_gather(turned_acts.astype(jnp.bfloat16), 'dp', axis=0, tiled=True)  27.7 us
  transfers between devices with their start and end apart: 4, of which 4 were waited for; matrix products, arithmetic and copies ran while one was open for 1% of the time, Pallas kernels for 0%

commit v1 on v0

v1 whole, which is shorter than its diff:
```python
import jax
import jax.numpy as jnp
from jax import lax
from jax.experimental import pallas as pl
from jax.experimental.pallas import tpu as pltpu
from jax.sharding import PartitionSpec as P

IN = 4096
OUT = 28672
TS = 32
TQ = 32

damping = 0.1

NZ, NYL, NX, NYH, NC = 8, 2, 4, 2, 2
GROUPS = NZ * NYL
CHIPS = NX * NYH


def dp_index(z, yl):
    return (z % NZ) * NYL + yl % NYL


def mp_index(x, yh, core):
    return ((x % NX) * NYH + yh % NYH) * NC + core % NC


def dp_shift(dz, dyl):
    return [
        (dp_index(z, y), dp_index(z + dz, y + dyl)) for z in range(NZ) for y in range(NYL)
    ]


CORE_SWAP = [
    (mp_index(x, h, c), mp_index(x, h, c + 1))
    for x in range(NX)
    for h in range(NYH)
    for c in range(NC)
]
TRANSPOSE = [(d * 16 + m, m * 16 + d) for d in range(16) for m in range(16)]
SAME_CORE = [
    [mp_index(x, h, c) for x in range(NX) for h in range(NYH)] for c in range(NC)
]

CHUNKS = (((0, 0), (0, 1), (1, 0), (-1, 0), (1, 1), (-1, 1),
           (2, 0), (-2, 0), (2, 1), (-2, 1), (3, 0), (-3, 0), (3, 1), (-3, 1), (4, 0), (4, 1)),)


def exchange(x, axis, **kw):
    return lax.all_to_all(x, axis, 0, 0, tiled=True, **kw)


def share(x, count, axis, **kw):
    return exchange(jnp.tile(x, (count, 1)), axis, **kw)


def ring_gather(own):
    held = {(0, 0): own}
    up = down = own
    for k in (1, 2, 3):
        up = lax.ppermute(up, "dp", dp_shift(-1, 0))
        down = lax.ppermute(down, "dp", dp_shift(1, 0))
        held[(k, 0)], held[(-k, 0)] = up, down
    half = own.shape[0] // 2
    held[(4, 0)] = jnp.concatenate(
        [
            lax.ppermute(up[:half], "dp", dp_shift(-1, 0)),
            lax.ppermute(down[half:], "dp", dp_shift(1, 0)),
        ],
        0,
    )
    across = dp_shift(0, 1)
    held[(0, 1)] = lax.ppermute(own, "dp", across)
    for k in (1, 2, 3):
        pair = lax.ppermute(
            jnp.concatenate([held[(k, 0)], held[(-k, 0)]], 0), "dp", across
        )
        held[(k, 1)], held[(-k, 1)] = pair[: own.shape[0]], pair[own.shape[0] :]
    held[(4, 1)] = lax.ppermute(held[(4, 0)], "dp", across)
    return held


def score_kernel(order_ref, place_ref, grads_ref, own_acts_ref, sib_acts_ref, own_inv_ref,
                 sib_inv_ref, out_ref, train_grads, query_acts, train_acts, sums):
    half = own_acts_ref.shape[1]
    rows = 2 * TQ
    for r in range(GROUPS):
        train_grads[r * TS : (r + 1) * TS, :] = grads_ref[r * rows + TQ : (r + 1) * rows, :]
        start = pl.multiple_of(order_ref[r] * rows, rows)
        middle = pl.multiple_of(start + TQ, TQ)
        for ref, at in ((own_acts_ref, 0), (sib_acts_ref, half)):
            query_acts[r * TQ : (r + 1) * TQ, at : at + half] = ref[pl.ds(start, TQ), :]
            train_acts[r * TS : (r + 1) * TS, at : at + half] = ref[
                pl.ds(middle, TS), :
            ].astype(jnp.float32)

    def one_query(n, carry):
        grads = grads_ref[pl.ds(pl.multiple_of(n * rows, rows), TQ), :]
        total = jnp.zeros((GROUPS, 128), jnp.float32)
        for at, inv_ref in ((0, own_inv_ref), (half, sib_inv_ref)):
            acts = query_acts[pl.ds(pl.multiple_of(n * TQ, TQ), TQ), at : at + half]
            gradient = lax.dot_general(
                grads, acts, (((0,), (0,)), ((), ())), preferred_element_type=jnp.float32
            )
            preconditioned = (gradient * inv_ref[...]).astype(jnp.bfloat16)
            projected = jnp.dot(
                train_grads[...], preconditioned, preferred_element_type=jnp.float32
            )
            terms = projected * train_acts[:, at : at + half]
            terms = terms.reshape(GROUPS, TS, half).sum(1)
            for lane in range(0, half, 128):
                total = total + terms[:, lane : lane + 128]
        sums[pl.ds(n, 1)] = total[None]
        return carry

    lax.fori_loop(0, GROUPS, one_query, 0)
    scores = jnp.sum(sums[...], axis=2)
    hot = place_ref[...]
    hot_t = jnp.transpose(hot)
    scores = jnp.dot(
        hot, jnp.dot(scores, hot_t, precision=lax.Precision.HIGHEST),
        precision=lax.Precision.HIGHEST,
    )
    out_ref[...] = jnp.concatenate(
        [scores, jnp.zeros((GROUPS, 128 - GROUPS), jnp.float32)], 1
    )


def score_blocks(order, place, grads, own_acts, sib_acts, own_inv, sib_inv):
    units, half = own_inv.shape
    vmem = pl.BlockSpec(memory_space=pltpu.VMEM)
    return pl.pallas_call(
        score_kernel,
        out_shape=jax.ShapeDtypeStruct((GROUPS, 128), jnp.float32),
        in_specs=[pl.BlockSpec(memory_space=pltpu.SMEM)] + [vmem] * 6,
        out_specs=vmem,
        scratch_shapes=[
            pltpu.VMEM((GROUPS * TS, units), jnp.bfloat16),
            pltpu.VMEM((GROUPS * TQ, 2 * half), jnp.bfloat16),
            pltpu.VMEM((GROUPS * TS, 2 * half), jnp.float32),
            pltpu.VMEM((GROUPS, GROUPS, 128), jnp.float32),
        ],
        compiler_params=pltpu.CompilerParams(vmem_limit_bytes=40 * 1024 * 1024),
        cost_estimate=pl.CostEstimate(
            flops=2 * GROUPS * units * 2 * half * (GROUPS * TS + TQ),
            bytes_accessed=8 * 1024 * 1024,
            transcendentals=0,
        ),
    )(order, place, grads, own_acts, sib_acts, own_inv, sib_inv)


def shards(query_acts, query_grads, train_acts, train_grads, basis_in, basis_out, eigen):
    in_local = query_acts.shape[2]
    out_local = query_grads.shape[2]
    rows = 2 * TQ
    acts = jnp.concatenate(
        [query_acts.reshape(TQ, in_local), train_acts.reshape(TS, in_local)], 0
    )
    grads = jnp.concatenate(
        [query_grads.reshape(TQ, out_local), train_grads.reshape(TS, out_local)], 0
    )
    dp = lax.axis_index("dp")
    core = lax.axis_index("mp") % NC
    half = out_local // 2
    own_at, sib_at = core * half, (1 - core) * half

    own_inv = 1.0 / (lax.dynamic_slice_in_dim(eigen, own_at, half, 0) + damping)
    sib_inv = 1.0 / (
        lax.ppermute(lax.dynamic_slice_in_dim(eigen, sib_at, half, 0), "mp", CORE_SWAP) + damping
    )
    own_basis = lax.dynamic_slice_in_dim(basis_out, own_at, half, 1)
    sib_basis = lax.dynamic_slice_in_dim(basis_out, sib_at, half, 1)

    moved = lax.ppermute(acts, ("dp", "mp"), TRANSPOSE)
    all_acts = share(moved, GROUPS, "mp")
    part_acts = jnp.dot(all_acts, basis_in, preferred_element_type=jnp.float32)
    own_rows = exchange(part_acts, "dp").reshape(GROUPS, rows, in_local).sum(0)
    own_acts = share(own_rows.astype(jnp.bfloat16), GROUPS, "dp")
    sib_acts = lax.ppermute(own_acts, "mp", CORE_SWAP)

    held = ring_gather(grads)
    turned = []
    for chunk in CHUNKS:
        tokens = jnp.concatenate([held[place] for place in chunk], 0)
        sib_part = jnp.dot(tokens, sib_basis, preferred_element_type=jnp.float32)
        got = lax.ppermute(sib_part.astype(jnp.bfloat16), "mp", CORE_SWAP)
        own_part = jnp.dot(tokens, own_basis, preferred_element_type=jnp.float32)
        pair = (own_part + got.astype(jnp.float32)).astype(jnp.bfloat16)
        parts = exchange(pair, "mp", axis_index_groups=SAME_CORE)
        summed = parts.reshape(CHIPS, -1, half).astype(jnp.float32).sum(0)
        turned.append(
            share(summed.astype(jnp.bfloat16), CHIPS, "mp", axis_index_groups=SAME_CORE)
        )
    all_grads = jnp.concatenate(turned, 0)

    places = [place for chunk in CHUNKS for place in chunk]
    dz = jnp.array([p[0] for p in places], jnp.int32)
    dy = jnp.array([p[1] for p in places], jnp.int32)
    order = ((dp // NYL + dz + NZ) % NZ) * NYL + (dp % NYL + dy) % NYL
    place = (order[None, :] == jnp.arange(GROUPS, dtype=jnp.int32)[:, None]).astype(jnp.float32)

    scores = score_blocks(order, place, all_grads, own_acts, sib_acts, own_inv, sib_inv)
    normalizer = float(TQ * TS * IN * OUT) ** (-0.5)
    scores = share(scores * normalizer, GROUPS, "mp").reshape(GROUPS, GROUPS, 128).sum(0)
    scores = share(scores, GROUPS, "dp").reshape(GROUPS, GROUPS, 128).sum(0)
    return scores[:, :GROUPS]


def solution(mesh):
    placed = (
        P("dp", None, "mp"),
        P("dp", None, "mp"),
        P("dp", None, "mp"),
        P("dp", None, "mp"),
        P("dp", "mp"),
        P("mp", "dp"),
        P("dp", "mp"),
    )
    return jax.shard_map(shards, mesh=mesh, in_specs=placed, out_specs=P(), check_vma=False)
```

time: 595 us -> 245 us (0.41)
  waiting for transfers between devices: 276 us -> 100 us
  blocking collectives: 128 us -> 27 us
  matrix products: 85.3 us -> 16.7 us
  local copies, waits for them, and re-layouts: 87.1 us -> 18.7 us
  starting transfers between devices: 0.12 us -> 57 us
  Pallas kernels: 0 us -> 16.8 us
  between operations: 13.2 us -> 0.19 us
    all_gather x3 -> x0, waiting for transfers between devices: 173 us -> none  [the longest x1 91.9 us: shards(): lax.all_gather(gradients, 'dp', axis=0, tiled=True)]
    reduce_scatter x1 -> x0, waiting for transfers between devices: 102 us -> none  [shards(): lax.psum_scatter(partial_grads, 'mp', scatter_dimension=1, tiled=True)]
    psum x1 -> x0, blocking collectives: 75.8 us -> none  [shards(): return lax.psum(partial_scores, ('dp', 'mp'))]
    all_to_all x0 -> x5, waiting for transfers between devices: none -> 73 us  [exchange(): return lax.all_to_all(x, axis, 0, 0, tiled=True, **kw)]
    dot_general x14 -> x3, matrix products: 85.3 us -> 16.7 us  [the longest x1 8.25 us: shards(): own_part = jnp.dot(tokens, own_basis, preferred_element_type=jnp.float32)]
    while x4 -> x0, local copies, waits for them, and re-layouts: 60.9 us -> none
    all_gather x2 -> x0, blocking collectives: 52.5 us -> none  [the longest x1 27.7 us: shards(): lax.all_gather(turned_acts.astype(jnp.bfloat16), 'dp', axis=0, tiled=True)]
    all_to_all x0 -> x5, starting transfers between devices: none -> 34 us  [exchange(): return lax.all_to_all(x, axis, 0, 0, tiled=True, **kw)]
  transfers between devices with their start and end apart: 4 -> 22, of which waited for: 4 -> 13; matrix products, arithmetic and copies ran while one was open for 1% -> 14% of each run, Pallas kernels for 0% -> 0%
where the time goes in v1:
time: 245 us; the launch traced here: 244 us
  waiting for transfers between devices  100 us (41%)
  starting transfers between devices  57 us (23%)
  blocking collectives  27 us (11%)
  local copies, waits for them, and re-layouts  18.7 us (8%)
  Pallas kernels  16.8 us (7%)
  matrix products  16.7 us (7%)
  other arithmetic  6.73 us (3%)
    all_to_all x5, waiting for transfers between devices, exchange(): return lax.all_to_all(x, axis, 0, 0, tiled=True, **kw)  73 us
    all_to_all x5, starting transfers between devices, exchange(): return lax.all_to_all(x, axis, 0, 0, tiled=True, **kw)  34 us
    all_to_all x2, blocking collectives, exchange(): return lax.all_to_all(x, axis, 0, 0, tiled=True, **kw)  27 us
    pallas_call x1, Pallas kernels, score_blocks(): pl.pallas_call(score_kernel, out_shape=jax.ShapeDtypeStruct((GROUPS, 128)...  16.8 us
    unnamed x28, local copies, waits for them, and re-layouts  14.8 us
    ppermute x3, waiting for transfers between devices, ring_gather(): lax.ppermute(jnp.concatenate([held[k, 0], held[-k, 0]], 0), 'dp', across)  11.6 us
    dot_general x1, matrix products, shards(): own_part = jnp.dot(tokens, own_basis, preferred_element_type=jnp.float32)  8.25 us
    ppermute x3, starting transfers between devices, ring_gather(): up = lax.ppermute(up, 'dp', dp_shift(-1, 0))  7.49 us
  transfers between devices with their start and end apart: 22, of which 13 were waited for; matrix products, arithmetic and copies ran while one was open for 14% of the time, Pallas kernels for 0%

profile of v1, /device:TPU:1, one launch (start us, length us, event | category | flops | bytes accessed | tf_op | source)
XLA Modules:
  0.0 243.6 jit_solution(4629740383963764520)
XLA Ops:
  1.0 6.5 %collective-permute-start.1 = (bf16[64,1792]{1,0:T(8,128)(2,1)S(1)}, bf16[64,1792]{1,0:T(8,128)(2,1)S(1)}, u32[]{:S(2)}, u32[]{:S(2)}) collective-permute-start(bf16[64,1792]{1,0:T(8,128)(2,1)S(1)} %pad_maximum_fusion.3), channel_id=1, source_target_pairs={{0,224},{16,240},{32,0},{48,16},{64,32},{80,48},{96,64},{112,80},{... | collective-permute-start | bytes 688136 | tf_op jit(solution)/shard_map/ppermute | solution.py:61
  9.5 3.2 %collective-permute-start.14 = (bf16[64,256]{1,0:T(8,128)(2,1)S(1)}, bf16[64,256]{1,0:T(8,128)(2,1)S(1)}, u32[]{:S(2)}, u32[]{:S(2)}) collective-permute-start(bf16[64,256]{1,0:T(8,128)(2,1)S(1)} %pad_maximum_fusion.5), channel_id=1, source_target_pairs={{0,0},{1,16},{2,32},{3,48},{4,64},{5,80},{6,96},{7,112},{8,128},{9... | collective-permute-start | bytes 98312 | tf_op jit(solution)/shard_map/ppermute | solution.py:174
  12.7 1.6 constant_dynamic-update-slice_fusion.14
  14.3 1.6 constant_dynamic-update-slice_fusion.13
  16.7 15.2 %all-to-all-start.2 = ((bf16[16,64,256]{2,1,0:T(8,128)(2,1)}), bf16[16,64,256]{2,1,0:T(8,128)(2,1)S(1)}, u32[]{:S(2)}, u32[]{:S(2)}) async-start(bf16[16,64,256]{2,1,0:T(8,128)(2,1)} %tile.11), calls=%async_computation.2 | async-start | bytes 1048576 | tf_op jit(solution)/shard_map/all_to_all | solution.py:50
  32.1 1.5 collective-permute-start.5
  35.7 3.6 %collective-permute-done.4 = bf16[64,1792]{1,0:T(8,128)(2,1)S(1)} collective-permute-done((bf16[64,1792]{1,0:T(8,128)(2,1)S(1)}, bf16[64,1792]{1,0:T(8,128)(2,1)S(1)}, u32[]{:S(2)}, u32[]{:S(2)}) %collective-permute-start.4) | collective-permute-done | bytes 229408 | tf_op jit(solution)/shard_map/ppermute | solution.py:61
  41.9 3.6 %collective-permute-done.7 = bf16[64,1792]{1,0:T(8,128)(2,1)S(1)} collective-permute-done((bf16[64,1792]{1,0:T(8,128)(2,1)S(1)}, bf16[64,1792]{1,0:T(8,128)(2,1)S(1)}, u32[]{:S(2)}, u32[]{:S(2)}) %collective-permute-start.7) | collective-permute-done | bytes 229408 | tf_op jit(solution)/shard_map/ppermute | solution.py:61
  45.5 1.5 collective-permute-done.8
  47.1 1.7 collective-permute-start.9
  54.1 4.0 %collective-permute-done.6 = bf16[128,1792]{1,0:T(8,128)(2,1)S(1)} collective-permute-done((bf16[128,1792]{1,0:T(8,128)(2,1)S(1)}, bf16[128,1792]{1,0:T(8,128)(2,1)S(1)}, u32[]{:S(2)}, u32[]{:S(2)}) %collective-permute-start.6) | collective-permute-done | bytes 458784 | tf_op jit(solution)/shard_map/ppermute | solution.py:75
  60.4 7.6 %collective-permute-done.9 = bf16[128,1792]{1,0:T(8,128)(2,1)S(1)} collective-permute-done((bf16[128,1792]{1,0:T(8,128)(2,1)S(1)}, bf16[128,1792]{1,0:T(8,128)(2,1)S(1)}, u32[]{:S(2)}, u32[]{:S(2)}) %collective-permute-start.9) | collective-permute-done | bytes 458784 | tf_op jit(solution)/shard_map/ppermute | solution.py:75
  70.1 2.8 %collective-permute-done.12 = bf16[64,1792]{1,0:T(8,128)(2,1)S(1)} collective-permute-done((bf16[64,1792]{1,0:T(8,128)(2,1)S(1)}, bf16[64,1792]{1,0:T(8,128)(2,1)S(1)}, u32[]{:S(2)}, u32[]{:S(2)}) %collective-permute-start.12) | collective-permute-done | bytes 229408 | tf_op jit(solution)/shard_map/ppermute | solution.py:79
  73.6 7.1 %fusion.4 = bf16[1024,896]{1,0:T(8,128)(2,1)} fusion(bf16[1024,1792]{1,0:T(8,128)(2,1)} %constant_dynamic-update-slice_fusion, bf16[1792,1792]{1,0:T(8,128)(2,1)S(1)} %copy-done.6, s32[]{:T(128)S(6)} %select_n.39), kind=kOutput, calls=%fused_computation.5 | convolution fusion | flops 3289251840 | bytes 8716292 | tf_op jit(solution)/shard_map/dot_general | solution.py:185
  81.6 1.3 fusion.9
  82.9 3.8 %all-to-all-start.3 = ((f32[16,64,256]{2,1,0:T(8,128)}), f32[16,64,256]{2,1,0:T(8,128)S(1)}, u32[]{:S(2)}, u32[]{:S(2)}) async-start(f32[16,64,256]{2,1,0:T(8,128)} %fusion.9), calls=%async_computation.3 | async-start | bytes 2097152 | tf_op jit(solution)/shard_map/all_to_all | solution.py:50
  86.8 8.2 %add_convert_fusion = bf16[1024,896]{1,0:T(8,128)(2,1)} fusion(bf16[1024,896]{1,0:T(8,128)(2,1)S(1)} %collective-permute-done.13, bf16[1024,1792]{1,0:T(8,128)(2,1)} %constant_dynamic-update-slice_fusion, bf16[1792,1792]{1,0:T(8,128)(2,1)} %param.14, s32[]{:T(128)S(6)} %select_n.38), kind=kOutput, calls=%fused_computation | convolution fusion | flops 3291086848 | bytes 10551300 | tf_op jit(solution)/shard_map/dot_general | solution.py:187
  95.0 18.8 %all-to-all-done.3 = f32[16,64,256]{2,1,0:T(8,128)S(1)} async-done(((f32[16,64,256]{2,1,0:T(8,128)}), f32[16,64,256]{2,1,0:T(8,128)S(1)}, u32[]{:S(2)}, u32[]{:S(2)}) %all-to-all-start.3) | async-done | bytes 1048608 | tf_op jit(solution)/shard_map/all_to_all | solution.py:50
  113.8 6.4 %all-to-all-start = ((bf16[8,128,896]{2,1,0:T(8,128)(2,1)}), bf16[8,128,896]{2,1,0:T(8,128)(2,1)S(1)}, u32[]{:S(2)}, u32[]{:S(2)}) async-start(bf16[8,128,896]{2,1,0:T(8,128)(2,1)} %bitcast.19), calls=%async_computation | async-start | bytes 3670016 | tf_op jit(solution)/shard_map/all_to_all | solution.py:50
  120.3 26.5 %all-to-all-done = bf16[8,128,896]{2,1,0:T(8,128)(2,1)S(1)} async-done(((bf16[8,128,896]{2,1,0:T(8,128)(2,1)}), bf16[8,128,896]{2,1,0:T(8,128)(2,1)S(1)}, u32[]{:S(2)}, u32[]{:S(2)}) %all-to-all-start) | async-done | bytes 1835040 | tf_op jit(solution)/shard_map/all_to_all | solution.py:50
  147.6 4.8 %all-to-all-start.4 = ((bf16[16,64,256]{2,1,0:T(8,128)(2,1)}), bf16[16,64,256]{2,1,0:T(8,128)(2,1)S(1)}, u32[]{:S(2)}, u32[]{:S(2)}) async-start(bf16[16,64,256]{2,1,0:T(8,128)(2,1)} %tile.12), calls=%async_computation.4 | async-start | bytes 1048576 | tf_op jit(solution)/shard_map/all_to_all | solution.py:50
  152.6 14.7 %all-to-all-done.4 = bf16[16,64,256]{2,1,0:T(8,128)(2,1)S(1)} async-done(((bf16[16,64,256]{2,1,0:T(8,128)(2,1)}), bf16[16,64,256]{2,1,0:T(8,128)(2,1)S(1)}, u32[]{:S(2)}, u32[]{:S(2)}) %all-to-all-start.4) | async-done | bytes 524320 | tf_op jit(solution)/shard_map/all_to_all | solution.py:50
  167.3 1.5 tile.10
  168.8 3.9 %all-to-all-start.1 = ((bf16[8,128,896]{2,1,0:T(8,128)(2,1)}), bf16[8,128,896]{2,1,0:T(8,128)(2,1)S(1)}, u32[]{:S(2)}, u32[]{:S(2)}) async-start(bf16[8,128,896]{2,1,0:T(8,128)(2,1)} %tile.10), calls=%async_computation.1 | async-start | bytes 3670016 | tf_op jit(solution)/shard_map/all_to_all | solution.py:50
  172.7 2.5 %constant_dynamic-slice_fusion = (f32[896,256]{1,0:T(8,128)S(1)}, f32[896,256]{1,0:T(8,128)}) fusion(f32[1792,256]{1,0:T(8,128)} %param.15, s32[]{:T(128)S(6)} %select_n.39, s32[]{:T(128)S(6)} %select_n.38), kind=kLoop, calls=%fused_computation.40 | loop fusion | flops 458752 | bytes 3670024 | tf_op jit(solution)/shard_map/dynamic_slice | solution.py:169
  175.2 3.4 %collective-permute-start.16 = (f32[896,256]{1,0:T(8,128)S(1)}, f32[896,256]{1,0:T(8,128)}, u32[]{:S(2)}, u32[]{:S(2)}) collective-permute-start(f32[896,256]{1,0:T(8,128)S(1)} %get-tuple-element.5), channel_id=1, source_target_pairs={{0,1},{1,0},{2,3},{3,2},{4,5},{5,4},{6,7},{7,6},{8,9},{9,8},{10,11... | collective-permute-start | bytes 2752520 | tf_op jit(solution)/shard_map/ppermute | solution.py:169
  178.7 2.9 %collective-permute-done.16 = f32[896,256]{1,0:T(8,128)} collective-permute-done((f32[896,256]{1,0:T(8,128)S(1)}, f32[896,256]{1,0:T(8,128)}, u32[]{:S(2)}, u32[]{:S(2)}) %collective-permute-start.16) | collective-permute-done | bytes 917536 | tf_op jit(solution)/shard_map/ppermute | solution.py:169
  181.6 1.3 add_divide_fusion.sib_inv_ref
  183.8 13.1 %all-to-all-done.1 = bf16[8,128,896]{2,1,0:T(8,128)(2,1)S(1)} async-done(((bf16[8,128,896]{2,1,0:T(8,128)(2,1)}), bf16[8,128,896]{2,1,0:T(8,128)(2,1)S(1)}, u32[]{:S(2)}, u32[]{:S(2)}) %all-to-all-start.1) | async-done | bytes 1835040 | tf_op jit(solution)/shard_map/all_to_all | solution.py:50
  199.0 16.8 %shard_map.91 = f32[16,128]{1,0:T(8,128)S(1)} custom-call(s32[16]{0:T(128)S(1)} %fusion.14.order_ref, f32[16,16]{1,0:T(8,128)S(1)} %fusion.11.place_ref, bf16[1024,896]{1,0:T(8,128)(2,1)S(1)} %bitcast.16, bf16[1024,256]{1,0:T(8,128)(2,1)S(1)} %bitcast.18, bf16[1024,256]{1,0:T(8,128)(2,1)S(1)} %copy-done.3, f32[896,256]{1,0:T(8,128)S(1)} %copy-done.1, ...), custom_call_target="tpu_custom_call" | custom-call | flops 7985954816 | bytes 8388608 | tf_op jit(solution)/shard_map/pallas_call | solution.py:132
  215.9 12.8 %all_to_all.49 = f32[16,16,128]{2,1,0:T(8,128)S(1)} all-to-all(f32[16,16,128]{2,1,0:T(8,128)S(1)} %tile.13), channel_id=1, replica_groups=mesh['dp'=16,'mp'=16] {'mp'}, dimensions={0} | all-to-all | bytes 262144 | tf_op jit(solution)/shard_map/all_to_all | solution.py:50
  228.8 14.2 %all_to_all.50 = f32[16,16,128]{2,1,0:T(8,128)S(1)} all-to-all(f32[16,16,128]{2,1,0:T(8,128)S(1)} %tile.14), channel_id=1, replica_groups=mesh['dp'=16,'mp'=16] {'dp'}, dimensions={0} | all-to-all | bytes 262144 | tf_op jit(solution)/shard_map/all_to_all | solution.py:50
  (69 shorter events, 25.2 us)
Async XLA Ops:
  0.0 81.6 %copy-start = (bf16[256,256]{1,0:T(8,128)(2,1)S(1)}, bf16[256,256]{1,0:T(8,128)(2,1)}, u32[]{:S(2)}) copy-start(bf16[256,256]{1,0:T(8,128)(2,1)} %param.13) | copy-start | bytes 393220
  1.0 30.9 %collective-permute-start.1 = (bf16[64,1792]{1,0:T(8,128)(2,1)S(1)}, bf16[64,1792]{1,0:T(8,128)(2,1)S(1)}, u32[]{:S(2)}, u32[]{:S(2)}) collective-permute-start(bf16[64,1792]{1,0:T(8,128)(2,1)S(1)} %pad_maximum_fusion.3), channel_id=1, source_target_pairs={{0,224},{16,240},{32,0},{48,16},{64,32},{80,48},{96,64},{112,80},{... | collective-permute-start | bytes 688136 | tf_op jit(solution)/shard_map/ppermute | solution.py:61
  7.5 26.1 %collective-permute-start = (bf16[64,1792]{1,0:T(8,128)(2,1)S(1)}, bf16[64,1792]{1,0:T(8,128)(2,1)S(1)}, u32[]{:S(2)}, u32[]{:S(2)}) collective-permute-start(bf16[64,1792]{1,0:T(8,128)(2,1)S(1)} %pad_maximum_fusion.3), channel_id=1, source_target_pairs={{0,16},{16,0},{32,48},{48,32},{64,80},{80,64},{96,112},{112,96},{1... | collective-permute-start | bytes 688136 | tf_op jit(solution)/shard_map/ppermute | solution.py:73
  8.8 23.1 %collective-permute-start.2 = (bf16[64,1792]{1,0:T(8,128)(2,1)S(1)}, bf16[64,1792]{1,0:T(8,128)(2,1)S(1)}, u32[]{:S(2)}, u32[]{:S(2)}) collective-permute-start(bf16[64,1792]{1,0:T(8,128)(2,1)S(1)} %pad_maximum_fusion.3), channel_id=1, source_target_pairs={{0,32},{16,48},{32,64},{48,80},{64,96},{80,112},{96,128},{112,144}... | collective-permute-start | bytes 688136 | tf_op jit(solution)/shard_map/ppermute | solution.py:62
  9.5 6.3 %collective-permute-start.14 = (bf16[64,256]{1,0:T(8,128)(2,1)S(1)}, bf16[64,256]{1,0:T(8,128)(2,1)S(1)}, u32[]{:S(2)}, u32[]{:S(2)}) collective-permute-start(bf16[64,256]{1,0:T(8,128)(2,1)S(1)} %pad_maximum_fusion.5), channel_id=1, source_target_pairs={{0,0},{1,16},{2,32},{3,48},{4,64},{5,80},{6,96},{7,112},{8,128},{9... | collective-permute-start | bytes 98312 | tf_op jit(solution)/shard_map/ppermute | solution.py:174
  16.7 64.9 %all-to-all-start.2 = ((bf16[16,64,256]{2,1,0:T(8,128)(2,1)}), bf16[16,64,256]{2,1,0:T(8,128)(2,1)S(1)}, u32[]{:S(2)}, u32[]{:S(2)}) async-start(bf16[16,64,256]{2,1,0:T(8,128)(2,1)} %tile.11), calls=%async_computation.2 | async-start | bytes 1048576 | tf_op jit(solution)/shard_map/all_to_all | solution.py:50
  31.9 18.4 %collective-permute-start.3 = (bf16[128,1792]{1,0:T(8,128)(2,1)S(1)}, bf16[128,1792]{1,0:T(8,128)(2,1)S(1)}, u32[]{:S(2)}, u32[]{:S(2)}) collective-permute-start(bf16[128,1792]{1,0:T(8,128)(2,1)S(1)} %pad_maximum_fusion), channel_id=1, source_target_pairs={{0,16},{16,0},{32,48},{48,32},{64,80},{80,64},{96,112},{112,96},{1... | collective-permute-start | bytes 1376264 | tf_op jit(solution)/shard_map/ppermute | solution.py:75
  32.0 7.2 %collective-permute-start.4 = (bf16[64,1792]{1,0:T(8,128)(2,1)S(1)}, bf16[64,1792]{1,0:T(8,128)(2,1)S(1)}, u32[]{:S(2)}, u32[]{:S(2)}) collective-permute-start(bf16[64,1792]{1,0:T(8,128)(2,1)S(1)} %collective-permute-done.1), channel_id=1, source_target_pairs={{0,224},{16,240},{32,0},{48,16},{64,32},{80,48},{96,64},{112,80},{... | collective-permute-start | bytes 688136 | tf_op jit(solution)/shard_map/ppermute | solution.py:61
  32.1 8.0 %collective-permute-start.5 = (bf16[64,1792]{1,0:T(8,128)(2,1)S(1)}, bf16[64,1792]{1,0:T(8,128)(2,1)S(1)}, u32[]{:S(2)}, u32[]{:S(2)}) collective-permute-start(bf16[64,1792]{1,0:T(8,128)(2,1)S(1)} %collective-permute-done.2), channel_id=1, source_target_pairs={{0,32},{16,48},{32,64},{48,80},{64,96},{80,112},{96,128},{112,144}... | collective-permute-start | bytes 688136 | tf_op jit(solution)/shard_map/ppermute | solution.py:62
  39.3 6.2 %collective-permute-start.7 = (bf16[64,1792]{1,0:T(8,128)(2,1)S(1)}, bf16[64,1792]{1,0:T(8,128)(2,1)S(1)}, u32[]{:S(2)}, u32[]{:S(2)}) collective-permute-start(bf16[64,1792]{1,0:T(8,128)(2,1)S(1)} %collective-permute-done.4), channel_id=1, source_target_pairs={{0,224},{16,240},{32,0},{48,16},{64,32},{80,48},{96,64},{112,80},{... | collective-permute-start | bytes 688136 | tf_op jit(solution)/shard_map/ppermute | solution.py:61
  40.2 6.8 %collective-permute-start.8 = (bf16[64,1792]{1,0:T(8,128)(2,1)S(1)}, bf16[64,1792]{1,0:T(8,128)(2,1)S(1)}, u32[]{:S(2)}, u32[]{:S(2)}) collective-permute-start(bf16[64,1792]{1,0:T(8,128)(2,1)S(1)} %collective-permute-done.5), channel_id=1, source_target_pairs={{0,32},{16,48},{32,64},{48,80},{64,96},{80,112},{96,128},{112,144}... | collective-permute-start | bytes 688136 | tf_op jit(solution)/shard_map/ppermute | solution.py:62
  40.8 32.8 %copy-start.6 = (bf16[1792,1792]{1,0:T(8,128)(2,1)S(1)}, bf16[1792,1792]{1,0:T(8,128)(2,1)}, u32[]{:S(2)}) copy-start(bf16[1792,1792]{1,0:T(8,128)(2,1)} %param.14) | copy-start | bytes 19267588
  40.8 17.4 %collective-permute-start.6 = (bf16[128,1792]{1,0:T(8,128)(2,1)S(1)}, bf16[128,1792]{1,0:T(8,128)(2,1)S(1)}, u32[]{:S(2)}, u32[]{:S(2)}) collective-permute-start(bf16[128,1792]{1,0:T(8,128)(2,1)S(1)} %pad_maximum_fusion.1), channel_id=1, source_target_pairs={{0,16},{16,0},{32,48},{48,32},{64,80},{80,64},{96,112},{112,96},{1... | collective-permute-start | bytes 1376264 | tf_op jit(solution)/shard_map/ppermute | solution.py:75
  47.1 20.9 %collective-permute-start.9 = (bf16[128,1792]{1,0:T(8,128)(2,1)S(1)}, bf16[128,1792]{1,0:T(8,128)(2,1)S(1)}, u32[]{:S(2)}, u32[]{:S(2)}) collective-permute-start(bf16[128,1792]{1,0:T(8,128)(2,1)S(1)} %pad_maximum_fusion.2), channel_id=1, source_target_pairs={{0,16},{16,0},{32,48},{48,32},{64,80},{80,64},{96,112},{112,96},{1... | collective-permute-start | bytes 1376264 | tf_op jit(solution)/shard_map/ppermute | solution.py:75
  48.7 4.0 %collective-permute-start.10 = (bf16[32,1792]{1,0:T(8,128)(2,1)S(1)}, bf16[32,1792]{1,0:T(8,128)(2,1)S(1)}, u32[]{:S(2)}, u32[]{:S(2)}) collective-permute-start(bf16[32,1792]{1,0:T(8,128)(2,1)S(1)} %slice.21), channel_id=1, source_target_pairs={{0,224},{16,240},{32,0},{48,16},{64,32},{80,48},{96,64},{112,80},{... | collective-permute-start | bytes 344072 | tf_op jit(solution)/shard_map/ppermute | solution.py:67
  49.1 4.9 %collective-permute-start.11 = (bf16[32,1792]{1,0:T(8,128)(2,1)S(1)}, bf16[32,1792]{1,0:T(8,128)(2,1)S(1)}, u32[]{:S(2)}, u32[]{:S(2)}) collective-permute-start(bf16[32,1792]{1,0:T(8,128)(2,1)S(1)} %slice.22), channel_id=1, source_target_pairs={{0,32},{16,48},{32,64},{48,80},{64,96},{80,112},{96,128},{112,144}... | collective-permute-start | bytes 344072 | tf_op jit(solution)/shard_map/ppermute | solution.py:68
  54.0 18.9 %collective-permute-start.12 = (bf16[64,1792]{1,0:T(8,128)(2,1)S(1)}, bf16[64,1792]{1,0:T(8,128)(2,1)S(1)}, u32[]{:S(2)}, u32[]{:S(2)}) collective-permute-start(bf16[64,1792]{1,0:T(8,128)(2,1)S(1)} %pad_maximum_fusion.4), channel_id=1, source_target_pairs={{0,16},{16,0},{32,48},{48,32},{64,80},{80,64},{96,112},{112,96},{1... | collective-permute-start | bytes 688136 | tf_op jit(solution)/shard_map/ppermute | solution.py:79
  80.7 6.0 %collective-permute-start.13 = (bf16[1024,896]{1,0:T(8,128)(2,1)}, bf16[1024,896]{1,0:T(8,128)(2,1)S(1)}, u32[]{:S(2)}, u32[]{:S(2)}) collective-permute-start(bf16[1024,896]{1,0:T(8,128)(2,1)} %fusion.4), channel_id=1, source_target_pairs={{0,1},{1,0},{2,3},{3,2},{4,5},{5,4},{6,7},{7,6},{8,9},{9,8},{10,11... | collective-permute-start | bytes 5505032 | tf_op jit(solution)/shard_map/ppermute | solution.py:186
  82.9 30.9 %all-to-all-start.3 = ((f32[16,64,256]{2,1,0:T(8,128)}), f32[16,64,256]{2,1,0:T(8,128)S(1)}, u32[]{:S(2)}, u32[]{:S(2)}) async-start(f32[16,64,256]{2,1,0:T(8,128)} %fusion.9), calls=%async_computation.3 | async-start | bytes 2097152 | tf_op jit(solution)/shard_map/all_to_all | solution.py:50
  113.8 32.9 %all-to-all-start = ((bf16[8,128,896]{2,1,0:T(8,128)(2,1)}), bf16[8,128,896]{2,1,0:T(8,128)(2,1)S(1)}, u32[]{:S(2)}, u32[]{:S(2)}) async-start(bf16[8,128,896]{2,1,0:T(8,128)(2,1)} %bitcast.19), calls=%async_computation | async-start | bytes 3670016 | tf_op jit(solution)/shard_map/all_to_all | solution.py:50
  147.6 19.7 %all-to-all-start.4 = ((bf16[16,64,256]{2,1,0:T(8,128)(2,1)}), bf16[16,64,256]{2,1,0:T(8,128)(2,1)S(1)}, u32[]{:S(2)}, u32[]{:S(2)}) async-start(bf16[16,64,256]{2,1,0:T(8,128)(2,1)} %tile.12), calls=%async_computation.4 | async-start | bytes 1048576 | tf_op jit(solution)/shard_map/all_to_all | solution.py:50
  168.8 9.8 %copy-start.4 = (s32[16]{0:T(128)S(1)}, s32[16]{0:T(128)}, u32[]{:S(2)}) copy-start(s32[16]{0:T(128)} %constant.76.clone) | copy-start | bytes 196
  168.8 9.8 %copy-start.5 = (s32[16]{0:T(128)S(1)}, s32[16]{0:T(128)}, u32[]{:S(2)}) copy-start(s32[16]{0:T(128)} %constant.77.clone) | copy-start | bytes 196
  168.8 28.0 %all-to-all-start.1 = ((bf16[8,128,896]{2,1,0:T(8,128)(2,1)}), bf16[8,128,896]{2,1,0:T(8,128)(2,1)S(1)}, u32[]{:S(2)}, u32[]{:S(2)}) async-start(bf16[8,128,896]{2,1,0:T(8,128)(2,1)} %tile.10), calls=%async_computation.1 | async-start | bytes 3670016 | tf_op jit(solution)/shard_map/all_to_all | solution.py:50
  175.2 6.4 %collective-permute-start.16 = (f32[896,256]{1,0:T(8,128)S(1)}, f32[896,256]{1,0:T(8,128)}, u32[]{:S(2)}, u32[]{:S(2)}) collective-permute-start(f32[896,256]{1,0:T(8,128)S(1)} %get-tuple-element.5), channel_id=1, source_target_pairs={{0,1},{1,0},{2,3},{3,2},{4,5},{5,4},{6,7},{7,6},{8,9},{9,8},{10,11... | collective-permute-start | bytes 2752520 | tf_op jit(solution)/shard_map/ppermute | solution.py:169
  178.7 4.3 %collective-permute-start.15 = (bf16[1024,256]{1,0:T(8,128)(2,1)S(1)}, bf16[1024,256]{1,0:T(8,128)(2,1)S(1)}, u32[]{:S(2)}, u32[]{:S(2)}) collective-permute-start(bf16[1024,256]{1,0:T(8,128)(2,1)S(1)} %bitcast.17), channel_id=1, source_target_pairs={{0,1},{1,0},{2,3},{3,2},{4,5},{5,4},{6,7},{7,6},{8,9},{9,8},{10,11... | collective-permute-start | bytes 1572872 | tf_op jit(solution)/shard_map/ppermute | solution.py:179
  183.0 0.8 copy-start.2
  196.8 1.2 copy-start.1
  198.0 1.0 copy-start.3

commit v2 on v1

v2 whole, which is shorter than its diff:
```python
import functools

import jax
import jax.numpy as jnp
from jax import lax
from jax.experimental import pallas as pl
from jax.experimental.pallas import tpu as pltpu
from jax.sharding import PartitionSpec as P

IN = 4096
OUT = 28672
TS = 32
TQ = 32

damping = 0.1

NZ, NYL, NX, NYH, NC = 8, 2, 4, 2, 2
GROUPS = NZ * NYL
CHIPS = NX * NYH


def dp_index(z, yl):
    return (z % NZ) * NYL + yl % NYL


def mp_index(x, yh, core):
    return ((x % NX) * NYH + yh % NYH) * NC + core % NC


def dp_shift(dz, dyl):
    return [
        (dp_index(z, y), dp_index(z + dz, y + dyl)) for z in range(NZ) for y in range(NYL)
    ]


CORE_SWAP = [
    (mp_index(x, h, c), mp_index(x, h, c + 1))
    for x in range(NX)
    for h in range(NYH)
    for c in range(NC)
]
TRANSPOSE = [(d * 16 + m, m * 16 + d) for d in range(16) for m in range(16)]
CHIP_TRANSPOSE = [
    ((z * NYL + yl) * 16 + q * NC + c, (q * NYL + yl) * 16 + z * NC + c)
    for z in range(NZ)
    for yl in range(NYL)
    for q in range(NX * NYH)
    for c in range(NC)
]
SAME_CORE = [
    [mp_index(x, h, c) for x in range(NX) for h in range(NYH)] for c in range(NC)
]

CHUNKS = (
    ((0, 0), (0, 1), (1, 0), (-1, 0), (1, 1), (-1, 1), (2, 0), (2, 1)),
    ((-2, 0), (-2, 1), (3, 0), (-3, 0), (3, 1), (-3, 1), (4, 0), (4, 1)),
)
RING = (0, 1, -1, 2, -2, 3, -3, 4)


def exchange(x, axis, **kw):
    return lax.all_to_all(x, axis, 0, 0, tiled=True, **kw)


def share(x, count, axis, **kw):
    return exchange(jnp.tile(x, (count, 1)), axis, **kw)


def z_ring(own):
    held = {0: own}
    up = down = own
    for k in (1, 2, 3):
        up = lax.ppermute(up, "dp", dp_shift(-1, 0))
        down = lax.ppermute(down, "dp", dp_shift(1, 0))
        held[k], held[-k] = up, down
    half = own.shape[0] // 2
    held[4] = jnp.concatenate(
        [
            lax.ppermute(up[:half], "dp", dp_shift(-1, 0)),
            lax.ppermute(down[half:], "dp", dp_shift(1, 0)),
        ],
        0,
    )
    return held


def ring_gather(own):
    along = z_ring(own)
    held = {(k, 0): block for k, block in along.items()}
    across = dp_shift(0, 1)
    rows = own.shape[0]
    held[(0, 1)] = lax.ppermute(own, "dp", across)
    for k in (1, 2, 3):
        pair = lax.ppermute(jnp.concatenate([along[k], along[-k]], 0), "dp", across)
        held[(k, 1)], held[(-k, 1)] = pair[:rows], pair[rows:]
    held[(4, 1)] = lax.ppermute(along[4], "dp", across)
    return held


def turn_kernel(count, core_ref, *refs):
    del core_ref
    blocks = refs[:count]
    out_basis, in_basis, sib_ref, own_ref, tokens = refs[count:]
    rows = blocks[0].shape[0]
    features, units = out_basis.shape
    step = pl.program_id(0)

    @pl.when(step == 0)
    def _():
        for r, ref in enumerate(blocks):
            tokens[r * rows : (r + 1) * rows, :] = ref[...]

    def products():
        grads = jnp.dot(
            tokens[:, :features], out_basis[...], preferred_element_type=jnp.float32
        )
        acts = jnp.dot(
            tokens[:, features:], in_basis[...], preferred_element_type=jnp.float32
        )
        return grads, acts

    @pl.when(step == 0)
    def _():
        grads, acts = products()
        high = acts.astype(jnp.bfloat16)
        sib_ref[:, :units] = grads.astype(jnp.bfloat16)
        sib_ref[:, units : units + 128] = high
        sib_ref[:, units + 128 :] = (acts - high.astype(jnp.float32)).astype(jnp.bfloat16)

    @pl.when(step == 1)
    def _():
        grads, acts = products()
        own_ref[:, :units] = grads
        own_ref[:, units:] = acts


def turn(core, blocks, basis_out, basis_in):
    rows, width = blocks[0].shape
    features, units = basis_out.shape[0], basis_out.shape[1] // 2
    tokens = rows * len(blocks)
    whole = lambda i, core_ref: (0, 0)
    side = lambda i, core_ref: (0, jnp.where(i == 0, 1 - core_ref[0], core_ref[0]))
    return pl.pallas_call(
        functools.partial(turn_kernel, len(blocks)),
        grid_spec=pltpu.PrefetchScalarGridSpec(
            num_scalar_prefetch=1,
            grid=(2,),
            in_specs=[pl.BlockSpec((rows, width), whole)] * len(blocks)
            + [
                pl.BlockSpec((features, units), side),
                pl.BlockSpec((width - features, 128), side),
            ],
            out_specs=[
                pl.BlockSpec((tokens, units + 256), whole),
                pl.BlockSpec((tokens, units + 128), whole),
            ],
            scratch_shapes=[pltpu.VMEM((tokens, width), jnp.bfloat16)],
        ),
        out_shape=[
            jax.ShapeDtypeStruct((tokens, units + 256), jnp.bfloat16),
            jax.ShapeDtypeStruct((tokens, units + 128), jnp.float32),
        ],
        compiler_params=pltpu.CompilerParams(vmem_limit_bytes=32 * 1024 * 1024),
        cost_estimate=pl.CostEstimate(
            flops=2 * tokens * (features + 256) * (units + 128) * 2,
            bytes_accessed=2 * tokens * (width + 3 * units) + 4 * features * units,
            transcendentals=0,
        ),
    )(core.reshape(1), *blocks, basis_out, basis_in)


def pair_kernel(own_ref, got_ref, out_ref):
    units = own_ref.shape[1] - 128
    got = got_ref[...].astype(jnp.float32)
    grads = own_ref[:, :units] + got[:, :units]
    acts = own_ref[:, units:] + (got[:, units : units + 128] + got[:, units + 128 :])
    high = acts.astype(jnp.bfloat16)
    out_ref[:, :units] = grads.astype(jnp.bfloat16)
    out_ref[:, units : units + 128] = high
    out_ref[:, units + 128 :] = (acts - high.astype(jnp.float32)).astype(jnp.bfloat16)


def add_pair(own, got):
    vmem = pl.BlockSpec(memory_space=pltpu.VMEM)
    return pl.pallas_call(
        pair_kernel,
        out_shape=jax.ShapeDtypeStruct(got.shape, jnp.bfloat16),
        in_specs=[vmem, vmem],
        out_specs=vmem,
        compiler_params=pltpu.CompilerParams(vmem_limit_bytes=24 * 1024 * 1024),
        cost_estimate=pl.CostEstimate(
            flops=2 * own.size, bytes_accessed=own.size * 8, transcendentals=0
        ),
    )(own, got)


def score_kernel(acts_at_ref, inv_at_ref, place_ref, grads_ref, own_acts_ref, sib_acts_ref,
                 own_inv_ref, sib_inv_ref, out_ref, train_grads, query_acts, train_acts, inv,
                 sums):
    rows = TQ + TS
    for r in range(GROUPS):
        train_grads[r * TS : (r + 1) * TS, :] = grads_ref[r * rows + TQ : (r + 1) * rows, :]
        for part in range(2):
            start = pl.multiple_of(acts_at_ref[part * GROUPS + r], rows)
            middle = pl.multiple_of(start + TQ, TQ)
            lanes = slice(part * 128, part * 128 + 128)
            for ref, at in ((own_acts_ref, part * 128), (sib_acts_ref, part * 128 + 256)):
                query_acts[r * TQ : (r + 1) * TQ, at : at + 128] = ref[pl.ds(start, TQ), lanes]
                train_acts[r * TS : (r + 1) * TS, at : at + 128] = ref[
                    pl.ds(middle, TS), lanes
                ].astype(jnp.float32)
    same = inv_at_ref[0] == 1
    core_lanes = pl.multiple_of(inv_at_ref[1] * 128, 128)
    other_lanes = pl.multiple_of(128 - inv_at_ref[1] * 128, 128)
    for at, lanes in ((0, core_lanes), (256, other_lanes)):
        mine = own_inv_ref[:, pl.ds(lanes, 128)]
        theirs = sib_inv_ref[:, pl.ds(lanes, 128)]
        inv[:, at : at + 128] = jnp.where(same, mine, theirs)
        inv[:, at + 128 : at + 256] = jnp.where(same, theirs, mine)

    def one_query(n, carry):
        grads = grads_ref[pl.ds(pl.multiple_of(n * rows, rows), TQ), :]
        total = jnp.zeros((GROUPS, 128), jnp.float32)
        for at in (0, 256):
            acts = query_acts[pl.ds(pl.multiple_of(n * TQ, TQ), TQ), at : at + 256]
            gradient = lax.dot_general(
                grads, acts, (((0,), (0,)), ((), ())), preferred_element_type=jnp.float32
            )
            preconditioned = (gradient * inv[:, at : at + 256]).astype(jnp.bfloat16)
            projected = jnp.dot(
                train_grads[...], preconditioned, preferred_element_type=jnp.float32
            )
            terms = projected * train_acts[:, at : at + 256]
            terms = terms.reshape(GROUPS, TS, 256).sum(1)
            total = total + terms[:, :128] + terms[:, 128:]
        sums[pl.ds(n, 1)] = total[None]
        return carry

    lax.fori_loop(0, GROUPS, one_query, 0)
    scores = jnp.sum(sums[...], axis=2)
    hot = place_ref[...]
    scores = jnp.dot(
        hot, jnp.dot(scores, jnp.transpose(hot), precision=lax.Precision.HIGHEST),
        precision=lax.Precision.HIGHEST,
    )
    out_ref[...] = jnp.concatenate(
        [scores, jnp.zeros((GROUPS, 128 - GROUPS), jnp.float32)], 1
    )


def score_blocks(acts_at, inv_at, place, grads, own_acts, sib_acts, own_inv, sib_inv):
    units, features = own_inv.shape
    vmem = pl.BlockSpec(memory_space=pltpu.VMEM)
    smem = pl.BlockSpec(memory_space=pltpu.SMEM)
    return pl.pallas_call(
        score_kernel,
        out_shape=jax.ShapeDtypeStruct((GROUPS, 128), jnp.float32),
        in_specs=[smem] * 2 + [vmem] * 6,
        out_specs=vmem,
        scratch_shapes=[
            pltpu.VMEM((GROUPS * TS, units), jnp.bfloat16),
            pltpu.VMEM((GROUPS * TQ, 2 * features), jnp.bfloat16),
            pltpu.VMEM((GROUPS * TS, 2 * features), jnp.float32),
            pltpu.VMEM((units, 2 * features), jnp.float32),
            pltpu.VMEM((GROUPS, GROUPS, 128), jnp.float32),
        ],
        compiler_params=pltpu.CompilerParams(vmem_limit_bytes=24 * 1024 * 1024),
        cost_estimate=pl.CostEstimate(
            flops=2 * GROUPS * units * 2 * features * (GROUPS * TS + TQ),
            bytes_accessed=8 * 1024 * 1024,
            transcendentals=0,
        ),
    )(acts_at, inv_at, place, grads, own_acts, sib_acts, own_inv, sib_inv)


def shards(query_acts, query_grads, train_acts, train_grads, basis_in, basis_out, eigen):
    in_local = query_acts.shape[2]
    out_local = query_grads.shape[2]
    tokens = jnp.concatenate(
        [
            jnp.concatenate([query_grads[0], query_acts[0]], 1),
            jnp.concatenate([train_grads[0], train_acts[0]], 1),
        ],
        0,
    )
    dp, mp = lax.axis_index("dp"), lax.axis_index("mp")
    z, yl, q, core = dp // NYL, dp % NYL, mp // NC, mp % NC
    units = out_local // 2

    own_inv = 1.0 / (lax.dynamic_slice_in_dim(eigen, core * units, units, 0) + damping)
    sib_eigen = lax.ppermute(
        lax.dynamic_slice_in_dim(eigen, (1 - core) * units, units, 0), "mp", CORE_SWAP
    )
    sib_inv = 1.0 / (sib_eigen + damping)

    turned_basis = lax.ppermute(basis_in, ("dp", "mp"), TRANSPOSE)

    held = ring_gather(tokens)
    kept = []
    for chunk in CHUNKS:
        sib_part, own_part = turn(core, [held[place] for place in chunk], basis_out, turned_basis)
        pair = add_pair(own_part, lax.ppermute(sib_part, "mp", CORE_SWAP))
        parts = exchange(pair, "mp", axis_index_groups=SAME_CORE)
        kept.append(parts.reshape(CHIPS, -1, units + 256).astype(jnp.float32).sum(0))
    kept = jnp.concatenate(kept, 0)

    own_acts = (kept[:, units : units + 128] + kept[:, units + 128 :]).astype(jnp.bfloat16)
    own_acts = lax.ppermute(own_acts, ("dp", "mp"), CHIP_TRANSPOSE)
    own_acts = jnp.concatenate(
        [own_acts, lax.ppermute(own_acts, "dp", dp_shift(0, 1))], 1
    )
    around = z_ring(own_acts)
    own_acts = jnp.concatenate([around[k] for k in RING], 0)
    sib_acts = lax.ppermute(own_acts, "mp", CORE_SWAP)

    all_grads = share(
        kept[:, :units].astype(jnp.bfloat16), CHIPS, "mp", axis_index_groups=SAME_CORE
    )

    dz = jnp.array([CHUNKS[r % 2][r // 2][0] for r in range(GROUPS)], jnp.int32)
    dy = jnp.array([CHUNKS[r % 2][r // 2][1] for r in range(GROUPS)], jnp.int32)
    z_from, y_from = (z + dz + NZ) % NZ, (yl + dy) % NYL
    order = z_from * NYL + y_from
    place = (order[None, :] == jnp.arange(GROUPS, dtype=jnp.int32)[:, None]).astype(jnp.float32)
    at = {place: (half, i) for half in range(2) for i, place in enumerate(CHUNKS[half])}
    places = [(k if k <= 4 else k - NZ, j) for k in range(NZ) for j in range(NYL)]
    half_of = jnp.array([at[place][0] for place in places], jnp.int32)
    chip_of = jnp.array([at[place][1] for place in places], jnp.int32)
    ring_of = jnp.array(
        [RING.index(k if k <= 4 else k - NZ) for k in range(NZ)], jnp.int32
    )

    def stands(row_y):
        where = ((z_from - q + NZ) % NZ) * NYL + (y_from - row_y + NYL) % NYL
        piece = ring_of[(chip_of[where] - z + NZ) % NZ]
        return piece * (2 * (TQ + TS)) + half_of[where] * (TQ + TS)

    acts_at = jnp.concatenate([stands(yl), stands(1 - yl)])
    inv_at = jnp.stack([(yl == core).astype(jnp.int32), core.astype(jnp.int32)])

    scores = score_blocks(
        acts_at, inv_at, place, all_grads, own_acts, sib_acts, own_inv, sib_inv
    )
    normalizer = float(TQ * TS * IN * OUT) ** (-0.5)
    scores = share(scores * normalizer, GROUPS, "mp").reshape(GROUPS, GROUPS, 128).sum(0)
    scores = share(scores, GROUPS, "dp").reshape(GROUPS, GROUPS, 128).sum(0)
    return scores[:, :GROUPS]


def solution(mesh):
    placed = (
        P("dp", None, "mp"),
        P("dp", None, "mp"),
        P("dp", None, "mp"),
        P("dp", None, "mp"),
        P("dp", "mp"),
        P("mp", "dp"),
        P("dp", "mp"),
    )
    return jax.shard_map(shards, mesh=mesh, in_specs=placed, out_specs=P(), check_vma=False)
```

time: 245 us -> 239 us (0.976)
  waiting for transfers between devices: 100 us -> 77.1 us
  matrix products: 16.7 us -> 0 us
  Pallas kernels: 16.8 us -> 32.5 us
  starting transfers between devices: 57 us -> 71.3 us
  blocking collectives: 27 us -> 32.9 us
  local copies, waits for them, and re-layouts: 18.7 us -> 16 us
    all_to_all x5 -> x3, waiting for transfers between devices: 73 us -> 26.4 us  [exchange(): return lax.all_to_all(x, axis, 0, 0, tiled=True, **kw)]
    ppermute x15 -> x26, waiting for transfers between devices: 27.5 us -> 50.5 us  [the longest x1 15.1 us: shards(): lax.ppermute(own_acts, 'dp', dp_shift(0, 1))]
    ppermute x15 -> x26, starting transfers between devices: 21.6 us -> 43.3 us  [the longest x6 16.5 us: z_ring(): up = lax.ppermute(up, 'dp', dp_shift(-1, 0))]
    dot_general x3 -> x0, matrix products: 16.7 us -> none  [the longest x1 8.25 us: shards(): own_part = jnp.dot(tokens, own_basis, preferred_element_type=jnp.float32)]
    pallas_call x0 -> x4, Pallas kernels: none -> 15.6 us  [the longest x2 11.8 us: turn(): pl.pallas_call(functools.partial(turn_kernel, len(blocks)), grid_spec=plt...]
    all_to_all x5 -> x3, starting transfers between devices: 34 us -> 19.6 us  [exchange(): return lax.all_to_all(x, axis, 0, 0, tiled=True, **kw)]
    ppermute x1, starting transfers between devices: 0.01 us -> 7.11 us  [shards(): sib_acts = lax.ppermute(own_acts, 'mp', CORE_SWAP)]
    all_to_all x2, blocking collectives: 27 us -> 32.9 us  [exchange(): return lax.all_to_all(x, axis, 0, 0, tiled=True, **kw)]
  transfers between devices with their start and end apart: 22 -> 31, of which waited for: 13 -> 17; matrix products, arithmetic and copies ran while one was open for 14% -> 5% of each run, Pallas kernels for 0% -> 7%
where the time goes in v2:
time: 239 us; the launch traced here: 238 us
  waiting for transfers between devices  77.1 us (32%)
  starting transfers between devices  71.3 us (30%)
  blocking collectives  32.9 us (14%)
  Pallas kernels  32.5 us (14%)
  local copies, waits for them, and re-layouts  16 us (7%)
  other arithmetic  7.79 us (3%)
    all_to_all x2, blocking collectives, exchange(): return lax.all_to_all(x, axis, 0, 0, tiled=True, **kw)  32.9 us
    all_to_all x3, waiting for transfers between devices, exchange(): return lax.all_to_all(x, axis, 0, 0, tiled=True, **kw)  26.4 us
    all_to_all x3, starting transfers between devices, exchange(): return lax.all_to_all(x, axis, 0, 0, tiled=True, **kw)  19.6 us
    pallas_call x1, Pallas kernels, score_blocks(): pl.pallas_call(score_kernel, out_shape=jax.ShapeDtypeStruct((GROUPS, 128)...  16.9 us
    ppermute x6, starting transfers between devices, z_ring(): up = lax.ppermute(up, 'dp', dp_shift(-1, 0))  16.5 us
    ppermute x1, waiting for transfers between devices, shards(): lax.ppermute(own_acts, 'dp', dp_shift(0, 1))  15.1 us
    ppermute x6, waiting for transfers between devices, z_ring(): up = lax.ppermute(up, 'dp', dp_shift(-1, 0))  13.2 us
    pallas_call x2, Pallas kernels, turn(): pl.pallas_call(functools.partial(turn_kernel, len(blocks)), grid_spec=plt...  11.8 us
  transfers between devices with their start and end apart: 31, of which 17 were waited for; matrix products, arithmetic and copies ran while one was open for 5% of the time, Pallas kernels for 7%

profile of v2, /device:TPU:1, one launch (start us, length us, event | category | flops | bytes accessed | tf_op | source)
XLA Modules:
  0.0 238.0 jit_solution(911992035759203503)
XLA Ops:
  1.0 6.5 %collective-permute-start.1 = (bf16[64,2048]{1,0:T(8,128)(2,1)S(1)}, bf16[64,2048]{1,0:T(8,128)(2,1)S(1)}, u32[]{:S(2)}, u32[]{:S(2)}) collective-permute-start(bf16[64,2048]{1,0:T(8,128)(2,1)S(1)} %maximum_maximum_fusion.refs_0_), channel_id=1, source_target_pairs={{0,224},{16,240},{32,0},{48,16},{64,32},{80,48},{96,64},{112,80},{... | collective-permute-start | bytes 786440 | tf_op jit(solution)/shard_map/ppermute | solution.py:73
  7.5 5.0 %collective-permute-done.1.refs_2_ = bf16[64,2048]{1,0:T(8,128)(2,1)S(1)} collective-permute-done((bf16[64,2048]{1,0:T(8,128)(2,1)S(1)}, bf16[64,2048]{1,0:T(8,128)(2,1)S(1)}, u32[]{:S(2)}, u32[]{:S(2)}) %collective-permute-start.1) | collective-permute-done | bytes 262176 | tf_op jit(solution)/shard_map/ppermute | solution.py:73
  12.5 3.4 %collective-permute-start.4 = (bf16[64,2048]{1,0:T(8,128)(2,1)S(1)}, bf16[64,2048]{1,0:T(8,128)(2,1)S(1)}, u32[]{:S(2)}, u32[]{:S(2)}) collective-permute-start(bf16[64,2048]{1,0:T(8,128)(2,1)S(1)} %collective-permute-done.1.refs_2_), channel_id=1, source_target_pairs={{0,224},{16,240},{32,0},{48,16},{64,32},{80,48},{96,64},{112,80},{... | collective-permute-start | bytes 786440 | tf_op jit(solution)/shard_map/ppermute | solution.py:73
  17.3 2.6 %collective-permute-done.4.refs_6_ = bf16[64,2048]{1,0:T(8,128)(2,1)S(1)} collective-permute-done((bf16[64,2048]{1,0:T(8,128)(2,1)S(1)}, bf16[64,2048]{1,0:T(8,128)(2,1)S(1)}, u32[]{:S(2)}, u32[]{:S(2)}) %collective-permute-start.4) | collective-permute-done | bytes 262176 | tf_op jit(solution)/shard_map/ppermute | solution.py:73
  19.9 3.4 %collective-permute-start.9 = (bf16[64,2048]{1,0:T(8,128)(2,1)S(1)}, bf16[64,2048]{1,0:T(8,128)(2,1)S(1)}, u32[]{:S(2)}, u32[]{:S(2)}) collective-permute-start(bf16[64,2048]{1,0:T(8,128)(2,1)S(1)} %collective-permute-done.4.refs_6_), channel_id=1, source_target_pairs={{0,224},{16,240},{32,0},{48,16},{64,32},{80,48},{96,64},{112,80},{... | collective-permute-start | bytes 786440 | tf_op jit(solution)/shard_map/ppermute | solution.py:73
  24.6 5.0 %collective-permute-start.7 = (bf16[256,256]{1,0:T(8,128)(2,1)}, bf16[256,256]{1,0:T(8,128)(2,1)S(1)}, u32[]{:S(2)}, u32[]{:S(2)}) collective-permute-start(bf16[256,256]{1,0:T(8,128)(2,1)} %param.16), channel_id=1, source_target_pairs={{0,0},{1,16},{2,32},{3,48},{4,64},{5,80},{6,96},{7,112},{8,128},{9... | collective-permute-start | bytes 393224 | tf_op jit(solution)/shard_map/ppermute | solution.py:296
  31.4 6.4 %collective-permute-start.12 = (bf16[32,2048]{1,0:T(8,128)(2,1)S(1)}, bf16[32,2048]{1,0:T(8,128)(2,1)S(1)}, u32[]{:S(2)}, u32[]{:S(2)}) collective-permute-start(bf16[32,2048]{1,0:T(8,128)(2,1)S(1)} %slice.75), channel_id=1, source_target_pairs={{0,224},{16,240},{32,0},{48,16},{64,32},{80,48},{96,64},{112,80},{... | collective-permute-start | bytes 393224 | tf_op jit(solution)/shard_map/ppermute | solution.py:79
  37.9 5.9 %collective-permute-done.12 = bf16[32,2048]{1,0:T(8,128)(2,1)S(1)} collective-permute-done((bf16[32,2048]{1,0:T(8,128)(2,1)S(1)}, bf16[32,2048]{1,0:T(8,128)(2,1)S(1)}, u32[]{:S(2)}, u32[]{:S(2)}) %collective-permute-start.12) | collective-permute-done | bytes 131104 | tf_op jit(solution)/shard_map/ppermute | solution.py:79
  43.8 3.9 %collective-permute-done.6 = bf16[128,2048]{1,0:T(8,128)(2,1)S(1)} collective-permute-done((bf16[128,2048]{1,0:T(8,128)(2,1)S(1)}, bf16[128,2048]{1,0:T(8,128)(2,1)S(1)}, u32[]{:S(2)}, u32[]{:S(2)}) %collective-permute-start.6) | collective-permute-done | bytes 524320 | tf_op jit(solution)/shard_map/ppermute | solution.py:94
  47.9 2.8 %copy-done.3 = bf16[1792,1792]{1,0:T(8,128)(2,1)S(1)} copy-done((bf16[1792,1792]{1,0:T(8,128)(2,1)S(1)}, bf16[1792,1792]{1,0:T(8,128)(2,1)}, u32[]{:S(2)}) %copy-start.3) | copy-done | bytes 6422552
  50.7 5.9 %shard_map.118 = (bf16[512,1152]{1,0:T(8,128)(2,1)}, f32[512,1024]{1,0:T(8,128)S(1)}) custom-call(s32[1]{0:T(128)} %bitcast.5.core_ref, bf16[64,2048]{1,0:T(8,128)(2,1)S(1)} %maximum_maximum_fusion.refs_0_, bf16[64,2048]{1,0:T(8,128)(2,1)S(1)} %collective-permute-done.refs_1_, bf16[64,2048]{1,0:T(8,128)(2,1)S(1)} %collective-permute-done.1.refs_2_, ...), custom_call_target="tpu_custom_call" | custom-call | flops 4294967296 | bytes 11272192 | tf_op jit(solution)/shard_map/pallas_call | solution.py:143
  56.6 6.0 %collective-permute-start.8 = (bf16[512,1152]{1,0:T(8,128)(2,1)}, bf16[512,1152]{1,0:T(8,128)(2,1)}, u32[]{:S(2)}, u32[]{:S(2)}) collective-permute-start(bf16[512,1152]{1,0:T(8,128)(2,1)} %get-tuple-element.10), channel_id=1, source_target_pairs={{0,1},{1,0},{2,3},{3,2},{4,5},{5,4},{6,7},{7,6},{8,9},{9,8},{10,11... | collective-permute-start | bytes 3538952 | tf_op jit(solution)/shard_map/ppermute | solution.py:302
  62.7 7.9 %collective-permute-done.14.refs_7_ = bf16[64,2048]{1,0:T(8,128)(2,1)S(1)} collective-permute-done((bf16[64,2048]{1,0:T(8,128)(2,1)S(1)}, bf16[64,2048]{1,0:T(8,128)(2,1)S(1)}, u32[]{:S(2)}, u32[]{:S(2)}) %collective-permute-start.14) | collective-permute-done | bytes 262176 | tf_op jit(solution)/shard_map/ppermute | solution.py:96
  70.6 2.8 %copy-done.4 = bf16[1792,1792]{1,0:T(8,128)(2,1)S(1)} copy-done((bf16[1792,1792]{1,0:T(8,128)(2,1)S(1)}, bf16[1792,1792]{1,0:T(8,128)(2,1)}, u32[]{:S(2)}) %copy-start.4) | copy-done | bytes 6422552
  73.4 5.9 %shard_map.120 = (bf16[512,1152]{1,0:T(8,128)(2,1)}, f32[512,1024]{1,0:T(8,128)S(1)}) custom-call(s32[1]{0:T(128)} %bitcast.5.core_ref, bf16[64,2048]{1,0:T(8,128)(2,1)S(1)} %collective-permute-done.5.refs_0_, bf16[64,2048]{1,0:T(8,128)(2,1)S(1)} %get-tuple-element.22.refs_1_, bf16[64,2048]{1,0:T(8,128)(2,1)S(1)} %collective-permute-done.9.refs_2_, ...), custom_call_target="tpu_custom_call" | custom-call | flops 4294967296 | bytes 11272192 | tf_op jit(solution)/shard_map/pallas_call | solution.py:143
  81.7 2.5 %shard_map.119 = bf16[512,1152]{1,0:T(8,128)(2,1)} custom-call(f32[512,1024]{1,0:T(8,128)S(1)} %copy-done.1, bf16[512,1152]{1,0:T(8,128)(2,1)} %collective-permute-done.8.got_ref), custom_call_target="tpu_custom_call" | custom-call | flops 1048576 | bytes 4194304 | tf_op jit(solution)/shard_map/pallas_call | solution.py:185
  84.3 4.3 %all-to-all-start = ((bf16[8,64,1152]{2,1,0:T(8,128)(2,1)}), bf16[8,64,1152]{2,1,0:T(8,128)(2,1)}, u32[]{:S(2)}, u32[]{:S(2)}) async-start(bf16[8,64,1152]{2,1,0:T(8,128)(2,1)} %bitcast.10), calls=%async_computation | async-start | bytes 2359296 | tf_op jit(solution)/shard_map/all_to_all | solution.py:62
  88.6 2.8 %constant_dynamic-slice_fusion = (f32[896,256]{1,0:T(8,128)}, f32[896,256]{1,0:T(8,128)}) fusion(f32[1792,256]{1,0:T(8,128)} %param.18, s32[]{:T(128)S(6)} %select_n.114, s32[]{:T(128)S(6)} %select_n.113), kind=kLoop, calls=%fused_computation.87 | loop fusion | flops 458752 | bytes 3670024 | tf_op jit(solution)/shard_map/dynamic_slice | solution.py:292
  95.4 12.3 %all-to-all-done = bf16[8,64,1152]{2,1,0:T(8,128)(2,1)} async-done(((bf16[8,64,1152]{2,1,0:T(8,128)(2,1)}), bf16[8,64,1152]{2,1,0:T(8,128)(2,1)}, u32[]{:S(2)}, u32[]{:S(2)}) %all-to-all-start) | async-done | bytes 1179680 | tf_op jit(solution)/shard_map/all_to_all | solution.py:62
  107.7 3.9 %all-to-all-start.1 = ((bf16[8,64,1152]{2,1,0:T(8,128)(2,1)}), bf16[8,64,1152]{2,1,0:T(8,128)(2,1)S(1)}, u32[]{:S(2)}, u32[]{:S(2)}) async-start(bf16[8,64,1152]{2,1,0:T(8,128)(2,1)} %bitcast.11), calls=%async_computation.1 | async-start | bytes 2359296 | tf_op jit(solution)/shard_map/all_to_all | solution.py:62
  114.5 14.2 %all-to-all-done.1 = bf16[8,64,1152]{2,1,0:T(8,128)(2,1)S(1)} async-done(((bf16[8,64,1152]{2,1,0:T(8,128)(2,1)}), bf16[8,64,1152]{2,1,0:T(8,128)(2,1)S(1)}, u32[]{:S(2)}, u32[]{:S(2)}) %all-to-all-start.1) | async-done | bytes 1179680 | tf_op jit(solution)/shard_map/all_to_all | solution.py:62
  131.0 11.4 %all-to-all-start.2 = ((bf16[8,128,896]{2,1,0:T(8,128)(2,1)}), bf16[8,128,896]{2,1,0:T(8,128)(2,1)S(1)}, u32[]{:S(2)}, u32[]{:S(2)}) async-start(bf16[8,128,896]{2,1,0:T(8,128)(2,1)} %tile.6), calls=%async_computation.2 | async-start | bytes 3670016 | tf_op jit(solution)/shard_map/all_to_all | solution.py:62
  142.5 15.1 %collective-permute-done.17 = bf16[128,128]{1,0:T(8,128)(2,1)S(1)} collective-permute-done((bf16[128,128]{1,0:T(8,128)(2,1)S(1)}, bf16[128,128]{1,0:T(8,128)(2,1)S(1)}, u32[]{:S(2)}, u32[]{:S(2)}) %collective-permute-start.17) | collective-permute-done | bytes 32800 | tf_op jit(solution)/shard_map/ppermute | solution.py:310
  159.3 1.9 collective-permute-done.18
  162.6 2.5 %collective-permute-done.20 = bf16[128,256]{1,0:T(8,128)(2,1)S(1)} collective-permute-done((bf16[128,256]{1,0:T(8,128)(2,1)S(1)}, bf16[128,256]{1,0:T(8,128)(2,1)S(1)}, u32[]{:S(2)}, u32[]{:S(2)}) %collective-permute-start.20) | collective-permute-done | bytes 65568 | tf_op jit(solution)/shard_map/ppermute | solution.py:73
  165.1 1.9 collective-permute-start.22
  168.5 3.0 %collective-permute-start.24 = (bf16[64,256]{1,0:T(8,128)(2,1)S(1)}, bf16[64,256]{1,0:T(8,128)(2,1)S(1)}, u32[]{:S(2)}, u32[]{:S(2)}) collective-permute-start(bf16[64,256]{1,0:T(8,128)(2,1)S(1)} %slice.81), channel_id=1, source_target_pairs={{0,224},{16,240},{32,0},{48,16},{64,32},{80,48},{96,64},{112,80},{... | collective-permute-start | bytes 98312 | tf_op jit(solution)/shard_map/ppermute | solution.py:79
  172.5 3.3 %collective-permute-done.25 = bf16[64,256]{1,0:T(8,128)(2,1)S(1)} collective-permute-done((bf16[64,256]{1,0:T(8,128)(2,1)S(1)}, bf16[64,256]{1,0:T(8,128)(2,1)S(1)}, u32[]{:S(2)}, u32[]{:S(2)}) %collective-permute-start.25) | collective-permute-done | bytes 32800 | tf_op jit(solution)/shard_map/ppermute | solution.py:80
  175.9 7.1 %collective-permute-start.26 = (bf16[1024,256]{1,0:T(8,128)(2,1)S(1)}, bf16[1024,256]{1,0:T(8,128)(2,1)S(1)}, u32[]{:S(2)}, u32[]{:S(2)}) collective-permute-start(bf16[1024,256]{1,0:T(8,128)(2,1)S(1)} %constant_dynamic-update-slice_fusion.4.own_acts_ref), channel_id=1, source_target_pairs={{0,1},{1,0},{2,3},{3,2},{4,5},{5,4},{6,7},{7,6},{8,9},{9,8},{10,11... | collective-permute-start | bytes 1572872 | tf_op jit(solution)/shard_map/ppermute | solution.py:314
  187.5 16.9 %shard_map.122 = f32[16,128]{1,0:T(8,128)S(1)} custom-call(s32[32]{0:T(128)S(1)} %pad_add_fusion.acts_at_ref, s32[2]{0:T(128)S(1)} %pad_add_fusion.1.inv_at_ref, f32[16,16]{1,0:T(8,128)S(1)} %fusion.5.place_ref, bf16[1024,896]{1,0:T(8,128)(2,1)S(1)} %bitcast.18, bf16[1024,256]{1,0:T(8,128)(2,1)S(1)} %constant_dynamic-update-slice_fusion.4.own_acts_ref, ...), custom_call_target="tpu_custom_call" | custom-call | flops 7985954816 | bytes 8388608 | tf_op jit(solution)/shard_map/pallas_call | solution.py:255
  204.5 18.5 %all_to_all.38 = f32[16,16,128]{2,1,0:T(8,128)S(1)} all-to-all(f32[16,16,128]{2,1,0:T(8,128)S(1)} %tile.7), channel_id=1, replica_groups=mesh['dp'=16,'mp'=16] {'mp'}, dimensions={0} | all-to-all | bytes 262144 | tf_op jit(solution)/shard_map/all_to_all | solution.py:62
  223.0 14.4 %all_to_all.39 = f32[16,16,128]{2,1,0:T(8,128)S(1)} all-to-all(f32[16,16,128]{2,1,0:T(8,128)S(1)} %tile.8), channel_id=1, replica_groups=mesh['dp'=16,'mp'=16] {'dp'}, dimensions={0} | all-to-all | bytes 262144 | tf_op jit(solution)/shard_map/all_to_all | solution.py:62
  (115 shorter events, 28.2 us)
Async XLA Ops:
  1.0 11.5 %collective-permute-start.1 = (bf16[64,2048]{1,0:T(8,128)(2,1)S(1)}, bf16[64,2048]{1,0:T(8,128)(2,1)S(1)}, u32[]{:S(2)}, u32[]{:S(2)}) collective-permute-start(bf16[64,2048]{1,0:T(8,128)(2,1)S(1)} %maximum_maximum_fusion.refs_0_), channel_id=1, source_target_pairs={{0,224},{16,240},{32,0},{48,16},{64,32},{80,48},{96,64},{112,80},{... | collective-permute-start | bytes 786440 | tf_op jit(solution)/shard_map/ppermute | solution.py:73
  7.5 8.4 %collective-permute-start.2 = (bf16[64,2048]{1,0:T(8,128)(2,1)S(1)}, bf16[64,2048]{1,0:T(8,128)(2,1)S(1)}, u32[]{:S(2)}, u32[]{:S(2)}) collective-permute-start(bf16[64,2048]{1,0:T(8,128)(2,1)S(1)} %maximum_maximum_fusion.refs_0_), channel_id=1, source_target_pairs={{0,32},{16,48},{32,64},{48,80},{64,96},{80,112},{96,128},{112,144}... | collective-permute-start | bytes 786440 | tf_op jit(solution)/shard_map/ppermute | solution.py:74
  12.5 7.5 %collective-permute-start.4 = (bf16[64,2048]{1,0:T(8,128)(2,1)S(1)}, bf16[64,2048]{1,0:T(8,128)(2,1)S(1)}, u32[]{:S(2)}, u32[]{:S(2)}) collective-permute-start(bf16[64,2048]{1,0:T(8,128)(2,1)S(1)} %collective-permute-done.1.refs_2_), channel_id=1, source_target_pairs={{0,224},{16,240},{32,0},{48,16},{64,32},{80,48},{96,64},{112,80},{... | collective-permute-start | bytes 786440 | tf_op jit(solution)/shard_map/ppermute | solution.py:73
  15.9 7.5 %collective-permute-start.5 = (bf16[64,2048]{1,0:T(8,128)(2,1)S(1)}, bf16[64,2048]{1,0:T(8,128)(2,1)S(1)}, u32[]{:S(2)}, u32[]{:S(2)}) collective-permute-start(bf16[64,2048]{1,0:T(8,128)(2,1)S(1)} %collective-permute-done.2.refs_3_), channel_id=1, source_target_pairs={{0,32},{16,48},{32,64},{48,80},{64,96},{80,112},{96,128},{112,144}... | collective-permute-start | bytes 786440 | tf_op jit(solution)/shard_map/ppermute | solution.py:74
  15.9 15.5 %collective-permute-start.3 = (bf16[128,2048]{1,0:T(8,128)(2,1)S(1)}, bf16[128,2048]{1,0:T(8,128)(2,1)S(1)}, u32[]{:S(2)}, u32[]{:S(2)}) collective-permute-start(bf16[128,2048]{1,0:T(8,128)(2,1)S(1)} %pad_maximum_fusion), channel_id=1, source_target_pairs={{0,16},{16,0},{32,48},{48,32},{64,80},{80,64},{96,112},{112,96},{1... | collective-permute-start | bytes 1572872 | tf_op jit(solution)/shard_map/ppermute | solution.py:94
  19.9 9.8 %collective-permute-start.9 = (bf16[64,2048]{1,0:T(8,128)(2,1)S(1)}, bf16[64,2048]{1,0:T(8,128)(2,1)S(1)}, u32[]{:S(2)}, u32[]{:S(2)}) collective-permute-start(bf16[64,2048]{1,0:T(8,128)(2,1)S(1)} %collective-permute-done.4.refs_6_), channel_id=1, source_target_pairs={{0,224},{16,240},{32,0},{48,16},{64,32},{80,48},{96,64},{112,80},{... | collective-permute-start | bytes 786440 | tf_op jit(solution)/shard_map/ppermute | solution.py:73
  23.3 6.5 %collective-permute-start.10 = (bf16[64,2048]{1,0:T(8,128)(2,1)S(1)}, bf16[64,2048]{1,0:T(8,128)(2,1)S(1)}, u32[]{:S(2)}, u32[]{:S(2)}) collective-permute-start(bf16[64,2048]{1,0:T(8,128)(2,1)S(1)} %collective-permute-done.5.refs_0_), channel_id=1, source_target_pairs={{0,32},{16,48},{32,64},{48,80},{64,96},{80,112},{96,128},{112,144}... | collective-permute-start | bytes 786440 | tf_op jit(solution)/shard_map/ppermute | solution.py:74
  23.4 24.5 %collective-permute-start = (bf16[64,2048]{1,0:T(8,128)(2,1)S(1)}, bf16[64,2048]{1,0:T(8,128)(2,1)S(1)}, u32[]{:S(2)}, u32[]{:S(2)}) collective-permute-start(bf16[64,2048]{1,0:T(8,128)(2,1)S(1)} %maximum_maximum_fusion.refs_0_), channel_id=1, source_target_pairs={{0,16},{16,0},{32,48},{48,32},{64,80},{80,64},{96,112},{112,96},{1... | collective-permute-start | bytes 786440 | tf_op jit(solution)/shard_map/ppermute | solution.py:92
  24.6 23.2 %collective-permute-start.7 = (bf16[256,256]{1,0:T(8,128)(2,1)}, bf16[256,256]{1,0:T(8,128)(2,1)S(1)}, u32[]{:S(2)}, u32[]{:S(2)}) collective-permute-start(bf16[256,256]{1,0:T(8,128)(2,1)} %param.16), channel_id=1, source_target_pairs={{0,0},{1,16},{2,32},{3,48},{4,64},{5,80},{6,96},{7,112},{8,128},{9... | collective-permute-start | bytes 393224 | tf_op jit(solution)/shard_map/ppermute | solution.py:296
  29.7 18.1 %collective-permute-start.6 = (bf16[128,2048]{1,0:T(8,128)(2,1)S(1)}, bf16[128,2048]{1,0:T(8,128)(2,1)S(1)}, u32[]{:S(2)}, u32[]{:S(2)}) collective-permute-start(bf16[128,2048]{1,0:T(8,128)(2,1)S(1)} %pad_maximum_fusion.1), channel_id=1, source_target_pairs={{0,16},{16,0},{32,48},{48,32},{64,80},{80,64},{96,112},{112,96},{1... | collective-permute-start | bytes 1572872 | tf_op jit(solution)/shard_map/ppermute | solution.py:94
  29.9 32.8 %collective-permute-start.11 = (bf16[128,2048]{1,0:T(8,128)(2,1)S(1)}, bf16[128,2048]{1,0:T(8,128)(2,1)S(1)}, u32[]{:S(2)}, u32[]{:S(2)}) collective-permute-start(bf16[128,2048]{1,0:T(8,128)(2,1)S(1)} %pad_maximum_fusion.2), channel_id=1, source_target_pairs={{0,16},{16,0},{32,48},{48,32},{64,80},{80,64},{96,112},{112,96},{1... | collective-permute-start | bytes 1572872 | tf_op jit(solution)/shard_map/ppermute | solution.py:94
  31.4 12.4 %collective-permute-start.12 = (bf16[32,2048]{1,0:T(8,128)(2,1)S(1)}, bf16[32,2048]{1,0:T(8,128)(2,1)S(1)}, u32[]{:S(2)}, u32[]{:S(2)}) collective-permute-start(bf16[32,2048]{1,0:T(8,128)(2,1)S(1)} %slice.75), channel_id=1, source_target_pairs={{0,224},{16,240},{32,0},{48,16},{64,32},{80,48},{96,64},{112,80},{... | collective-permute-start | bytes 393224 | tf_op jit(solution)/shard_map/ppermute | solution.py:79
  43.8 18.8 %collective-permute-start.13 = (bf16[32,2048]{1,0:T(8,128)(2,1)S(1)}, bf16[32,2048]{1,0:T(8,128)(2,1)S(1)}, u32[]{:S(2)}, u32[]{:S(2)}) collective-permute-start(bf16[32,2048]{1,0:T(8,128)(2,1)S(1)} %slice.76), channel_id=1, source_target_pairs={{0,32},{16,48},{32,64},{48,80},{64,96},{80,112},{96,128},{112,144}... | collective-permute-start | bytes 393224 | tf_op jit(solution)/shard_map/ppermute | solution.py:80
  56.6 22.8 %copy-start = (f32[512,1024]{1,0:T(8,128)}, f32[512,1024]{1,0:T(8,128)S(1)}, u32[]{:S(2)}) copy-start(f32[512,1024]{1,0:T(8,128)S(1)} %get-tuple-element.9.own_ref) | copy-start | bytes 6291460
  56.6 23.6 %collective-permute-start.8 = (bf16[512,1152]{1,0:T(8,128)(2,1)}, bf16[512,1152]{1,0:T(8,128)(2,1)}, u32[]{:S(2)}, u32[]{:S(2)}) collective-permute-start(bf16[512,1152]{1,0:T(8,128)(2,1)} %get-tuple-element.10), channel_id=1, source_target_pairs={{0,1},{1,0},{2,3},{3,2},{4,5},{5,4},{6,7},{7,6},{8,9},{9,8},{10,11... | collective-permute-start | bytes 3538952 | tf_op jit(solution)/shard_map/ppermute | solution.py:302
  62.6 8.0 %collective-permute-start.14 = (bf16[64,2048]{1,0:T(8,128)(2,1)S(1)}, bf16[64,2048]{1,0:T(8,128)(2,1)S(1)}, u32[]{:S(2)}, u32[]{:S(2)}) collective-permute-start(bf16[64,2048]{1,0:T(8,128)(2,1)S(1)} %constant_dynamic-update-slice_fusion.refs_6_), channel_id=1, source_target_pairs={{0,16},{16,0},{32,48},{48,32},{64,80},{80,64},{96,112},{112,96},{1... | collective-permute-start | bytes 786440 | tf_op jit(solution)/shard_map/ppermute | solution.py:96
  79.3 14.8 %collective-permute-start.15 = (bf16[512,1152]{1,0:T(8,128)(2,1)}, bf16[512,1152]{1,0:T(8,128)(2,1)S(1)}, u32[]{:S(2)}, u32[]{:S(2)}) collective-permute-start(bf16[512,1152]{1,0:T(8,128)(2,1)} %get-tuple-element.12), channel_id=1, source_target_pairs={{0,1},{1,0},{2,3},{3,2},{4,5},{5,4},{6,7},{7,6},{8,9},{9,8},{10,11... | collective-permute-start | bytes 3538952 | tf_op jit(solution)/shard_map/ppermute | solution.py:302
  84.3 23.4 %all-to-all-start = ((bf16[8,64,1152]{2,1,0:T(8,128)(2,1)}), bf16[8,64,1152]{2,1,0:T(8,128)(2,1)}, u32[]{:S(2)}, u32[]{:S(2)}) async-start(bf16[8,64,1152]{2,1,0:T(8,128)(2,1)} %bitcast.10), calls=%async_computation | async-start | bytes 2359296 | tf_op jit(solution)/shard_map/all_to_all | solution.py:62
  91.4 91.6 %collective-permute-start.27 = (f32[896,256]{1,0:T(8,128)}, f32[896,256]{1,0:T(8,128)}, u32[]{:S(2)}, u32[]{:S(2)}) collective-permute-start(f32[896,256]{1,0:T(8,128)} %get-tuple-element.18), channel_id=1, source_target_pairs={{0,1},{1,0},{2,3},{3,2},{4,5},{5,4},{6,7},{7,6},{8,9},{9,8},{10,11... | collective-permute-start | bytes 2752520 | tf_op jit(solution)/shard_map/ppermute | solution.py:291
  107.7 20.9 %all-to-all-start.1 = ((bf16[8,64,1152]{2,1,0:T(8,128)(2,1)}), bf16[8,64,1152]{2,1,0:T(8,128)(2,1)S(1)}, u32[]{:S(2)}, u32[]{:S(2)}) async-start(bf16[8,64,1152]{2,1,0:T(8,128)(2,1)} %bitcast.11), calls=%async_computation.1 | async-start | bytes 2359296 | tf_op jit(solution)/shard_map/all_to_all | solution.py:62
  128.8 13.6 %collective-permute-start.16 = (bf16[128,128]{1,0:T(8,128)(2,1)S(1)}, bf16[128,128]{1,0:T(8,128)(2,1)S(1)}, u32[]{:S(2)}, u32[]{:S(2)}) collective-permute-start(bf16[128,128]{1,0:T(8,128)(2,1)S(1)} %fusion.4), channel_id=1, source_target_pairs={{0,0},{1,1},{2,32},{3,33},{4,64},{5,65},{6,96},{7,97},{8,128},{9,1... | collective-permute-start | bytes 98312 | tf_op jit(solution)/shard_map/ppermute | solution.py:308
  131.0 54.3 %all-to-all-start.2 = ((bf16[8,128,896]{2,1,0:T(8,128)(2,1)}), bf16[8,128,896]{2,1,0:T(8,128)(2,1)S(1)}, u32[]{:S(2)}, u32[]{:S(2)}) async-start(bf16[8,128,896]{2,1,0:T(8,128)(2,1)} %tile.6), calls=%async_computation.2 | async-start | bytes 3670016 | tf_op jit(solution)/shard_map/all_to_all | solution.py:62
  142.4 15.2 %collective-permute-start.17 = (bf16[128,128]{1,0:T(8,128)(2,1)S(1)}, bf16[128,128]{1,0:T(8,128)(2,1)S(1)}, u32[]{:S(2)}, u32[]{:S(2)}) collective-permute-start(bf16[128,128]{1,0:T(8,128)(2,1)S(1)} %collective-permute-done.16), channel_id=1, source_target_pairs={{0,16},{16,0},{32,48},{48,32},{64,80},{80,64},{96,112},{112,96},{1... | collective-permute-start | bytes 98312 | tf_op jit(solution)/shard_map/ppermute | solution.py:310
  157.6 3.5 %collective-permute-start.18 = (bf16[128,256]{1,0:T(8,128)(2,1)S(1)}, bf16[128,256]{1,0:T(8,128)(2,1)S(1)}, u32[]{:S(2)}, u32[]{:S(2)}) collective-permute-start(bf16[128,256]{1,0:T(8,128)(2,1)S(1)} %get-tuple-element.26), channel_id=1, source_target_pairs={{0,224},{16,240},{32,0},{48,16},{64,32},{80,48},{96,64},{112,80},{... | collective-permute-start | bytes 196616 | tf_op jit(solution)/shard_map/ppermute | solution.py:73
  157.7 4.7 %collective-permute-start.19 = (bf16[128,256]{1,0:T(8,128)(2,1)S(1)}, bf16[128,256]{1,0:T(8,128)(2,1)S(1)}, u32[]{:S(2)}, u32[]{:S(2)}) collective-permute-start(bf16[128,256]{1,0:T(8,128)(2,1)S(1)} %get-tuple-element.26), channel_id=1, source_target_pairs={{0,32},{16,48},{32,64},{48,80},{64,96},{80,112},{96,128},{112,144}... | collective-permute-start | bytes 196616 | tf_op jit(solution)/shard_map/ppermute | solution.py:74
  161.1 4.0 %collective-permute-start.20 = (bf16[128,256]{1,0:T(8,128)(2,1)S(1)}, bf16[128,256]{1,0:T(8,128)(2,1)S(1)}, u32[]{:S(2)}, u32[]{:S(2)}) collective-permute-start(bf16[128,256]{1,0:T(8,128)(2,1)S(1)} %collective-permute-done.18), channel_id=1, source_target_pairs={{0,224},{16,240},{32,0},{48,16},{64,32},{80,48},{96,64},{112,80},{... | collective-permute-start | bytes 196616 | tf_op jit(solution)/shard_map/ppermute | solution.py:73
  162.4 4.6 %collective-permute-start.21 = (bf16[128,256]{1,0:T(8,128)(2,1)S(1)}, bf16[128,256]{1,0:T(8,128)(2,1)S(1)}, u32[]{:S(2)}, u32[]{:S(2)}) collective-permute-start(bf16[128,256]{1,0:T(8,128)(2,1)S(1)} %collective-permute-done.19), channel_id=1, source_target_pairs={{0,32},{16,48},{32,64},{48,80},{64,96},{80,112},{96,128},{112,144}... | collective-permute-start | bytes 196616 | tf_op jit(solution)/shard_map/ppermute | solution.py:74
  165.1 3.4 %collective-permute-start.22 = (bf16[128,256]{1,0:T(8,128)(2,1)S(1)}, bf16[128,256]{1,0:T(8,128)(2,1)S(1)}, u32[]{:S(2)}, u32[]{:S(2)}) collective-permute-start(bf16[128,256]{1,0:T(8,128)(2,1)S(1)} %collective-permute-done.20), channel_id=1, source_target_pairs={{0,224},{16,240},{32,0},{48,16},{64,32},{80,48},{96,64},{112,80},{... | collective-permute-start | bytes 196616 | tf_op jit(solution)/shard_map/ppermute | solution.py:73
  167.1 4.8 %collective-permute-start.23 = (bf16[128,256]{1,0:T(8,128)(2,1)S(1)}, bf16[128,256]{1,0:T(8,128)(2,1)S(1)}, u32[]{:S(2)}, u32[]{:S(2)}) collective-permute-start(bf16[128,256]{1,0:T(8,128)(2,1)S(1)} %collective-permute-done.21), channel_id=1, source_target_pairs={{0,32},{16,48},{32,64},{48,80},{64,96},{80,112},{96,128},{112,144}... | collective-permute-start | bytes 196616 | tf_op jit(solution)/shard_map/ppermute | solution.py:74
  168.5 4.0 %collective-permute-start.24 = (bf16[64,256]{1,0:T(8,128)(2,1)S(1)}, bf16[64,256]{1,0:T(8,128)(2,1)S(1)}, u32[]{:S(2)}, u32[]{:S(2)}) collective-permute-start(bf16[64,256]{1,0:T(8,128)(2,1)S(1)} %slice.81), channel_id=1, source_target_pairs={{0,224},{16,240},{32,0},{48,16},{64,32},{80,48},{96,64},{112,80},{... | collective-permute-start | bytes 98312 | tf_op jit(solution)/shard_map/ppermute | solution.py:79
  171.9 4.0 %collective-permute-start.25 = (bf16[64,256]{1,0:T(8,128)(2,1)S(1)}, bf16[64,256]{1,0:T(8,128)(2,1)S(1)}, u32[]{:S(2)}, u32[]{:S(2)}) collective-permute-start(bf16[64,256]{1,0:T(8,128)(2,1)S(1)} %slice.82), channel_id=1, source_target_pairs={{0,32},{16,48},{32,64},{48,80},{64,96},{80,112},{96,128},{112,144}... | collective-permute-start | bytes 98312 | tf_op jit(solution)/shard_map/ppermute | solution.py:80
  175.9 8.6 %collective-permute-start.26 = (bf16[1024,256]{1,0:T(8,128)(2,1)S(1)}, bf16[1024,256]{1,0:T(8,128)(2,1)S(1)}, u32[]{:S(2)}, u32[]{:S(2)}) collective-permute-start(bf16[1024,256]{1,0:T(8,128)(2,1)S(1)} %constant_dynamic-update-slice_fusion.4.own_acts_ref), channel_id=1, source_target_pairs={{0,1},{1,0},{2,3},{3,2},{4,5},{5,4},{6,7},{7,6},{8,9},{9,8},{10,11... | collective-permute-start | bytes 1572872 | tf_op jit(solution)/shard_map/ppermute | solution.py:314
  (11 other events, 26.5 us)

commit v3 on v1

v3 whole, which is shorter than its diff:
```python
import functools

import jax
import jax.numpy as jnp
from jax import lax
from jax.experimental import pallas as pl
from jax.experimental.pallas import tpu as pltpu
from jax.sharding import PartitionSpec as P

IN = 4096
OUT = 28672
TS = 32
TQ = 32

damping = 0.1

NZ, NYL, NX, NYH, NC = 8, 2, 4, 2, 2
GROUPS = NZ * NYL
CHIPS = NX * NYH


def dp_index(z, yl):
    return (z % NZ) * NYL + yl % NYL


def mp_index(x, yh, core):
    return ((x % NX) * NYH + yh % NYH) * NC + core % NC


def dp_shift(dz, dyl):
    return [
        (dp_index(z, y), dp_index(z + dz, y + dyl)) for z in range(NZ) for y in range(NYL)
    ]


CORE_SWAP = [
    (mp_index(x, h, c), mp_index(x, h, c + 1))
    for x in range(NX)
    for h in range(NYH)
    for c in range(NC)
]
TRANSPOSE = [(d * 16 + m, m * 16 + d) for d in range(16) for m in range(16)]
SAME_CORE = [
    [mp_index(x, h, c) for x in range(NX) for h in range(NYH)] for c in range(NC)
]

CHUNKS = (
    ((0, 0), (0, 1), (1, 0), (-1, 0), (1, 1), (-1, 1), (2, 0), (-2, 0)),
    ((2, 1), (-2, 1), (3, 0), (-3, 0), (3, 1), (-3, 1), (4, 0), (4, 1)),
)


def dp_swap(z_bit, y_bit):
    return [
        (dp_index(z, y), dp_index(z ^ z_bit, y ^ y_bit)) for z in range(NZ) for y in range(NYL)
    ]


DP_SWAPS = tuple(dp_swap(*bits) for bits in ((0, 1), (1, 0), (2, 0), (4, 0)))


def exchange(x, axis, **kw):
    return lax.all_to_all(x, axis, 0, 0, tiled=True, **kw)


def share(x, count, axis, **kw):
    return exchange(jnp.tile(x, (count, 1)), axis, **kw)


def fence_kernel(*refs):
    del refs


def fence(*arrays):
    anywhere = pl.BlockSpec(memory_space=pl.ANY)
    return pl.pallas_call(
        fence_kernel,
        out_shape=[jax.ShapeDtypeStruct(a.shape, a.dtype) for a in arrays],
        in_specs=[anywhere] * len(arrays),
        out_specs=[anywhere] * len(arrays),
        input_output_aliases={i: i for i in range(len(arrays))},
        compiler_params=pltpu.CompilerParams(vmem_limit_bytes=1024 * 1024),
    )(*arrays)


def up(x):
    return lax.ppermute(x, "dp", dp_shift(-1, 0))


def down(x):
    return lax.ppermute(x, "dp", dp_shift(1, 0))


def over(x):
    return lax.ppermute(x, "dp", dp_shift(0, 1))


def turn_kernel(count, core_ref, *refs):
    del core_ref
    blocks, basis_ref = refs[:count], refs[count]
    sib_ref, own_ref, tokens = refs[-3:]
    rows = blocks[0].shape[0]
    step = pl.program_id(0)

    @pl.when(step == 0)
    def _():
        for r, ref in enumerate(blocks):
            tokens[r * rows : (r + 1) * rows, :] = ref[...]
        sib_ref[...] = jnp.dot(
            tokens[...], basis_ref[...], preferred_element_type=jnp.float32
        ).astype(jnp.bfloat16)

    @pl.when(step == 1)
    def _():
        own_ref[...] = jnp.dot(
            tokens[...], basis_ref[...], preferred_element_type=jnp.float32
        )


def turn(core, blocks, basis, needs=()):
    rows, features = blocks[0].shape
    units = basis.shape[1] // 2
    tokens = rows * len(blocks)
    whole = lambda i, core_ref: (0, 0)
    side = lambda i, core_ref: (0, jnp.where(i == 0, 1 - core_ref[0], core_ref[0]))
    return pl.pallas_call(
        functools.partial(turn_kernel, len(blocks)),
        grid_spec=pltpu.PrefetchScalarGridSpec(
            num_scalar_prefetch=1,
            grid=(2,),
            in_specs=[pl.BlockSpec((rows, features), whole)] * len(blocks)
            + [pl.BlockSpec((features, units), side)]
            + [pl.BlockSpec(memory_space=pl.ANY)] * len(needs),
            out_specs=[pl.BlockSpec((tokens, units), whole)] * 2,
            scratch_shapes=[pltpu.VMEM((tokens, features), jnp.bfloat16)],
        ),
        out_shape=[
            jax.ShapeDtypeStruct((tokens, units), jnp.bfloat16),
            jax.ShapeDtypeStruct((tokens, units), jnp.float32),
        ],
        compiler_params=pltpu.CompilerParams(vmem_limit_bytes=56 * 1024 * 1024),
        cost_estimate=pl.CostEstimate(
            flops=2 * tokens * features * units * 2,
            bytes_accessed=2 * tokens * (features + 3 * units) + 4 * features * units,
            transcendentals=0,
        ),
    )(core.reshape(1), *blocks, basis, *needs)


def after(x, y):
    return x + jnp.minimum(jnp.abs(y[:1, :1]), 0).astype(x.dtype)


def sum_kernel(parts_ref, *refs):
    out_ref = refs[-1]
    rows = parts_ref.shape[0] // CHIPS
    total = parts_ref[:rows, :].astype(jnp.float32)
    for i in range(1, CHIPS):
        total = total + parts_ref[i * rows : (i + 1) * rows, :].astype(jnp.float32)
    total = total.astype(jnp.bfloat16)
    for i in range(CHIPS):
        out_ref[i * rows : (i + 1) * rows, :] = total


def sum_and_copy(parts, *needs):
    vmem = pl.BlockSpec(memory_space=pltpu.VMEM)
    return pl.pallas_call(
        sum_kernel,
        out_shape=jax.ShapeDtypeStruct(parts.shape, jnp.bfloat16),
        in_specs=[vmem] + [pl.BlockSpec(memory_space=pl.ANY)] * len(needs),
        out_specs=vmem,
        compiler_params=pltpu.CompilerParams(vmem_limit_bytes=16 * 1024 * 1024),
        cost_estimate=pl.CostEstimate(
            flops=parts.size, bytes_accessed=parts.size * 4, transcendentals=0
        ),
    )(parts, *needs)


def score_kernel(acts_at_ref, place_ref, grads_hbm, own_acts_ref, sib_acts_ref, own_hbm,
                 sib_hbm, out_ref, train_grads, query_acts, train_acts, sums, grads_ref,
                 own_inv_ref, sib_inv_ref, arrived):
    rows = TQ + TS
    copies = [
        pltpu.make_async_copy(source, target, arrived.at[i])
        for i, (source, target) in enumerate(
            ((grads_hbm, grads_ref), (own_hbm, own_inv_ref), (sib_hbm, sib_inv_ref))
        )
    ]
    for copy in copies:
        copy.start()
    for r in range(GROUPS):
        for part, ref in ((0, own_acts_ref), (1, sib_acts_ref)):
            start = pl.multiple_of(acts_at_ref[r], rows)
            middle = pl.multiple_of(start + TQ, TQ)
            lanes = slice(part * 256, part * 256 + 256)
            query_acts[r * TQ : (r + 1) * TQ, lanes] = ref[pl.ds(start, TQ), :]
            train_acts[r * TS : (r + 1) * TS, lanes] = ref[pl.ds(middle, TS), :].astype(
                jnp.float32
            )
    copies[0].wait()
    for r in range(GROUPS):
        train_grads[r * TS : (r + 1) * TS, :] = grads_ref[r * rows + TQ : (r + 1) * rows, :]
    copies[1].wait()
    copies[2].wait()

    def one_query(n):
        grads = grads_ref[pl.ds(pl.multiple_of(n * rows, rows), TQ), :]
        total = jnp.zeros((GROUPS, 128), jnp.float32)
        for at, inv_ref in ((0, own_inv_ref), (256, sib_inv_ref)):
            acts = query_acts[pl.ds(pl.multiple_of(n * TQ, TQ), TQ), at : at + 256]
            gradient = lax.dot_general(
                grads, acts, (((0,), (0,)), ((), ())), preferred_element_type=jnp.float32
            )
            preconditioned = (gradient * inv_ref[...]).astype(jnp.bfloat16)
            projected = jnp.dot(
                train_grads[...], preconditioned, preferred_element_type=jnp.float32
            )
            terms = projected * train_acts[:, at : at + 256]
            terms = terms.reshape(GROUPS, TS, 256).sum(1)
            total = total + terms[:, :128] + terms[:, 128:]
        sums[pl.ds(n, 1)] = total[None]

    def four_queries(i, carry):
        for j in range(4):
            one_query(i * 4 + j)
        return carry

    lax.fori_loop(0, GROUPS // 4, four_queries, 0)
    scores = jnp.sum(sums[...], axis=2)
    hot = place_ref[...]
    scores = jnp.dot(
        hot, jnp.dot(scores, jnp.transpose(hot), precision=lax.Precision.HIGHEST),
        precision=lax.Precision.HIGHEST,
    )
    out_ref[...] = jnp.concatenate(
        [scores, jnp.zeros((GROUPS, 128 - GROUPS), jnp.float32)], 1
    )


def score_blocks(acts_at, place, grads, own_acts, sib_acts, own_inv, sib_inv):
    units, features = own_inv.shape
    vmem = pl.BlockSpec(memory_space=pltpu.VMEM)
    smem = pl.BlockSpec(memory_space=pltpu.SMEM)
    hbm = pl.BlockSpec(memory_space=pl.ANY)
    return pl.pallas_call(
        score_kernel,
        out_shape=jax.ShapeDtypeStruct((GROUPS, 128), jnp.float32),
        in_specs=[smem, vmem, hbm, vmem, vmem, hbm, hbm],
        out_specs=vmem,
        scratch_shapes=[
            pltpu.VMEM((GROUPS * TS, units), jnp.bfloat16),
            pltpu.VMEM((GROUPS * TQ, 2 * features), jnp.bfloat16),
            pltpu.VMEM((GROUPS * TS, 2 * features), jnp.float32),
            pltpu.VMEM((GROUPS, GROUPS, 128), jnp.float32),
            pltpu.VMEM(grads.shape, jnp.bfloat16),
            pltpu.VMEM((units, features), jnp.float32),
            pltpu.VMEM((units, features), jnp.float32),
            pltpu.SemaphoreType.DMA((3,)),
        ],
        compiler_params=pltpu.CompilerParams(vmem_limit_bytes=56 * 1024 * 1024),
        cost_estimate=pl.CostEstimate(
            flops=2 * GROUPS * units * 2 * features * (GROUPS * TS + TQ),
            bytes_accessed=8 * 1024 * 1024,
            transcendentals=0,
        ),
    )(acts_at, place, grads, own_acts, sib_acts, own_inv, sib_inv)


def shards(query_acts, query_grads, train_acts, train_grads, basis_in, basis_out, eigen):
    in_local = query_acts.shape[2]
    out_local = query_grads.shape[2]
    acts = jnp.concatenate([query_acts[0], train_acts[0]], 0)
    grads = jnp.concatenate([query_grads[0], train_grads[0]], 0)
    dp, mp = lax.axis_index("dp"), lax.axis_index("mp")
    z, yl, core = dp // NYL, dp % NYL, mp % NC
    units = out_local // 2
    rows = TQ + TS

    own_inv = 1.0 / (lax.dynamic_slice_in_dim(eigen, core * units, units, 0) + damping)
    sib_eigen = lax.ppermute(
        lax.dynamic_slice_in_dim(eigen, (1 - core) * units, units, 0), "mp", CORE_SWAP
    )
    sib_inv = 1.0 / (sib_eigen + damping)

    held = {(0, 0): grads}
    moved = lax.ppermute(acts, ("dp", "mp"), TRANSPOSE)
    held[(0, 0)], held[(1, 0)], held[(-1, 0)], held[(0, 1)] = fence(
        grads, up(grads), down(grads), over(grads)
    )
    held[(1, 0)], held[(-1, 0)], held[(2, 0)], held[(-2, 0)], held[(1, 1)] = fence(
        held[(1, 0)], held[(-1, 0)], up(held[(1, 0)]), down(held[(-1, 0)]),
        over(held[(1, 0)]),
    )
    (held[(2, 0)], held[(-2, 0)], held[(3, 0)], held[(-3, 0)], held[(1, 1)], held[(-1, 1)],
     moved) = fence(
        held[(2, 0)], held[(-2, 0)], up(held[(2, 0)]), down(held[(-2, 0)]), held[(1, 1)],
        over(held[(-1, 0)]), moved,
    )
    every_acts = share(moved, GROUPS, "mp")
    held[(3, 0)], held[(-3, 0)], held[(2, 1)], held[(-2, 1)], held[(4, 0)], held[(3, 1)] = fence(
        held[(3, 0)], held[(-3, 0)], up(held[(1, 1)]), down(held[(-1, 1)]), down(held[(-3, 0)]),
        over(held[(3, 0)]),
    )
    held[(4, 1)], held[(-3, 1)] = up(held[(3, 1)]), over(held[(-3, 0)])

    summed = jnp.dot(every_acts, basis_in, preferred_element_type=jnp.float32)
    bits = (yl, z % 2, z // 2 % 2, z // 4)
    sums = []
    for k, (swap, bit) in enumerate(zip(DP_SWAPS, bits)):
        half = summed.shape[0] // 2
        away = lax.dynamic_slice_in_dim(summed, (1 - bit) * half, half, 0)
        mine = lax.dynamic_slice_in_dim(summed, bit * half, half, 0)
        if k == 0:
            first = away = away.astype(jnp.bfloat16)
        summed = mine + lax.ppermute(away, "dp", swap).astype(jnp.float32)
        sums.append(summed)
    own_acts = summed.astype(jnp.bfloat16)

    pairs = []
    for chunk, needs in zip(CHUNKS, ((held[(3, 1)],), (own_inv, sib_inv, first))):
        sib_part, own_part = turn(core, [held[place] for place in chunk], basis_out, needs)
        got = lax.ppermute(sib_part, "mp", CORE_SWAP).astype(jnp.float32)
        if pairs:
            got = after(got, sums[0])
        pairs.append((own_part + got).astype(jnp.bfloat16))
    pairs = jnp.concatenate(pairs, 0)
    parts = exchange(pairs, "mp", axis_index_groups=SAME_CORE)
    copies = sum_and_copy(parts)

    own_acts = after(own_acts, copies)
    for swap in DP_SWAPS[::-1]:
        own_acts = jnp.concatenate([own_acts, lax.ppermute(own_acts, "dp", swap)], 0)
    sib_acts = lax.ppermute(own_acts, "mp", CORE_SWAP)

    all_grads = exchange(copies, "mp", axis_index_groups=SAME_CORE)

    places = [place for chunk in CHUNKS for place in chunk]
    dz = jnp.array([p[0] for p in places], jnp.int32)
    dy = jnp.array([p[1] for p in places], jnp.int32)
    order = ((z + dz + NZ) % NZ) * NYL + (yl + dy) % NYL
    place = (order[None, :] == jnp.arange(GROUPS, dtype=jnp.int32)[:, None]).astype(jnp.float32)

    kept = bits[0] * 8 + bits[1] * 4 + bits[2] * 2 + bits[3]
    acts_at = (order ^ kept) * rows

    scores = score_blocks(
        acts_at, place, all_grads, own_acts, sib_acts, own_inv, sib_inv
    )
    normalizer = float(TQ * TS * IN * OUT) ** (-0.5)
    scores = share(scores * normalizer, GROUPS, "mp").reshape(GROUPS, GROUPS, 128).sum(0)
    scores = share(scores, GROUPS, "dp").reshape(GROUPS, GROUPS, 128).sum(0)
    return scores[:, :GROUPS]


def solution(mesh):
    placed = (
        P("dp", None, "mp"),
        P("dp", None, "mp"),
        P("dp", None, "mp"),
        P("dp", None, "mp"),
        P("dp", "mp"),
        P("mp", "dp"),
        P("dp", "mp"),
    )
    return jax.shard_map(shards, mesh=mesh, in_specs=placed, out_specs=P(), check_vma=False)
```

time: 245 us -> 206 us (0.84)
  waiting for transfers between devices: 100 us -> 63.7 us
  Pallas kernels: 16.8 us -> 34.2 us
  matrix products: 16.7 us -> 0.29 us
  local copies, waits for them, and re-layouts: 18.7 us -> 4.64 us
  other arithmetic: 6.73 us -> 12.4 us
  starting transfers between devices: 57 us -> 61.9 us
    all_to_all x5 -> x3, waiting for transfers between devices: 73 us -> 11.4 us  [exchange(): return lax.all_to_all(x, axis, 0, 0, tiled=True, **kw)]
    ppermute x15 -> x26, waiting for transfers between devices: 27.5 us -> 49.9 us  [the longest x4 23 us: shards(): lax.ppermute(own_acts, 'dp', swap)]
    pallas_call x0 -> x7, Pallas kernels: none -> 16.7 us  [the longest x2 16.4 us: turn(): pl.pallas_call(functools.partial(turn_kernel, len(blocks)), grid_spec=plt...]
    dot_general x3 -> x1, matrix products: 16.7 us -> 0.29 us  [shards(): summed = jnp.dot(every_acts, basis_in, preferred_element_type=jnp.float32)]
    unnamed x28 -> x53, local copies, waits for them, and re-layouts: 14.8 us -> 1.81 us
    all_to_all x5 -> x3, starting transfers between devices: 34 us -> 23.3 us  [exchange(): return lax.all_to_all(x, axis, 0, 0, tiled=True, **kw)]
    ppermute x15 -> x26, starting transfers between devices: 19.7 us -> 30.2 us  [the longest x5 17.5 us: up(): return lax.ppermute(x, 'dp', dp_shift(-1, 0))]
    ppermute x1, starting transfers between devices: 0.01 us -> 2.73 us  [shards(): sib_acts = lax.ppermute(own_acts, 'mp', CORE_SWAP)]
  transfers between devices with their start and end apart: 22 -> 31, of which waited for: 13 -> 12; matrix products, arithmetic and copies ran while one was open for 14% -> 6% of each run, Pallas kernels for 0% -> 8%
where the time goes in v3:
time: 206 us
  waiting for transfers between devices  63.7 us (31%)
  starting transfers between devices  61.9 us (30%)
  Pallas kernels  34.2 us (17%)
  blocking collectives  26.4 us (13%)
  other arithmetic  12.4 us (6%)
  local copies, waits for them, and re-layouts  4.64 us (2%)
    all_to_all x2, blocking collectives, exchange(): return lax.all_to_all(x, axis, 0, 0, tiled=True, **kw)  26.4 us
    all_to_all x3, starting transfers between devices, exchange(): return lax.all_to_all(x, axis, 0, 0, tiled=True, **kw)  23.3 us
    ppermute x4, waiting for transfers between devices, shards(): lax.ppermute(own_acts, 'dp', swap)  23 us
    ppermute x4, waiting for transfers between devices, shards(): summed = mine + lax.ppermute(away, 'dp', swap).astype(jnp.float32)  21.1 us
    pallas_call x1, Pallas kernels, score_blocks(): pl.pallas_call(score_kernel, out_shape=jax.ShapeDtypeStruct((GROUPS, 128)...  17.5 us
    ppermute x5, starting transfers between devices, up(): return lax.ppermute(x, 'dp', dp_shift(-1, 0))  17.5 us
    pallas_call x2, Pallas kernels, turn(): pl.pallas_call(functools.partial(turn_kernel, len(blocks)), grid_spec=plt...  16.4 us
    all_to_all x3, waiting for transfers between devices, exchange(): return lax.all_to_all(x, axis, 0, 0, tiled=True, **kw)  11.4 us
  transfers between devices with their start and end apart: 31, of which 12 were waited for; matrix products, arithmetic and copies ran while one was open for 6% of the time, Pallas kernels for 8%

profile of v3, /device:TPU:1, one launch (start us, length us, event | category | flops | bytes accessed | tf_op | source)
XLA Modules:
  0.0 205.5 jit_solution(2315207044383876749)
XLA Ops:
  1.0 2.2 %collective-permute-start.2 = (bf16[64,1792]{1,0:T(8,128)(2,1)S(1)}, bf16[64,1792]{1,0:T(8,128)(2,1)S(1)}, u32[]{:S(2)}, u32[]{:S(2)}) collective-permute-start(bf16[64,1792]{1,0:T(8,128)(2,1)S(1)} %pad_maximum_fusion.2.refs_0_), channel_id=1, source_target_pairs={{0,16},{16,0},{32,48},{48,32},{64,80},{80,64},{96,112},{112,96},{1... | collective-permute-start | bytes 688136 | tf_op jit(solution)/shard_map/ppermute | solution.py:95
  3.2 1.6 collective-permute-start.1
  4.9 3.9 %collective-permute-start = (bf16[64,1792]{1,0:T(8,128)(2,1)S(1)}, bf16[64,1792]{1,0:T(8,128)(2,1)S(1)}, u32[]{:S(2)}, u32[]{:S(2)}) collective-permute-start(bf16[64,1792]{1,0:T(8,128)(2,1)S(1)} %pad_maximum_fusion.2.refs_0_), channel_id=1, source_target_pairs={{0,224},{16,240},{32,0},{48,16},{64,32},{80,48},{96,64},{112,80},{... | collective-permute-start | bytes 688136 | tf_op jit(solution)/shard_map/ppermute | solution.py:87
  8.8 5.0 %collective-permute-done.1.refs_2_ = bf16[64,1792]{1,0:T(8,128)(2,1)S(1)} collective-permute-done((bf16[64,1792]{1,0:T(8,128)(2,1)S(1)}, bf16[64,1792]{1,0:T(8,128)(2,1)S(1)}, u32[]{:S(2)}, u32[]{:S(2)}) %collective-permute-start.1) | collective-permute-done | bytes 229408 | tf_op jit(solution)/shard_map/ppermute | solution.py:91
  14.1 2.3 %collective-permute-start.3 = (bf16[64,1792]{1,0:T(8,128)(2,1)S(1)}, bf16[64,1792]{1,0:T(8,128)(2,1)S(1)}, u32[]{:S(2)}, u32[]{:S(2)}) collective-permute-start(bf16[64,1792]{1,0:T(8,128)(2,1)S(1)} %get-tuple-element.33.refs_0_), channel_id=1, source_target_pairs={{0,224},{16,240},{32,0},{48,16},{64,32},{80,48},{96,64},{112,80},{... | collective-permute-start | bytes 688136 | tf_op jit(solution)/shard_map/ppermute | solution.py:87
  16.4 2.9 %constant_dynamic-slice_fusion.3 = (f32[896,256]{1,0:T(8,128)}, f32[896,256]{1,0:T(8,128)}) fusion(f32[1792,256]{1,0:T(8,128)} %param.15, s32[]{:T(128)S(6)} %select_n.79, s32[]{:T(128)S(6)} %select_n.78), kind=kLoop, calls=%fused_computation.27 | loop fusion | flops 458752 | bytes 3670024 | tf_op jit(solution)/shard_map/dynamic_slice | solution.py:281
  19.3 2.4 %collective-permute-start.17 = (f32[896,256]{1,0:T(8,128)}, f32[896,256]{1,0:T(8,128)}, u32[]{:S(2)}, u32[]{:S(2)}) collective-permute-start(f32[896,256]{1,0:T(8,128)} %get-tuple-element.61), channel_id=1, source_target_pairs={{0,1},{1,0},{2,3},{3,2},{4,5},{5,4},{6,7},{7,6},{8,9},{9,8},{10,11... | collective-permute-start | bytes 2752520 | tf_op jit(solution)/shard_map/ppermute | solution.py:280
  23.8 2.2 %collective-permute-start.6 = (bf16[64,1792]{1,0:T(8,128)(2,1)S(1)}, bf16[64,1792]{1,0:T(8,128)(2,1)S(1)}, u32[]{:S(2)}, u32[]{:S(2)}) collective-permute-start(bf16[64,1792]{1,0:T(8,128)(2,1)S(1)} %get-tuple-element.37.refs_0_), channel_id=1, source_target_pairs={{0,224},{16,240},{32,0},{48,16},{64,32},{80,48},{96,64},{112,80},{... | collective-permute-start | bytes 688136 | tf_op jit(solution)/shard_map/ppermute | solution.py:87
  26.0 5.7 %collective-permute-start.9 = (bf16[64,256]{1,0:T(8,128)(2,1)S(1)}, bf16[64,256]{1,0:T(8,128)(2,1)S(1)}, u32[]{:S(2)}, u32[]{:S(2)}) collective-permute-start(bf16[64,256]{1,0:T(8,128)(2,1)S(1)} %pad_maximum_fusion.5), channel_id=1, source_target_pairs={{0,0},{1,16},{2,32},{3,48},{4,64},{5,80},{6,96},{7,112},{8,128},{9... | collective-permute-start | bytes 98312 | tf_op jit(solution)/shard_map/ppermute | solution.py:286
  31.7 2.1 collective-permute-done.9.refs_6_
  33.8 6.1 %collective-permute-start.10 = (bf16[64,1792]{1,0:T(8,128)(2,1)S(1)}, bf16[64,1792]{1,0:T(8,128)(2,1)S(1)}, u32[]{:S(2)}, u32[]{:S(2)}) collective-permute-start(bf16[64,1792]{1,0:T(8,128)(2,1)S(1)} %get-tuple-element.40.refs_4_), channel_id=1, source_target_pairs={{0,224},{16,240},{32,0},{48,16},{64,32},{80,48},{96,64},{112,80},{... | collective-permute-start | bytes 688136 | tf_op jit(solution)/shard_map/ppermute | solution.py:87
  40.9 12.3 %all-to-all-start = ((bf16[16,64,256]{2,1,0:T(8,128)(2,1)}), bf16[16,64,256]{2,1,0:T(8,128)(2,1)S(1)}, u32[]{:S(2)}, u32[]{:S(2)}) async-start(bf16[16,64,256]{2,1,0:T(8,128)(2,1)} %tile.6), calls=%async_computation | async-start | bytes 1048576 | tf_op jit(solution)/shard_map/all_to_all | solution.py:63
  54.5 3.0 %collective-permute-start.16 = (bf16[64,1792]{1,0:T(8,128)(2,1)S(1)}, bf16[64,1792]{1,0:T(8,128)(2,1)}, u32[]{:S(2)}, u32[]{:S(2)}) collective-permute-start(bf16[64,1792]{1,0:T(8,128)(2,1)S(1)} %get-tuple-element.46.refs_9_.refs_4_), channel_id=1, source_target_pairs={{0,224},{16,240},{32,0},{48,16},{64,32},{80,48},{96,64},{112,80},{... | collective-permute-start | bytes 688136 | tf_op jit(solution)/shard_map/ppermute | solution.py:87
  57.5 8.2 %shard_map.95 = (bf16[512,896]{1,0:T(8,128)(2,1)}, f32[512,896]{1,0:T(8,128)}) custom-call(s32[1]{0:T(128)} %bitcast.core_ref, bf16[64,1792]{1,0:T(8,128)(2,1)} %copy-done.2, bf16[64,1792]{1,0:T(8,128)(2,1)} %copy-done.10, bf16[64,1792]{1,0:T(8,128)(2,1)} %copy-done.4, bf16[64,1792]{1,0:T(8,128)(2,1)} %copy-done.3, bf16[64,1792]{1,0:T(8,128)(2,1)} %copy-done.5, ...), custom_call_target="tpu_custom_call" | custom-call | flops 3288334336 | bytes 11010048 | tf_op jit(solution)/shard_map/pallas_call | solution.py:126
  66.4 2.2 %add_divide_fusion.refs_10_.sib_hbm = f32[896,256]{1,0:T(8,128)} fusion(f32[896,256]{1,0:T(8,128)} %collective-permute-done.17), kind=kLoop, calls=%fused_computation.3 | loop fusion | flops 458752 | bytes 1835008 | tf_op jit(solution)/shard_map/div | solution.py:283
  69.7 8.2 %shard_map.96 = (bf16[512,896]{1,0:T(8,128)(2,1)}, f32[512,896]{1,0:T(8,128)}) custom-call(s32[1]{0:T(128)} %bitcast.core_ref, bf16[64,1792]{1,0:T(8,128)(2,1)} %copy-done.11, bf16[64,1792]{1,0:T(8,128)(2,1)} %copy-done.12, bf16[64,1792]{1,0:T(8,128)(2,1)} %copy-done.6, bf16[64,1792]{1,0:T(8,128)(2,1)} %copy-done.8, bf16[64,1792]{1,0:T(8,128)(2,1)} %copy-done.13, ...), custom_call_target="tpu_custom_call" | custom-call | flops 3288334336 | bytes 11010048 | tf_op jit(solution)/shard_map/pallas_call | solution.py:126
  78.4 7.1 %collective-permute-done.19 = bf16[512,256]{1,0:T(8,128)(2,1)S(1)} collective-permute-done((bf16[512,256]{1,0:T(8,128)(2,1)S(1)}, bf16[512,256]{1,0:T(8,128)(2,1)S(1)}, u32[]{:S(2)}, u32[]{:S(2)}) %collective-permute-start.19) | collective-permute-done | bytes 262176 | tf_op jit(solution)/shard_map/ppermute | solution.py:315
  86.8 2.0 add_convert_fusion.1
  90.7 7.4 %all-to-all-start.1 = ((bf16[8,128,896]{2,1,0:T(8,128)(2,1)}), bf16[8,128,896]{2,1,0:T(8,128)(2,1)S(1)}, u32[]{:S(2)}, u32[]{:S(2)}) async-start(bf16[8,128,896]{2,1,0:T(8,128)(2,1)} %bitcast.17), calls=%async_computation.1 | async-start | bytes 3670016 | tf_op jit(solution)/shard_map/all_to_all | solution.py:63
  98.3 6.2 %collective-permute-done.20 = f32[256,256]{1,0:T(8,128)S(1)} collective-permute-done((f32[256,256]{1,0:T(8,128)S(1)}, f32[256,256]{1,0:T(8,128)S(1)}, u32[]{:S(2)}, u32[]{:S(2)}) %collective-permute-start.20) | collective-permute-done | bytes 262176 | tf_op jit(solution)/shard_map/ppermute | solution.py:315
  104.7 7.8 %collective-permute-done.21 = f32[128,256]{1,0:T(8,128)S(1)} collective-permute-done((f32[128,256]{1,0:T(8,128)S(1)}, f32[128,256]{1,0:T(8,128)S(1)}, u32[]{:S(2)}, u32[]{:S(2)}) %collective-permute-start.21) | collective-permute-done | bytes 131104 | tf_op jit(solution)/shard_map/ppermute | solution.py:315
  112.9 11.4 %all-to-all-done.1 = bf16[8,128,896]{2,1,0:T(8,128)(2,1)S(1)} async-done(((bf16[8,128,896]{2,1,0:T(8,128)(2,1)}), bf16[8,128,896]{2,1,0:T(8,128)(2,1)S(1)}, u32[]{:S(2)}, u32[]{:S(2)}) %all-to-all-start.1) | async-done | bytes 1835040 | tf_op jit(solution)/shard_map/all_to_all | solution.py:63
  125.8 3.6 %all-to-all-start.2 = ((bf16[8,128,896]{2,1,0:T(8,128)(2,1)}), bf16[8,128,896]{2,1,0:T(8,128)(2,1)S(1)}, u32[]{:S(2)}, u32[]{:S(2)}) async-start(bf16[8,128,896]{2,1,0:T(8,128)(2,1)} %bitcast.16), calls=%async_computation.2 | async-start | bytes 3670016 | tf_op jit(solution)/shard_map/all_to_all | solution.py:63
  129.4 1.7 collective-permute-start.23
  131.2 5.0 %collective-permute-done.23 = bf16[64,256]{1,0:T(8,128)(2,1)S(1)} collective-permute-done((bf16[64,256]{1,0:T(8,128)(2,1)S(1)}, bf16[64,256]{1,0:T(8,128)(2,1)S(1)}, u32[]{:S(2)}, u32[]{:S(2)}) %collective-permute-start.23) | collective-permute-done | bytes 32800 | tf_op jit(solution)/shard_map/ppermute | solution.py:332
  136.2 4.3 %collective-permute-done.24 = bf16[128,256]{1,0:T(8,128)(2,1)S(1)} collective-permute-done((bf16[128,256]{1,0:T(8,128)(2,1)S(1)}, bf16[128,256]{1,0:T(8,128)(2,1)S(1)}, u32[]{:S(2)}, u32[]{:S(2)}) %collective-permute-start.24) | collective-permute-done | bytes 65568 | tf_op jit(solution)/shard_map/ppermute | solution.py:332
  140.6 4.8 %collective-permute-done.25 = bf16[256,256]{1,0:T(8,128)(2,1)S(1)} collective-permute-done((bf16[256,256]{1,0:T(8,128)(2,1)S(1)}, bf16[256,256]{1,0:T(8,128)(2,1)S(1)}, u32[]{:S(2)}, u32[]{:S(2)}) %collective-permute-start.25) | collective-permute-done | bytes 131104 | tf_op jit(solution)/shard_map/ppermute | solution.py:332
  145.6 8.9 %collective-permute-done.26 = bf16[512,256]{1,0:T(8,128)(2,1)S(1)} collective-permute-done((bf16[512,256]{1,0:T(8,128)(2,1)S(1)}, bf16[512,256]{1,0:T(8,128)(2,1)S(1)}, u32[]{:S(2)}, u32[]{:S(2)}) %collective-permute-start.26) | collective-permute-done | bytes 262176 | tf_op jit(solution)/shard_map/ppermute | solution.py:332
  154.6 2.7 %collective-permute-start.27 = (bf16[1024,256]{1,0:T(8,128)(2,1)S(1)}, bf16[1024,256]{1,0:T(8,128)(2,1)S(1)}, u32[]{:S(2)}, u32[]{:S(2)}) collective-permute-start(bf16[1024,256]{1,0:T(8,128)(2,1)S(1)} %constant_dynamic-update-slice_fusion.own_acts_ref), channel_id=1, source_target_pairs={{0,1},{1,0},{2,3},{3,2},{4,5},{5,4},{6,7},{7,6},{8,9},{9,8},{10,11... | collective-permute-start | bytes 1572872 | tf_op jit(solution)/shard_map/ppermute | solution.py:333
  160.2 17.5 %shard_map.98 = f32[16,128]{1,0:T(8,128)} custom-call(s32[16]{0:T(128)} %get-tuple-element.59.acts_at_ref, f32[16,16]{1,0:T(8,128)} %fusion.1.place_ref, bf16[1024,896]{1,0:T(8,128)(2,1)} %bitcast.19, bf16[1024,256]{1,0:T(8,128)(2,1)} %copy-done.21, bf16[1024,256]{1,0:T(8,128)(2,1)} %copy-done.24, f32[896,256]{1,0:T(8,128)} %get-tuple-element.62.refs_9_.own_hbm, ...), custom_call_target="tpu_custom_call" | custom-call | flops 7985954816 | bytes 8388608 | tf_op jit(solution)/shard_map/pallas_call | solution.py:245
  178.5 14.3 %all_to_all.43 = f32[16,16,128]{2,1,0:T(8,128)S(1)} all-to-all(f32[16,16,128]{2,1,0:T(8,128)S(1)} %tile.7), channel_id=1, replica_groups=mesh['dp'=16,'mp'=16] {'mp'}, dimensions={0} | all-to-all | bytes 262144 | tf_op jit(solution)/shard_map/all_to_all | solution.py:63
  192.8 12.1 %all_to_all.44 = f32[16,16,128]{2,1,0:T(8,128)S(1)} all-to-all(f32[16,16,128]{2,1,0:T(8,128)S(1)} %tile.8), channel_id=1, replica_groups=mesh['dp'=16,'mp'=16] {'dp'}, dimensions={0} | all-to-all | bytes 262144 | tf_op jit(solution)/shard_map/all_to_all | solution.py:63
  (123 shorter events, 16.4 us)
Async XLA Ops:
  0.0 68.6 %copy-start = (bf16[256,256]{1,0:T(8,128)(2,1)S(1)}, bf16[256,256]{1,0:T(8,128)(2,1)}, u32[]{:S(2)}) copy-start(bf16[256,256]{1,0:T(8,128)(2,1)} %param.13) | copy-start | bytes 393220
  1.0 7.8 %collective-permute-start.2 = (bf16[64,1792]{1,0:T(8,128)(2,1)S(1)}, bf16[64,1792]{1,0:T(8,128)(2,1)S(1)}, u32[]{:S(2)}, u32[]{:S(2)}) collective-permute-start(bf16[64,1792]{1,0:T(8,128)(2,1)S(1)} %pad_maximum_fusion.2.refs_0_), channel_id=1, source_target_pairs={{0,16},{16,0},{32,48},{48,32},{64,80},{80,64},{96,112},{112,96},{1... | collective-permute-start | bytes 688136 | tf_op jit(solution)/shard_map/ppermute | solution.py:95
  3.2 10.6 %collective-permute-start.1 = (bf16[64,1792]{1,0:T(8,128)(2,1)S(1)}, bf16[64,1792]{1,0:T(8,128)(2,1)S(1)}, u32[]{:S(2)}, u32[]{:S(2)}) collective-permute-start(bf16[64,1792]{1,0:T(8,128)(2,1)S(1)} %pad_maximum_fusion.2.refs_0_), channel_id=1, source_target_pairs={{0,32},{16,48},{32,64},{48,80},{64,96},{80,112},{96,128},{112,144}... | collective-permute-start | bytes 688136 | tf_op jit(solution)/shard_map/ppermute | solution.py:91
  4.9 8.9 %collective-permute-start = (bf16[64,1792]{1,0:T(8,128)(2,1)S(1)}, bf16[64,1792]{1,0:T(8,128)(2,1)S(1)}, u32[]{:S(2)}, u32[]{:S(2)}) collective-permute-start(bf16[64,1792]{1,0:T(8,128)(2,1)S(1)} %pad_maximum_fusion.2.refs_0_), channel_id=1, source_target_pairs={{0,224},{16,240},{32,0},{48,16},{64,32},{80,48},{96,64},{112,80},{... | collective-permute-start | bytes 688136 | tf_op jit(solution)/shard_map/ppermute | solution.py:87
  13.8 8.6 %collective-permute-start.5 = (bf16[64,1792]{1,0:T(8,128)(2,1)S(1)}, bf16[64,1792]{1,0:T(8,128)(2,1)S(1)}, u32[]{:S(2)}, u32[]{:S(2)}) collective-permute-start(bf16[64,1792]{1,0:T(8,128)(2,1)S(1)} %get-tuple-element.33.refs_0_), channel_id=1, source_target_pairs={{0,16},{16,0},{32,48},{48,32},{64,80},{80,64},{96,112},{112,96},{1... | collective-permute-start | bytes 688136 | tf_op jit(solution)/shard_map/ppermute | solution.py:95
  14.1 8.4 %collective-permute-start.3 = (bf16[64,1792]{1,0:T(8,128)(2,1)S(1)}, bf16[64,1792]{1,0:T(8,128)(2,1)S(1)}, u32[]{:S(2)}, u32[]{:S(2)}) collective-permute-start(bf16[64,1792]{1,0:T(8,128)(2,1)S(1)} %get-tuple-element.33.refs_0_), channel_id=1, source_target_pairs={{0,224},{16,240},{32,0},{48,16},{64,32},{80,48},{96,64},{112,80},{... | collective-permute-start | bytes 688136 | tf_op jit(solution)/shard_map/ppermute | solution.py:87
  16.4 6.1 %collective-permute-start.4 = (bf16[64,1792]{1,0:T(8,128)(2,1)S(1)}, bf16[64,1792]{1,0:T(8,128)(2,1)S(1)}, u32[]{:S(2)}, u32[]{:S(2)}) collective-permute-start(bf16[64,1792]{1,0:T(8,128)(2,1)S(1)} %get-tuple-element.34.refs_1_), channel_id=1, source_target_pairs={{0,32},{16,48},{32,64},{48,80},{64,96},{80,112},{96,128},{112,144}... | collective-permute-start | bytes 688136 | tf_op jit(solution)/shard_map/ppermute | solution.py:91
  19.3 47.1 %collective-permute-start.17 = (f32[896,256]{1,0:T(8,128)}, f32[896,256]{1,0:T(8,128)}, u32[]{:S(2)}, u32[]{:S(2)}) collective-permute-start(f32[896,256]{1,0:T(8,128)} %get-tuple-element.61), channel_id=1, source_target_pairs={{0,1},{1,0},{2,3},{3,2},{4,5},{5,4},{6,7},{7,6},{8,9},{9,8},{10,11... | collective-permute-start | bytes 2752520 | tf_op jit(solution)/shard_map/ppermute | solution.py:280
  22.5 11.3 %collective-permute-start.8 = (bf16[64,1792]{1,0:T(8,128)(2,1)S(1)}, bf16[64,1792]{1,0:T(8,128)(2,1)S(1)}, u32[]{:S(2)}, u32[]{:S(2)}) collective-permute-start(bf16[64,1792]{1,0:T(8,128)(2,1)S(1)} %get-tuple-element.36.refs_3_), channel_id=1, source_target_pairs={{0,16},{16,0},{32,48},{48,32},{64,80},{80,64},{96,112},{112,96},{1... | collective-permute-start | bytes 688136 | tf_op jit(solution)/shard_map/ppermute | solution.py:95
  23.8 9.9 %collective-permute-start.6 = (bf16[64,1792]{1,0:T(8,128)(2,1)S(1)}, bf16[64,1792]{1,0:T(8,128)(2,1)S(1)}, u32[]{:S(2)}, u32[]{:S(2)}) collective-permute-start(bf16[64,1792]{1,0:T(8,128)(2,1)S(1)} %get-tuple-element.37.refs_0_), channel_id=1, source_target_pairs={{0,224},{16,240},{32,0},{48,16},{64,32},{80,48},{96,64},{112,80},{... | collective-permute-start | bytes 688136 | tf_op jit(solution)/shard_map/ppermute | solution.py:87
  26.0 7.7 %collective-permute-start.7 = (bf16[64,1792]{1,0:T(8,128)(2,1)S(1)}, bf16[64,1792]{1,0:T(8,128)(2,1)S(1)}, u32[]{:S(2)}, u32[]{:S(2)}) collective-permute-start(bf16[64,1792]{1,0:T(8,128)(2,1)S(1)} %get-tuple-element.38.refs_1_), channel_id=1, source_target_pairs={{0,32},{16,48},{32,64},{48,80},{64,96},{80,112},{96,128},{112,144}... | collective-permute-start | bytes 688136 | tf_op jit(solution)/shard_map/ppermute | solution.py:91
  26.0 7.7 %collective-permute-start.9 = (bf16[64,256]{1,0:T(8,128)(2,1)S(1)}, bf16[64,256]{1,0:T(8,128)(2,1)S(1)}, u32[]{:S(2)}, u32[]{:S(2)}) collective-permute-start(bf16[64,256]{1,0:T(8,128)(2,1)S(1)} %pad_maximum_fusion.5), channel_id=1, source_target_pairs={{0,0},{1,16},{2,32},{3,48},{4,64},{5,80},{6,96},{7,112},{8,128},{9... | collective-permute-start | bytes 98312 | tf_op jit(solution)/shard_map/ppermute | solution.py:286
  33.8 19.3 %collective-permute-start.10 = (bf16[64,1792]{1,0:T(8,128)(2,1)S(1)}, bf16[64,1792]{1,0:T(8,128)(2,1)S(1)}, u32[]{:S(2)}, u32[]{:S(2)}) collective-permute-start(bf16[64,1792]{1,0:T(8,128)(2,1)S(1)} %get-tuple-element.40.refs_4_), channel_id=1, source_target_pairs={{0,224},{16,240},{32,0},{48,16},{64,32},{80,48},{96,64},{112,80},{... | collective-permute-start | bytes 688136 | tf_op jit(solution)/shard_map/ppermute | solution.py:87
  39.9 13.2 %collective-permute-start.11 = (bf16[64,1792]{1,0:T(8,128)(2,1)S(1)}, bf16[64,1792]{1,0:T(8,128)(2,1)S(1)}, u32[]{:S(2)}, u32[]{:S(2)}) collective-permute-start(bf16[64,1792]{1,0:T(8,128)(2,1)S(1)} %get-tuple-element.41.refs_5_), channel_id=1, source_target_pairs={{0,32},{16,48},{32,64},{48,80},{64,96},{80,112},{96,128},{112,144}... | collective-permute-start | bytes 688136 | tf_op jit(solution)/shard_map/ppermute | solution.py:91
  39.9 13.3 %collective-permute-start.13 = (bf16[64,1792]{1,0:T(8,128)(2,1)S(1)}, bf16[64,1792]{1,0:T(8,128)(2,1)S(1)}, u32[]{:S(2)}, u32[]{:S(2)}) collective-permute-start(bf16[64,1792]{1,0:T(8,128)(2,1)S(1)} %get-tuple-element.44.refs_0_), channel_id=1, source_target_pairs={{0,16},{16,0},{32,48},{48,32},{64,80},{80,64},{96,112},{112,96},{1... | collective-permute-start | bytes 688136 | tf_op jit(solution)/shard_map/ppermute | solution.py:95
  39.9 13.3 %collective-permute-start.12 = (bf16[64,1792]{1,0:T(8,128)(2,1)S(1)}, bf16[64,1792]{1,0:T(8,128)(2,1)S(1)}, u32[]{:S(2)}, u32[]{:S(2)}) collective-permute-start(bf16[64,1792]{1,0:T(8,128)(2,1)S(1)} %get-tuple-element.45.refs_1_), channel_id=1, source_target_pairs={{0,32},{16,48},{32,64},{48,80},{64,96},{80,112},{96,128},{112,144}... | collective-permute-start | bytes 688136 | tf_op jit(solution)/shard_map/ppermute | solution.py:91
  40.9 27.8 %all-to-all-start = ((bf16[16,64,256]{2,1,0:T(8,128)(2,1)}), bf16[16,64,256]{2,1,0:T(8,128)(2,1)S(1)}, u32[]{:S(2)}, u32[]{:S(2)}) async-start(bf16[16,64,256]{2,1,0:T(8,128)(2,1)} %tile.6), calls=%async_computation | async-start | bytes 1048576 | tf_op jit(solution)/shard_map/all_to_all | solution.py:63
  53.3 16.4 %collective-permute-start.15 = (bf16[64,1792]{1,0:T(8,128)(2,1)S(1)}, bf16[64,1792]{1,0:T(8,128)(2,1)}, u32[]{:S(2)}, u32[]{:S(2)}) collective-permute-start(bf16[64,1792]{1,0:T(8,128)(2,1)S(1)} %get-tuple-element.52.refs_3_), channel_id=1, source_target_pairs={{0,16},{16,0},{32,48},{48,32},{64,80},{80,64},{96,112},{112,96},{1... | collective-permute-start | bytes 688136 | tf_op jit(solution)/shard_map/ppermute | solution.py:95
  54.5 15.2 %collective-permute-start.16 = (bf16[64,1792]{1,0:T(8,128)(2,1)S(1)}, bf16[64,1792]{1,0:T(8,128)(2,1)}, u32[]{:S(2)}, u32[]{:S(2)}) collective-permute-start(bf16[64,1792]{1,0:T(8,128)(2,1)S(1)} %get-tuple-element.46.refs_9_.refs_4_), channel_id=1, source_target_pairs={{0,224},{16,240},{32,0},{48,16},{64,32},{80,48},{96,64},{112,80},{... | collective-permute-start | bytes 688136 | tf_op jit(solution)/shard_map/ppermute | solution.py:87
  65.7 21.1 %collective-permute-start.14 = (bf16[512,896]{1,0:T(8,128)(2,1)}, bf16[512,896]{1,0:T(8,128)(2,1)}, u32[]{:S(2)}, u32[]{:S(2)}) collective-permute-start(bf16[512,896]{1,0:T(8,128)(2,1)} %get-tuple-element.48), channel_id=1, source_target_pairs={{0,1},{1,0},{2,3},{3,2},{4,5},{5,4},{6,7},{7,6},{8,9},{9,8},{10,11... | collective-permute-start | bytes 2752520 | tf_op jit(solution)/shard_map/ppermute | solution.py:322
  78.0 10.8 %collective-permute-start.18 = (bf16[512,896]{1,0:T(8,128)(2,1)}, bf16[512,896]{1,0:T(8,128)(2,1)S(1)}, u32[]{:S(2)}, u32[]{:S(2)}) collective-permute-start(bf16[512,896]{1,0:T(8,128)(2,1)} %get-tuple-element.56), channel_id=1, source_target_pairs={{0,1},{1,0},{2,3},{3,2},{4,5},{5,4},{6,7},{7,6},{8,9},{9,8},{10,11... | collective-permute-start | bytes 2752520 | tf_op jit(solution)/shard_map/ppermute | solution.py:322
  78.0 7.5 %collective-permute-start.19 = (bf16[512,256]{1,0:T(8,128)(2,1)S(1)}, bf16[512,256]{1,0:T(8,128)(2,1)S(1)}, u32[]{:S(2)}, u32[]{:S(2)}) collective-permute-start(bf16[512,256]{1,0:T(8,128)(2,1)S(1)} %copy-done.18), channel_id=1, source_target_pairs={{0,16},{16,0},{32,48},{48,32},{64,80},{80,64},{96,112},{112,96},{1... | collective-permute-start | bytes 786440 | tf_op jit(solution)/shard_map/ppermute | solution.py:315
  90.7 33.5 %all-to-all-start.1 = ((bf16[8,128,896]{2,1,0:T(8,128)(2,1)}), bf16[8,128,896]{2,1,0:T(8,128)(2,1)S(1)}, u32[]{:S(2)}, u32[]{:S(2)}) async-start(bf16[8,128,896]{2,1,0:T(8,128)(2,1)} %bitcast.17), calls=%async_computation.1 | async-start | bytes 3670016 | tf_op jit(solution)/shard_map/all_to_all | solution.py:63
  98.2 6.4 %collective-permute-start.20 = (f32[256,256]{1,0:T(8,128)S(1)}, f32[256,256]{1,0:T(8,128)S(1)}, u32[]{:S(2)}, u32[]{:S(2)}) collective-permute-start(f32[256,256]{1,0:T(8,128)S(1)} %constant_dynamic-slice_fusion.2), channel_id=1, source_target_pairs={{0,32},{16,48},{32,0},{48,16},{64,96},{80,112},{96,64},{112,80},{1... | collective-permute-start | bytes 786440 | tf_op jit(solution)/shard_map/ppermute | solution.py:315
  104.6 7.9 %collective-permute-start.21 = (f32[128,256]{1,0:T(8,128)S(1)}, f32[128,256]{1,0:T(8,128)S(1)}, u32[]{:S(2)}, u32[]{:S(2)}) collective-permute-start(f32[128,256]{1,0:T(8,128)S(1)} %constant_dynamic-slice_fusion.1), channel_id=1, source_target_pairs={{0,64},{16,80},{32,96},{48,112},{64,0},{80,16},{96,32},{112,48},{1... | collective-permute-start | bytes 393224 | tf_op jit(solution)/shard_map/ppermute | solution.py:315
  112.5 16.9 %collective-permute-start.22 = (f32[64,256]{1,0:T(8,128)S(1)}, f32[64,256]{1,0:T(8,128)S(1)}, u32[]{:S(2)}, u32[]{:S(2)}) collective-permute-start(f32[64,256]{1,0:T(8,128)S(1)} %constant_dynamic-slice_fusion), channel_id=1, source_target_pairs={{0,128},{16,144},{32,160},{48,176},{64,192},{80,208},{96,224},{112... | collective-permute-start | bytes 196616 | tf_op jit(solution)/shard_map/ppermute | solution.py:315
  125.8 33.1 %all-to-all-start.2 = ((bf16[8,128,896]{2,1,0:T(8,128)(2,1)}), bf16[8,128,896]{2,1,0:T(8,128)(2,1)S(1)}, u32[]{:S(2)}, u32[]{:S(2)}) async-start(bf16[8,128,896]{2,1,0:T(8,128)(2,1)} %bitcast.16), calls=%async_computation.2 | async-start | bytes 3670016 | tf_op jit(solution)/shard_map/all_to_all | solution.py:63
  129.4 6.8 %collective-permute-start.23 = (bf16[64,256]{1,0:T(8,128)(2,1)S(1)}, bf16[64,256]{1,0:T(8,128)(2,1)S(1)}, u32[]{:S(2)}, u32[]{:S(2)}) collective-permute-start(bf16[64,256]{1,0:T(8,128)(2,1)S(1)} %get-tuple-element.58), channel_id=1, source_target_pairs={{0,128},{16,144},{32,160},{48,176},{64,192},{80,208},{96,224},{112... | collective-permute-start | bytes 98312 | tf_op jit(solution)/shard_map/ppermute | solution.py:332
  136.2 4.3 %collective-permute-start.24 = (bf16[128,256]{1,0:T(8,128)(2,1)S(1)}, bf16[128,256]{1,0:T(8,128)(2,1)S(1)}, u32[]{:S(2)}, u32[]{:S(2)}) collective-permute-start(bf16[128,256]{1,0:T(8,128)(2,1)S(1)} %pad_maximum_fusion.4), channel_id=1, source_target_pairs={{0,64},{16,80},{32,96},{48,112},{64,0},{80,16},{96,32},{112,48},{1... | collective-permute-start | bytes 196616 | tf_op jit(solution)/shard_map/ppermute | solution.py:332
  140.5 4.9 %collective-permute-start.25 = (bf16[256,256]{1,0:T(8,128)(2,1)S(1)}, bf16[256,256]{1,0:T(8,128)(2,1)S(1)}, u32[]{:S(2)}, u32[]{:S(2)}) collective-permute-start(bf16[256,256]{1,0:T(8,128)(2,1)S(1)} %pad_maximum_fusion.3), channel_id=1, source_target_pairs={{0,32},{16,48},{32,0},{48,16},{64,96},{80,112},{96,64},{112,80},{1... | collective-permute-start | bytes 393224 | tf_op jit(solution)/shard_map/ppermute | solution.py:332
  145.5 9.1 %collective-permute-start.26 = (bf16[512,256]{1,0:T(8,128)(2,1)S(1)}, bf16[512,256]{1,0:T(8,128)(2,1)S(1)}, u32[]{:S(2)}, u32[]{:S(2)}) collective-permute-start(bf16[512,256]{1,0:T(8,128)(2,1)S(1)} %pad_maximum_fusion.1), channel_id=1, source_target_pairs={{0,16},{16,0},{32,48},{48,32},{64,80},{80,64},{96,112},{112,96},{1... | collective-permute-start | bytes 786440 | tf_op jit(solution)/shard_map/ppermute | solution.py:332
  154.6 4.3 %collective-permute-start.27 = (bf16[1024,256]{1,0:T(8,128)(2,1)S(1)}, bf16[1024,256]{1,0:T(8,128)(2,1)S(1)}, u32[]{:S(2)}, u32[]{:S(2)}) collective-permute-start(bf16[1024,256]{1,0:T(8,128)(2,1)S(1)} %constant_dynamic-update-slice_fusion.own_acts_ref), channel_id=1, source_target_pairs={{0,1},{1,0},{2,3},{3,2},{4,5},{5,4},{6,7},{7,6},{8,9},{9,8},{10,11... | collective-permute-start | bytes 1572872 | tf_op jit(solution)/shard_map/ppermute | solution.py:333
  (24 other events, 326.6 us)

commit v4 on v3

--- a/solution.py
+++ b/solution.py
@@ -147,10 +147,6 @@
     )(core.reshape(1), *blocks, basis, *needs)
 
 
-def after(x, y):
-    return x + jnp.minimum(jnp.abs(y[:1, :1]), 0).astype(x.dtype)
-
-
 def sum_kernel(parts_ref, *refs):
     out_ref = refs[-1]
     rows = parts_ref.shape[0] // CHIPS
@@ -287,51 +283,56 @@
     held[(0, 0)], held[(1, 0)], held[(-1, 0)], held[(0, 1)] = fence(
         grads, up(grads), down(grads), over(grads)
     )
-    held[(1, 0)], held[(-1, 0)], held[(2, 0)], held[(-2, 0)], held[(1, 1)] = fence(
+    (held[(1, 0)], held[(-1, 0)], held[(2, 0)], held[(-2, 0)], held[(1, 1)], moved, own_inv,
+     sib_inv) = fence(
         held[(1, 0)], held[(-1, 0)], up(held[(1, 0)]), down(held[(-1, 0)]),
-        over(held[(1, 0)]),
+        over(held[(1, 0)]), moved, own_inv, sib_inv,
     )
     (held[(2, 0)], held[(-2, 0)], held[(3, 0)], held[(-3, 0)], held[(1, 1)], held[(-1, 1)],
-     moved) = fence(
+     every_acts) = fence(
         held[(2, 0)], held[(-2, 0)], up(held[(2, 0)]), down(held[(-2, 0)]), held[(1, 1)],
-        over(held[(-1, 0)]), moved,
-    )
-    every_acts = share(moved, GROUPS, "mp")
-    held[(3, 0)], held[(-3, 0)], held[(2, 1)], held[(-2, 1)], held[(4, 0)], held[(3, 1)] = fence(
+        over(held[(-1, 0)]), share(moved, GROUPS, "mp"),
+    )
+
+    bits = (yl, z % 2, z // 2 % 2, z // 4)
+
+    def halves(x, bit):
+        half = x.shape[0] // 2
+        return (
+            lax.dynamic_slice_in_dim(x, bit * half, half, 0),
+            lax.dynamic_slice_in_dim(x, (1 - bit) * half, half, 0),
+        )
+
+    mine, away = halves(
+        jnp.dot(every_acts, basis_in, preferred_element_type=jnp.float32), bits[0]
+    )
+    (held[(3, 0)], held[(-3, 0)], held[(2, 1)], held[(-2, 1)], held[(4, 0)], held[(3, 1)],
+     away) = fence(
         held[(3, 0)], held[(-3, 0)], up(held[(1, 1)]), down(held[(-1, 1)]), down(held[(-3, 0)]),
-        over(held[(3, 0)]),
+        over(held[(3, 0)]), away.astype(jnp.bfloat16),
     )
     held[(4, 1)], held[(-3, 1)] = up(held[(3, 1)]), over(held[(-3, 0)])
-
-    summed = jnp.dot(every_acts, basis_in, preferred_element_type=jnp.float32)
-    bits = (yl, z % 2, z // 2 % 2, z // 4)
-    sums = []
-    for k, (swap, bit) in enumerate(zip(DP_SWAPS, bits)):
-        half = summed.shape[0] // 2
-        away = lax.dynamic_slice_in_dim(summed, (1 - bit) * half, half, 0)
-        mine = lax.dynamic_slice_in_dim(summed, bit * half, half, 0)
-        if k == 0:
-            first = away = away.astype(jnp.bfloat16)
-        summed = mine + lax.ppermute(away, "dp", swap).astype(jnp.float32)
-        sums.append(summed)
+    first = mine + lax.ppermute(away, "dp", DP_SWAPS[0]).astype(jnp.float32)
+    summed = first
+    for swap, bit in zip(DP_SWAPS[1:], bits[1:]):
+        mine, away = halves(summed, bit)
+        summed = mine + lax.ppermute(away, "dp", swap)
     own_acts = summed.astype(jnp.bfloat16)
 
     pairs = []
-    for chunk, needs in zip(CHUNKS, ((held[(3, 1)],), (own_inv, sib_inv, first))):
+    for chunk, needs in zip(CHUNKS, ((held[(3, 1)],), (first,))):
         sib_part, own_part = turn(core, [held[place] for place in chunk], basis_out, needs)
-        got = lax.ppermute(sib_part, "mp", CORE_SWAP).astype(jnp.float32)
-        if pairs:
-            got = after(got, sums[0])
-        pairs.append((own_part + got).astype(jnp.bfloat16))
-    pairs = jnp.concatenate(pairs, 0)
-    parts = exchange(pairs, "mp", axis_index_groups=SAME_CORE)
-    copies = sum_and_copy(parts)
-
-    own_acts = after(own_acts, copies)
+        got = lax.ppermute(sib_part, "mp", CORE_SWAP)
+        pairs.append((own_part + got.astype(jnp.float32)).astype(jnp.bfloat16))
+    parts = exchange(jnp.concatenate(pairs, 0), "mp", axis_index_groups=SAME_CORE)
+
+    doubled = []
     for swap in DP_SWAPS[::-1]:
         own_acts = jnp.concatenate([own_acts, lax.ppermute(own_acts, "dp", swap)], 0)
+        doubled.append(own_acts)
     sib_acts = lax.ppermute(own_acts, "mp", CORE_SWAP)
 
+    copies = sum_and_copy(parts, doubled[0])
     all_grads = exchange(copies, "mp", axis_index_groups=SAME_CORE)
 
     places = [place for chunk in CHUNKS for place in chunk]

time: 206 us -> 215 us (1.044)
  waiting for transfers between devices: 63.7 us -> 82.7 us
  starting transfers between devices: 61.9 us -> 55.3 us
  other arithmetic: 12.4 us -> 8.21 us
    ppermute x5, waiting for transfers between devices: 0.01 us -> 14.2 us  [up(): return lax.ppermute(x, 'dp', dp_shift(-1, 0))]
    all_to_all x3, waiting for transfers between devices: 11.4 us -> 0.01 us  [exchange(): return lax.all_to_all(x, axis, 0, 0, tiled=True, **kw)]
    ppermute x5, starting transfers between devices: 17.5 us -> 6.41 us  [up(): return lax.ppermute(x, 'dp', dp_shift(-1, 0))]
    ppermute x5, waiting for transfers between devices: 5.78 us -> 12.7 us  [down(): return lax.ppermute(x, 'dp', dp_shift(1, 0))]
    ppermute x6, starting transfers between devices: 1.72 us -> 8.37 us  [the longest x3 4 us: shards(): summed = mine + lax.ppermute(away, 'dp', swap)]
    ppermute x4, waiting for transfers between devices: 23 us -> 29.4 us  [shards(): lax.ppermute(own_acts, 'dp', swap)]
    ppermute x5, waiting for transfers between devices: 0.01 us -> 4.1 us  [over(): return lax.ppermute(x, 'dp', dp_shift(0, 1))]
    unnamed x53 -> x65, local copies, waits for them, and re-layouts: 1.81 us -> 5.24 us
  transfers between devices with their start and end apart: 31 -> 31, of which waited for: 12 -> 19; matrix products, arithmetic and copies ran while one was open for 6% -> 1% of each run, Pallas kernels for 8% -> 8%
where the time goes in v4:
time: 215 us; the launch traced here: 214 us
  waiting for transfers between devices  82.7 us (38%)
  starting transfers between devices  55.3 us (26%)
  Pallas kernels  34.2 us (16%)
  blocking collectives  27 us (13%)
  other arithmetic  8.21 us (4%)
  local copies, waits for them, and re-layouts  6.31 us (3%)
    ppermute x4, waiting for transfers between devices, shards(): lax.ppermute(own_acts, 'dp', swap)  29.4 us
    all_to_all x2, blocking collectives, exchange(): return lax.all_to_all(x, axis, 0, 0, tiled=True, **kw)  27 us
    all_to_all x3, starting transfers between devices, exchange(): return lax.all_to_all(x, axis, 0, 0, tiled=True, **kw)  22.7 us
    ppermute x3, waiting for transfers between devices, shards(): summed = mine + lax.ppermute(away, 'dp', swap)  19.7 us
    pallas_call x1, Pallas kernels, score_blocks(): pl.pallas_call(score_kernel, out_shape=jax.ShapeDtypeStruct((GROUPS, 128)...  17.5 us
    pallas_call x2, Pallas kernels, turn(): pl.pallas_call(functools.partial(turn_kernel, len(blocks)), grid_spec=plt...  16.4 us
    ppermute x5, waiting for transfers between devices, up(): return lax.ppermute(x, 'dp', dp_shift(-1, 0))  14.2 us
    ppermute x5, waiting for transfers between devices, down(): return lax.ppermute(x, 'dp', dp_shift(1, 0))  12.7 us
  transfers between devices with their start and end apart: 31, of which 19 were waited for; matrix products, arithmetic and copies ran while one was open for 1% of the time, Pallas kernels for 8%

profile of v4, /device:TPU:1, one launch (start us, length us, event | category | flops | bytes accessed | tf_op | source)
XLA Modules:
  0.0 214.4 jit_solution(16292876366140822788)
XLA Ops:
  0.0 1.7 constant_dynamic-slice_fusion.3
  1.7 3.3 %collective-permute-start.7 = (f32[896,256]{1,0:T(8,128)S(1)}, f32[896,256]{1,0:T(8,128)S(1)}, u32[]{:S(2)}, u32[]{:S(2)}) collective-permute-start(f32[896,256]{1,0:T(8,128)S(1)} %get-tuple-element.69), channel_id=1, source_target_pairs={{0,1},{1,0},{2,3},{3,2},{4,5},{5,4},{6,7},{7,6},{8,9},{9,8},{10,11... | collective-permute-start | bytes 2752520 | tf_op jit(solution)/shard_map/ppermute | solution.py:276
  5.0 3.9 %collective-permute-start = (bf16[64,1792]{1,0:T(8,128)(2,1)S(1)}, bf16[64,1792]{1,0:T(8,128)(2,1)S(1)}, u32[]{:S(2)}, u32[]{:S(2)}) collective-permute-start(bf16[64,1792]{1,0:T(8,128)(2,1)S(1)} %pad_maximum_fusion.2.refs_0_), channel_id=1, source_target_pairs={{0,224},{16,240},{32,0},{48,16},{64,32},{80,48},{96,64},{112,80},{... | collective-permute-start | bytes 688136 | tf_op jit(solution)/shard_map/ppermute | solution.py:87
  10.3 2.6 %collective-permute-start.6 = (bf16[64,256]{1,0:T(8,128)(2,1)S(1)}, bf16[64,256]{1,0:T(8,128)(2,1)S(1)}, u32[]{:S(2)}, u32[]{:S(2)}) collective-permute-start(bf16[64,256]{1,0:T(8,128)(2,1)S(1)} %pad_maximum_fusion.5), channel_id=1, source_target_pairs={{0,0},{1,16},{2,32},{3,48},{4,64},{5,80},{6,96},{7,112},{8,128},{9... | collective-permute-start | bytes 98312 | tf_op jit(solution)/shard_map/ppermute | solution.py:282
  14.0 3.1 %collective-permute-done.1.refs_2_ = bf16[64,1792]{1,0:T(8,128)(2,1)S(1)} collective-permute-done((bf16[64,1792]{1,0:T(8,128)(2,1)S(1)}, bf16[64,1792]{1,0:T(8,128)(2,1)S(1)}, u32[]{:S(2)}, u32[]{:S(2)}) %collective-permute-start.1) | collective-permute-done | bytes 229408 | tf_op jit(solution)/shard_map/ppermute | solution.py:91
  17.8 2.1 collective-permute-start.3
  20.7 3.8 %collective-permute-done.3.refs_2_ = bf16[64,1792]{1,0:T(8,128)(2,1)S(1)} collective-permute-done((bf16[64,1792]{1,0:T(8,128)(2,1)S(1)}, bf16[64,1792]{1,0:T(8,128)(2,1)S(1)}, u32[]{:S(2)}, u32[]{:S(2)}) %collective-permute-start.3) | collective-permute-done | bytes 229408 | tf_op jit(solution)/shard_map/ppermute | solution.py:87
  24.4 1.9 collective-permute-done.4.refs_3_
  28.3 10.2 %all-to-all-start = ((bf16[16,64,256]{2,1,0:T(8,128)(2,1)}), bf16[16,64,256]{2,1,0:T(8,128)(2,1)S(1)}, u32[]{:S(2)}, u32[]{:S(2)}) async-start(bf16[16,64,256]{2,1,0:T(8,128)(2,1)} %tile.6), calls=%async_computation | async-start | bytes 1048576 | tf_op jit(solution)/shard_map/all_to_all | solution.py:63
  39.9 5.7 %collective-permute-done.8.refs_2_ = bf16[64,1792]{1,0:T(8,128)(2,1)S(1)} collective-permute-done((bf16[64,1792]{1,0:T(8,128)(2,1)S(1)}, bf16[64,1792]{1,0:T(8,128)(2,1)S(1)}, u32[]{:S(2)}, u32[]{:S(2)}) %collective-permute-start.8) | collective-permute-done | bytes 229408 | tf_op jit(solution)/shard_map/ppermute | solution.py:87
  46.8 4.1 %collective-permute-done.10.refs_5_ = bf16[64,1792]{1,0:T(8,128)(2,1)} collective-permute-done((bf16[64,1792]{1,0:T(8,128)(2,1)S(1)}, bf16[64,1792]{1,0:T(8,128)(2,1)}, u32[]{:S(2)}, u32[]{:S(2)}) %collective-permute-start.10) | collective-permute-done | bytes 229408 | tf_op jit(solution)/shard_map/ppermute | solution.py:95
  53.7 3.6 %collective-permute-done.11.refs_2_ = bf16[64,1792]{1,0:T(8,128)(2,1)S(1)} collective-permute-done((bf16[64,1792]{1,0:T(8,128)(2,1)S(1)}, bf16[64,1792]{1,0:T(8,128)(2,1)S(1)}, u32[]{:S(2)}, u32[]{:S(2)}) %collective-permute-start.11) | collective-permute-done | bytes 229408 | tf_op jit(solution)/shard_map/ppermute | solution.py:87
  58.9 4.9 %collective-permute-done.13.refs_4_ = bf16[64,1792]{1,0:T(8,128)(2,1)S(1)} collective-permute-done((bf16[64,1792]{1,0:T(8,128)(2,1)S(1)}, bf16[64,1792]{1,0:T(8,128)(2,1)S(1)}, u32[]{:S(2)}, u32[]{:S(2)}) %collective-permute-start.13) | collective-permute-done | bytes 229408 | tf_op jit(solution)/shard_map/ppermute | solution.py:91
  65.4 8.1 %shard_map.95 = (bf16[512,896]{1,0:T(8,128)(2,1)}, f32[512,896]{1,0:T(8,128)}) custom-call(s32[1]{0:T(128)} %bitcast.core_ref, bf16[64,1792]{1,0:T(8,128)(2,1)} %copy-done.6, bf16[64,1792]{1,0:T(8,128)(2,1)} %copy-done.16, bf16[64,1792]{1,0:T(8,128)(2,1)} %copy-done.4, bf16[64,1792]{1,0:T(8,128)(2,1)} %copy-done.5, bf16[64,1792]{1,0:T(8,128)(2,1)} %copy-done.8, ...), custom_call_target="tpu_custom_call" | custom-call | flops 3288334336 | bytes 11010048 | tf_op jit(solution)/shard_map/pallas_call | solution.py:126
  73.6 2.5 %collective-permute-start.15 = (bf16[512,896]{1,0:T(8,128)(2,1)}, bf16[512,896]{1,0:T(8,128)(2,1)S(1)}, u32[]{:S(2)}, u32[]{:S(2)}) collective-permute-start(bf16[512,896]{1,0:T(8,128)(2,1)} %get-tuple-element.54), channel_id=1, source_target_pairs={{0,1},{1,0},{2,3},{3,2},{4,5},{5,4},{6,7},{7,6},{8,9},{9,8},{10,11... | collective-permute-start | bytes 2752520 | tf_op jit(solution)/shard_map/ppermute | solution.py:325
  77.7 8.2 %shard_map.96 = (bf16[512,896]{1,0:T(8,128)(2,1)}, f32[512,896]{1,0:T(8,128)}) custom-call(s32[1]{0:T(128)} %bitcast.core_ref, bf16[64,1792]{1,0:T(8,128)(2,1)} %copy-done.12, bf16[64,1792]{1,0:T(8,128)(2,1)} %copy-done.13, bf16[64,1792]{1,0:T(8,128)(2,1)} %copy-done.10, bf16[64,1792]{1,0:T(8,128)(2,1)} %copy-done.11, bf16[64,1792]{1,0:T(8,128)(2,1)} %copy-done.15, ...), custom_call_target="tpu_custom_call" | custom-call | flops 3288334336 | bytes 11010048 | tf_op jit(solution)/shard_map/pallas_call | solution.py:126
  87.6 2.3 %collective-permute-done.19 = bf16[512,896]{1,0:T(8,128)(2,1)} collective-permute-done((bf16[512,896]{1,0:T(8,128)(2,1)}, bf16[512,896]{1,0:T(8,128)(2,1)}, u32[]{:S(2)}, u32[]{:S(2)}) %collective-permute-start.19) | collective-permute-done | bytes 917536 | tf_op jit(solution)/shard_map/ppermute | solution.py:325
  92.7 6.4 %all-to-all-start.1 = ((bf16[8,128,896]{2,1,0:T(8,128)(2,1)}), bf16[8,128,896]{2,1,0:T(8,128)(2,1)S(1)}, u32[]{:S(2)}, u32[]{:S(2)}) async-start(bf16[8,128,896]{2,1,0:T(8,128)(2,1)} %bitcast.16), calls=%async_computation.1 | async-start | bytes 3670016 | tf_op jit(solution)/shard_map/all_to_all | solution.py:63
  99.5 6.9 %collective-permute-done.20 = f32[256,256]{1,0:T(8,128)S(1)} collective-permute-done((f32[256,256]{1,0:T(8,128)S(1)}, f32[256,256]{1,0:T(8,128)S(1)}, u32[]{:S(2)}, u32[]{:S(2)}) %collective-permute-start.20) | collective-permute-done | bytes 262176 | tf_op jit(solution)/shard_map/ppermute | solution.py:319
  107.0 8.2 %collective-permute-done.21 = f32[128,256]{1,0:T(8,128)S(1)} collective-permute-done((f32[128,256]{1,0:T(8,128)S(1)}, f32[128,256]{1,0:T(8,128)S(1)}, u32[]{:S(2)}, u32[]{:S(2)}) %collective-permute-start.21) | collective-permute-done | bytes 131104 | tf_op jit(solution)/shard_map/ppermute | solution.py:319
  115.2 3.1 %collective-permute-start.22 = (f32[64,256]{1,0:T(8,128)S(1)}, f32[64,256]{1,0:T(8,128)S(1)}, u32[]{:S(2)}, u32[]{:S(2)}) collective-permute-start(f32[64,256]{1,0:T(8,128)S(1)} %constant_dynamic-slice_fusion), channel_id=1, source_target_pairs={{0,128},{16,144},{32,160},{48,176},{64,192},{80,208},{96,224},{112... | collective-permute-start | bytes 196616 | tf_op jit(solution)/shard_map/ppermute | solution.py:319
  118.3 4.6 %collective-permute-done.22 = f32[64,256]{1,0:T(8,128)S(1)} collective-permute-done((f32[64,256]{1,0:T(8,128)S(1)}, f32[64,256]{1,0:T(8,128)S(1)}, u32[]{:S(2)}, u32[]{:S(2)}) %collective-permute-start.22) | collective-permute-done | bytes 65568 | tf_op jit(solution)/shard_map/ppermute | solution.py:319
  122.9 2.5 %collective-permute-start.23 = (bf16[64,256]{1,0:T(8,128)(2,1)S(1)}, bf16[64,256]{1,0:T(8,128)(2,1)S(1)}, u32[]{:S(2)}, u32[]{:S(2)}) collective-permute-start(bf16[64,256]{1,0:T(8,128)(2,1)S(1)} %get-tuple-element.66), channel_id=1, source_target_pairs={{0,128},{16,144},{32,160},{48,176},{64,192},{80,208},{96,224},{112... | collective-permute-start | bytes 98312 | tf_op jit(solution)/shard_map/ppermute | solution.py:331
  125.4 4.3 %collective-permute-done.23 = bf16[64,256]{1,0:T(8,128)(2,1)S(1)} collective-permute-done((bf16[64,256]{1,0:T(8,128)(2,1)S(1)}, bf16[64,256]{1,0:T(8,128)(2,1)S(1)}, u32[]{:S(2)}, u32[]{:S(2)}) %collective-permute-start.23) | collective-permute-done | bytes 32800 | tf_op jit(solution)/shard_map/ppermute | solution.py:331
  131.2 6.1 %all-to-all-start.2 = ((bf16[8,128,896]{2,1,0:T(8,128)(2,1)}), bf16[8,128,896]{2,1,0:T(8,128)(2,1)S(1)}, u32[]{:S(2)}, u32[]{:S(2)}) async-start(bf16[8,128,896]{2,1,0:T(8,128)(2,1)} %bitcast.14), calls=%async_computation.2 | async-start | bytes 3670016 | tf_op jit(solution)/shard_map/all_to_all | solution.py:63
  137.3 4.0 %collective-permute-done.24 = bf16[128,256]{1,0:T(8,128)(2,1)S(1)} collective-permute-done((bf16[128,256]{1,0:T(8,128)(2,1)S(1)}, bf16[128,256]{1,0:T(8,128)(2,1)S(1)}, u32[]{:S(2)}, u32[]{:S(2)}) %collective-permute-start.24) | collective-permute-done | bytes 65568 | tf_op jit(solution)/shard_map/ppermute | solution.py:331
  141.5 4.8 %collective-permute-done.25 = bf16[256,256]{1,0:T(8,128)(2,1)S(1)} collective-permute-done((bf16[256,256]{1,0:T(8,128)(2,1)S(1)}, bf16[256,256]{1,0:T(8,128)(2,1)S(1)}, u32[]{:S(2)}, u32[]{:S(2)}) %collective-permute-start.25) | collective-permute-done | bytes 131104 | tf_op jit(solution)/shard_map/ppermute | solution.py:331
  147.1 16.3 %collective-permute-done.26 = bf16[512,256]{1,0:T(8,128)(2,1)S(1)} collective-permute-done((bf16[512,256]{1,0:T(8,128)(2,1)S(1)}, bf16[512,256]{1,0:T(8,128)(2,1)S(1)}, u32[]{:S(2)}, u32[]{:S(2)}) %collective-permute-start.26) | collective-permute-done | bytes 262176 | tf_op jit(solution)/shard_map/ppermute | solution.py:331
  163.4 2.0 collective-permute-start.27
  168.4 17.5 %shard_map.98 = f32[16,128]{1,0:T(8,128)} custom-call(s32[16]{0:T(128)} %get-tuple-element.67.acts_at_ref, f32[16,16]{1,0:T(8,128)} %fusion.place_ref, bf16[1024,896]{1,0:T(8,128)(2,1)} %bitcast.17, bf16[1024,256]{1,0:T(8,128)(2,1)} %copy-done.25, bf16[1024,256]{1,0:T(8,128)(2,1)} %copy-done.28, f32[896,256]{1,0:T(8,128)} %copy-done.3, f32[896,256]{1,0:T(8,128)} %copy-done.2), custom_call_target="tpu_custom_call" | custom-call | flops 7985954816 | bytes 8388608 | tf_op jit(solution)/shard_map/pallas_call | solution.py:241
  186.7 15.4 %all_to_all.42 = f32[16,16,128]{2,1,0:T(8,128)S(1)} all-to-all(f32[16,16,128]{2,1,0:T(8,128)S(1)} %tile.7), channel_id=1, replica_groups=mesh['dp'=16,'mp'=16] {'mp'}, dimensions={0} | all-to-all | bytes 262144 | tf_op jit(solution)/shard_map/all_to_all | solution.py:63
  202.1 11.7 %all_to_all.43 = f32[16,16,128]{2,1,0:T(8,128)S(1)} all-to-all(f32[16,16,128]{2,1,0:T(8,128)S(1)} %tile.8), channel_id=1, replica_groups=mesh['dp'=16,'mp'=16] {'dp'}, dimensions={0} | all-to-all | bytes 262144 | tf_op jit(solution)/shard_map/all_to_all | solution.py:63
  (133 shorter events, 28.2 us)
Async XLA Ops:
  0.0 53.3 %copy-start = (bf16[256,256]{1,0:T(8,128)(2,1)S(1)}, bf16[256,256]{1,0:T(8,128)(2,1)}, u32[]{:S(2)}) copy-start(bf16[256,256]{1,0:T(8,128)(2,1)} %param.13) | copy-start | bytes 393220
  1.7 18.8 %collective-permute-start.7 = (f32[896,256]{1,0:T(8,128)S(1)}, f32[896,256]{1,0:T(8,128)S(1)}, u32[]{:S(2)}, u32[]{:S(2)}) collective-permute-start(f32[896,256]{1,0:T(8,128)S(1)} %get-tuple-element.69), channel_id=1, source_target_pairs={{0,1},{1,0},{2,3},{3,2},{4,5},{5,4},{6,7},{7,6},{8,9},{9,8},{10,11... | collective-permute-start | bytes 2752520 | tf_op jit(solution)/shard_map/ppermute | solution.py:276
  5.0 8.9 %collective-permute-start = (bf16[64,1792]{1,0:T(8,128)(2,1)S(1)}, bf16[64,1792]{1,0:T(8,128)(2,1)S(1)}, u32[]{:S(2)}, u32[]{:S(2)}) collective-permute-start(bf16[64,1792]{1,0:T(8,128)(2,1)S(1)} %pad_maximum_fusion.2.refs_0_), channel_id=1, source_target_pairs={{0,224},{16,240},{32,0},{48,16},{64,32},{80,48},{96,64},{112,80},{... | collective-permute-start | bytes 688136 | tf_op jit(solution)/shard_map/ppermute | solution.py:87
  9.0 8.1 %collective-permute-start.1 = (bf16[64,1792]{1,0:T(8,128)(2,1)S(1)}, bf16[64,1792]{1,0:T(8,128)(2,1)S(1)}, u32[]{:S(2)}, u32[]{:S(2)}) collective-permute-start(bf16[64,1792]{1,0:T(8,128)(2,1)S(1)} %pad_maximum_fusion.2.refs_0_), channel_id=1, source_target_pairs={{0,32},{16,48},{32,64},{48,80},{64,96},{80,112},{96,128},{112,144}... | collective-permute-start | bytes 688136 | tf_op jit(solution)/shard_map/ppermute | solution.py:91
  9.0 8.1 %collective-permute-start.2 = (bf16[64,1792]{1,0:T(8,128)(2,1)S(1)}, bf16[64,1792]{1,0:T(8,128)(2,1)S(1)}, u32[]{:S(2)}, u32[]{:S(2)}) collective-permute-start(bf16[64,1792]{1,0:T(8,128)(2,1)S(1)} %pad_maximum_fusion.2.refs_0_), channel_id=1, source_target_pairs={{0,16},{16,0},{32,48},{48,32},{64,80},{80,64},{96,112},{112,96},{1... | collective-permute-start | bytes 688136 | tf_op jit(solution)/shard_map/ppermute | solution.py:95
  10.3 10.4 %collective-permute-start.6 = (bf16[64,256]{1,0:T(8,128)(2,1)S(1)}, bf16[64,256]{1,0:T(8,128)(2,1)S(1)}, u32[]{:S(2)}, u32[]{:S(2)}) collective-permute-start(bf16[64,256]{1,0:T(8,128)(2,1)S(1)} %pad_maximum_fusion.5), channel_id=1, source_target_pairs={{0,0},{1,16},{2,32},{3,48},{4,64},{5,80},{6,96},{7,112},{8,128},{9... | collective-permute-start | bytes 98312 | tf_op jit(solution)/shard_map/ppermute | solution.py:282
  17.8 6.7 %collective-permute-start.3 = (bf16[64,1792]{1,0:T(8,128)(2,1)S(1)}, bf16[64,1792]{1,0:T(8,128)(2,1)S(1)}, u32[]{:S(2)}, u32[]{:S(2)}) collective-permute-start(bf16[64,1792]{1,0:T(8,128)(2,1)S(1)} %get-tuple-element.37.refs_0_), channel_id=1, source_target_pairs={{0,224},{16,240},{32,0},{48,16},{64,32},{80,48},{96,64},{112,80},{... | collective-permute-start | bytes 688136 | tf_op jit(solution)/shard_map/ppermute | solution.py:87
  19.9 6.5 %collective-permute-start.5 = (bf16[64,1792]{1,0:T(8,128)(2,1)S(1)}, bf16[64,1792]{1,0:T(8,128)(2,1)S(1)}, u32[]{:S(2)}, u32[]{:S(2)}) collective-permute-start(bf16[64,1792]{1,0:T(8,128)(2,1)S(1)} %get-tuple-element.37.refs_0_), channel_id=1, source_target_pairs={{0,16},{16,0},{32,48},{48,32},{64,80},{80,64},{96,112},{112,96},{1... | collective-permute-start | bytes 688136 | tf_op jit(solution)/shard_map/ppermute | solution.py:95
  20.2 6.1 %collective-permute-start.4 = (bf16[64,1792]{1,0:T(8,128)(2,1)S(1)}, bf16[64,1792]{1,0:T(8,128)(2,1)S(1)}, u32[]{:S(2)}, u32[]{:S(2)}) collective-permute-start(bf16[64,1792]{1,0:T(8,128)(2,1)S(1)} %get-tuple-element.38.refs_1_), channel_id=1, source_target_pairs={{0,32},{16,48},{32,64},{48,80},{64,96},{80,112},{96,128},{112,144}... | collective-permute-start | bytes 688136 | tf_op jit(solution)/shard_map/ppermute | solution.py:91
  28.3 22.6 %all-to-all-start = ((bf16[16,64,256]{2,1,0:T(8,128)(2,1)}), bf16[16,64,256]{2,1,0:T(8,128)(2,1)S(1)}, u32[]{:S(2)}, u32[]{:S(2)}) async-start(bf16[16,64,256]{2,1,0:T(8,128)(2,1)} %tile.6), calls=%async_computation | async-start | bytes 1048576 | tf_op jit(solution)/shard_map/all_to_all | solution.py:63
  38.5 7.1 %collective-permute-start.8 = (bf16[64,1792]{1,0:T(8,128)(2,1)S(1)}, bf16[64,1792]{1,0:T(8,128)(2,1)S(1)}, u32[]{:S(2)}, u32[]{:S(2)}) collective-permute-start(bf16[64,1792]{1,0:T(8,128)(2,1)S(1)} %get-tuple-element.41.refs_0_), channel_id=1, source_target_pairs={{0,224},{16,240},{32,0},{48,16},{64,32},{80,48},{96,64},{112,80},{... | collective-permute-start | bytes 688136 | tf_op jit(solution)/shard_map/ppermute | solution.py:87
  38.5 8.3 %collective-permute-start.9 = (bf16[64,1792]{1,0:T(8,128)(2,1)S(1)}, bf16[64,1792]{1,0:T(8,128)(2,1)S(1)}, u32[]{:S(2)}, u32[]{:S(2)}) collective-permute-start(bf16[64,1792]{1,0:T(8,128)(2,1)S(1)} %get-tuple-element.42.refs_1_), channel_id=1, source_target_pairs={{0,32},{16,48},{32,64},{48,80},{64,96},{80,112},{96,128},{112,144}... | collective-permute-start | bytes 688136 | tf_op jit(solution)/shard_map/ppermute | solution.py:91
  39.9 10.9 %collective-permute-start.10 = (bf16[64,1792]{1,0:T(8,128)(2,1)S(1)}, bf16[64,1792]{1,0:T(8,128)(2,1)}, u32[]{:S(2)}, u32[]{:S(2)}) collective-permute-start(bf16[64,1792]{1,0:T(8,128)(2,1)S(1)} %get-tuple-element.40.refs_3_), channel_id=1, source_target_pairs={{0,16},{16,0},{32,48},{48,32},{64,80},{80,64},{96,112},{112,96},{1... | collective-permute-start | bytes 688136 | tf_op jit(solution)/shard_map/ppermute | solution.py:95
  50.9 6.4 %collective-permute-start.11 = (bf16[64,1792]{1,0:T(8,128)(2,1)S(1)}, bf16[64,1792]{1,0:T(8,128)(2,1)S(1)}, u32[]{:S(2)}, u32[]{:S(2)}) collective-permute-start(bf16[64,1792]{1,0:T(8,128)(2,1)S(1)} %get-tuple-element.45.refs_4_), channel_id=1, source_target_pairs={{0,224},{16,240},{32,0},{48,16},{64,32},{80,48},{96,64},{112,80},{... | collective-permute-start | bytes 688136 | tf_op jit(solution)/shard_map/ppermute | solution.py:87
  51.2 7.6 %collective-permute-start.12 = (bf16[64,1792]{1,0:T(8,128)(2,1)}, bf16[64,1792]{1,0:T(8,128)(2,1)S(1)}, u32[]{:S(2)}, u32[]{:S(2)}) collective-permute-start(bf16[64,1792]{1,0:T(8,128)(2,1)} %get-tuple-element.46.refs_5_), channel_id=1, source_target_pairs={{0,32},{16,48},{32,64},{48,80},{64,96},{80,112},{96,128},{112,144}... | collective-permute-start | bytes 688136 | tf_op jit(solution)/shard_map/ppermute | solution.py:91
  52.4 11.3 %collective-permute-start.13 = (bf16[64,1792]{1,0:T(8,128)(2,1)S(1)}, bf16[64,1792]{1,0:T(8,128)(2,1)S(1)}, u32[]{:S(2)}, u32[]{:S(2)}) collective-permute-start(bf16[64,1792]{1,0:T(8,128)(2,1)S(1)} %get-tuple-element.50.refs_1_), channel_id=1, source_target_pairs={{0,32},{16,48},{32,64},{48,80},{64,96},{80,112},{96,128},{112,144}... | collective-permute-start | bytes 688136 | tf_op jit(solution)/shard_map/ppermute | solution.py:91
  52.5 11.3 %collective-permute-start.14 = (bf16[64,1792]{1,0:T(8,128)(2,1)S(1)}, bf16[64,1792]{1,0:T(8,128)(2,1)S(1)}, u32[]{:S(2)}, u32[]{:S(2)}) collective-permute-start(bf16[64,1792]{1,0:T(8,128)(2,1)S(1)} %get-tuple-element.49.refs_0_), channel_id=1, source_target_pairs={{0,16},{16,0},{32,48},{48,32},{64,80},{80,64},{96,112},{112,96},{1... | collective-permute-start | bytes 688136 | tf_op jit(solution)/shard_map/ppermute | solution.py:95
  63.9 13.1 %collective-permute-start.16 = (bf16[64,1792]{1,0:T(8,128)(2,1)S(1)}, bf16[64,1792]{1,0:T(8,128)(2,1)S(1)}, u32[]{:S(2)}, u32[]{:S(2)}) collective-permute-start(bf16[64,1792]{1,0:T(8,128)(2,1)S(1)} %get-tuple-element.58.refs_3_), channel_id=1, source_target_pairs={{0,16},{16,0},{32,48},{48,32},{64,80},{80,64},{96,112},{112,96},{1... | collective-permute-start | bytes 688136 | tf_op jit(solution)/shard_map/ppermute | solution.py:95
  65.0 11.9 %collective-permute-start.17 = (bf16[64,1792]{1,0:T(8,128)(2,1)S(1)}, bf16[64,1792]{1,0:T(8,128)(2,1)S(1)}, u32[]{:S(2)}, u32[]{:S(2)}) collective-permute-start(bf16[64,1792]{1,0:T(8,128)(2,1)S(1)} %get-tuple-element.52.refs_9_.refs_4_), channel_id=1, source_target_pairs={{0,224},{16,240},{32,0},{48,16},{64,32},{80,48},{96,64},{112,80},{... | collective-permute-start | bytes 688136 | tf_op jit(solution)/shard_map/ppermute | solution.py:87
  65.0 11.0 %collective-permute-start.18 = (bf16[512,256]{1,0:T(8,128)(2,1)S(1)}, bf16[512,256]{1,0:T(8,128)(2,1)S(1)}, u32[]{:S(2)}, u32[]{:S(2)}) collective-permute-start(bf16[512,256]{1,0:T(8,128)(2,1)S(1)} %get-tuple-element.60), channel_id=1, source_target_pairs={{0,16},{16,0},{32,48},{48,32},{64,80},{80,64},{96,112},{112,96},{1... | collective-permute-start | bytes 786440 | tf_op jit(solution)/shard_map/ppermute | solution.py:315
  73.6 13.9 %collective-permute-start.15 = (bf16[512,896]{1,0:T(8,128)(2,1)}, bf16[512,896]{1,0:T(8,128)(2,1)S(1)}, u32[]{:S(2)}, u32[]{:S(2)}) collective-permute-start(bf16[512,896]{1,0:T(8,128)(2,1)} %get-tuple-element.54), channel_id=1, source_target_pairs={{0,1},{1,0},{2,3},{3,2},{4,5},{5,4},{6,7},{7,6},{8,9},{9,8},{10,11... | collective-permute-start | bytes 2752520 | tf_op jit(solution)/shard_map/ppermute | solution.py:325
  86.0 4.0 %collective-permute-start.19 = (bf16[512,896]{1,0:T(8,128)(2,1)}, bf16[512,896]{1,0:T(8,128)(2,1)}, u32[]{:S(2)}, u32[]{:S(2)}) collective-permute-start(bf16[512,896]{1,0:T(8,128)(2,1)} %get-tuple-element.62), channel_id=1, source_target_pairs={{0,1},{1,0},{2,3},{3,2},{4,5},{5,4},{6,7},{7,6},{8,9},{9,8},{10,11... | collective-permute-start | bytes 2752520 | tf_op jit(solution)/shard_map/ppermute | solution.py:325
  92.7 37.0 %all-to-all-start.1 = ((bf16[8,128,896]{2,1,0:T(8,128)(2,1)}), bf16[8,128,896]{2,1,0:T(8,128)(2,1)S(1)}, u32[]{:S(2)}, u32[]{:S(2)}) async-start(bf16[8,128,896]{2,1,0:T(8,128)(2,1)} %bitcast.16), calls=%async_computation.1 | async-start | bytes 3670016 | tf_op jit(solution)/shard_map/all_to_all | solution.py:63
  99.1 7.3 %collective-permute-start.20 = (f32[256,256]{1,0:T(8,128)S(1)}, f32[256,256]{1,0:T(8,128)S(1)}, u32[]{:S(2)}, u32[]{:S(2)}) collective-permute-start(f32[256,256]{1,0:T(8,128)S(1)} %constant_dynamic-slice_fusion.2), channel_id=1, source_target_pairs={{0,32},{16,48},{32,0},{48,16},{64,96},{80,112},{96,64},{112,80},{1... | collective-permute-start | bytes 786440 | tf_op jit(solution)/shard_map/ppermute | solution.py:319
  106.5 8.7 %collective-permute-start.21 = (f32[128,256]{1,0:T(8,128)S(1)}, f32[128,256]{1,0:T(8,128)S(1)}, u32[]{:S(2)}, u32[]{:S(2)}) collective-permute-start(f32[128,256]{1,0:T(8,128)S(1)} %constant_dynamic-slice_fusion.1), channel_id=1, source_target_pairs={{0,64},{16,80},{32,96},{48,112},{64,0},{80,16},{96,32},{112,48},{1... | collective-permute-start | bytes 393224 | tf_op jit(solution)/shard_map/ppermute | solution.py:319
  115.2 7.7 %collective-permute-start.22 = (f32[64,256]{1,0:T(8,128)S(1)}, f32[64,256]{1,0:T(8,128)S(1)}, u32[]{:S(2)}, u32[]{:S(2)}) collective-permute-start(f32[64,256]{1,0:T(8,128)S(1)} %constant_dynamic-slice_fusion), channel_id=1, source_target_pairs={{0,128},{16,144},{32,160},{48,176},{64,192},{80,208},{96,224},{112... | collective-permute-start | bytes 196616 | tf_op jit(solution)/shard_map/ppermute | solution.py:319
  122.9 6.8 %collective-permute-start.23 = (bf16[64,256]{1,0:T(8,128)(2,1)S(1)}, bf16[64,256]{1,0:T(8,128)(2,1)S(1)}, u32[]{:S(2)}, u32[]{:S(2)}) collective-permute-start(bf16[64,256]{1,0:T(8,128)(2,1)S(1)} %get-tuple-element.66), channel_id=1, source_target_pairs={{0,128},{16,144},{32,160},{48,176},{64,192},{80,208},{96,224},{112... | collective-permute-start | bytes 98312 | tf_op jit(solution)/shard_map/ppermute | solution.py:331
  131.2 35.8 %all-to-all-start.2 = ((bf16[8,128,896]{2,1,0:T(8,128)(2,1)}), bf16[8,128,896]{2,1,0:T(8,128)(2,1)S(1)}, u32[]{:S(2)}, u32[]{:S(2)}) async-start(bf16[8,128,896]{2,1,0:T(8,128)(2,1)} %bitcast.14), calls=%async_computation.2 | async-start | bytes 3670016 | tf_op jit(solution)/shard_map/all_to_all | solution.py:63
  137.3 4.0 %collective-permute-start.24 = (bf16[128,256]{1,0:T(8,128)(2,1)S(1)}, bf16[128,256]{1,0:T(8,128)(2,1)S(1)}, u32[]{:S(2)}, u32[]{:S(2)}) collective-permute-start(bf16[128,256]{1,0:T(8,128)(2,1)S(1)} %pad_maximum_fusion.4.refs_0_), channel_id=1, source_target_pairs={{0,64},{16,80},{32,96},{48,112},{64,0},{80,16},{96,32},{112,48},{1... | collective-permute-start | bytes 196616 | tf_op jit(solution)/shard_map/ppermute | solution.py:331
  141.4 4.9 %collective-permute-start.25 = (bf16[256,256]{1,0:T(8,128)(2,1)S(1)}, bf16[256,256]{1,0:T(8,128)(2,1)S(1)}, u32[]{:S(2)}, u32[]{:S(2)}) collective-permute-start(bf16[256,256]{1,0:T(8,128)(2,1)S(1)} %pad_maximum_fusion.3), channel_id=1, source_target_pairs={{0,32},{16,48},{32,0},{48,16},{64,96},{80,112},{96,64},{112,80},{1... | collective-permute-start | bytes 393224 | tf_op jit(solution)/shard_map/ppermute | solution.py:331
  146.3 17.1 %collective-permute-start.26 = (bf16[512,256]{1,0:T(8,128)(2,1)S(1)}, bf16[512,256]{1,0:T(8,128)(2,1)S(1)}, u32[]{:S(2)}, u32[]{:S(2)}) collective-permute-start(bf16[512,256]{1,0:T(8,128)(2,1)S(1)} %pad_maximum_fusion.1), channel_id=1, source_target_pairs={{0,16},{16,0},{32,48},{48,32},{64,80},{80,64},{96,112},{112,96},{1... | collective-permute-start | bytes 786440 | tf_op jit(solution)/shard_map/ppermute | solution.py:331
  163.4 3.6 %collective-permute-start.27 = (bf16[1024,256]{1,0:T(8,128)(2,1)S(1)}, bf16[1024,256]{1,0:T(8,128)(2,1)S(1)}, u32[]{:S(2)}, u32[]{:S(2)}) collective-permute-start(bf16[1024,256]{1,0:T(8,128)(2,1)S(1)} %constant_dynamic-update-slice_fusion.own_acts_ref), channel_id=1, source_target_pairs={{0,1},{1,0},{2,3},{3,2},{4,5},{5,4},{6,7},{7,6},{8,9},{9,8},{10,11... | collective-permute-start | bytes 1572872 | tf_op jit(solution)/shard_map/ppermute | solution.py:333
  (30 other events, 304.1 us)

commit v5 on v4

--- a/solution.py
+++ b/solution.py
@@ -71,16 +71,16 @@
     del refs
 
 
-def fence(*arrays):
+def fence(*arrays, needs=()):
     anywhere = pl.BlockSpec(memory_space=pl.ANY)
     return pl.pallas_call(
         fence_kernel,
         out_shape=[jax.ShapeDtypeStruct(a.shape, a.dtype) for a in arrays],
-        in_specs=[anywhere] * len(arrays),
+        in_specs=[anywhere] * (len(arrays) + len(needs)),
         out_specs=[anywhere] * len(arrays),
         input_output_aliases={i: i for i in range(len(arrays))},
         compiler_params=pltpu.CompilerParams(vmem_limit_bytes=1024 * 1024),
-    )(*arrays)
+    )(*arrays, *needs)
 
 
 def up(x):
@@ -147,6 +147,10 @@
     )(core.reshape(1), *blocks, basis, *needs)
 
 
+def after(x, y):
+    return x + jnp.minimum(jnp.abs(y[:1, :1]), 0).astype(x.dtype)
+
+
 def sum_kernel(parts_ref, *refs):
     out_ref = refs[-1]
     rows = parts_ref.shape[0] // CHIPS
@@ -283,15 +287,14 @@
     held[(0, 0)], held[(1, 0)], held[(-1, 0)], held[(0, 1)] = fence(
         grads, up(grads), down(grads), over(grads)
     )
-    (held[(1, 0)], held[(-1, 0)], held[(2, 0)], held[(-2, 0)], held[(1, 1)], moved, own_inv,
-     sib_inv) = fence(
+    held[(1, 0)], held[(-1, 0)], held[(2, 0)], held[(-2, 0)], held[(1, 1)], moved = fence(
         held[(1, 0)], held[(-1, 0)], up(held[(1, 0)]), down(held[(-1, 0)]),
-        over(held[(1, 0)]), moved, own_inv, sib_inv,
-    )
-    (held[(2, 0)], held[(-2, 0)], held[(3, 0)], held[(-3, 0)], held[(1, 1)], held[(-1, 1)],
-     every_acts) = fence(
+        over(held[(1, 0)]), moved, needs=(own_inv, sib_inv),
+    )
+    every_acts = share(moved, GROUPS, "mp")
+    held[(2, 0)], held[(-2, 0)], held[(3, 0)], held[(-3, 0)], held[(1, 1)], held[(-1, 1)] = fence(
         held[(2, 0)], held[(-2, 0)], up(held[(2, 0)]), down(held[(-2, 0)]), held[(1, 1)],
-        over(held[(-1, 0)]), share(moved, GROUPS, "mp"),
+        over(held[(-1, 0)]),
     )
 
     bits = (yl, z % 2, z // 2 % 2, z // 4)
@@ -326,13 +329,13 @@
         pairs.append((own_part + got.astype(jnp.float32)).astype(jnp.bfloat16))
     parts = exchange(jnp.concatenate(pairs, 0), "mp", axis_index_groups=SAME_CORE)
 
-    doubled = []
+    copies = sum_and_copy(parts)
+
+    own_acts = after(own_acts, copies)
     for swap in DP_SWAPS[::-1]:
         own_acts = jnp.concatenate([own_acts, lax.ppermute(own_acts, "dp", swap)], 0)
-        doubled.append(own_acts)
     sib_acts = lax.ppermute(own_acts, "mp", CORE_SWAP)
 
-    copies = sum_and_copy(parts, doubled[0])
     all_grads = exchange(copies, "mp", axis_index_groups=SAME_CORE)
 
     places = [place for chunk in CHUNKS for place in chunk]

time: 215 us -> 211 us (0.981)
  local copies, waits for them, and re-layouts: 6.31 us -> 3.98 us
    ppermute x5, waiting for transfers between devices: 4.1 us -> 16.5 us  [over(): return lax.ppermute(x, 'dp', dp_shift(0, 1))]
    all_to_all x3, waiting for transfers between devices: 0.01 us -> 10.7 us  [exchange(): return lax.all_to_all(x, axis, 0, 0, tiled=True, **kw)]
    ppermute x4, waiting for transfers between devices: 29.4 us -> 19.9 us  [shards(): lax.ppermute(own_acts, 'dp', swap)]
    ppermute x5, waiting for transfers between devices: 14.2 us -> 7.59 us  [up(): return lax.ppermute(x, 'dp', dp_shift(-1, 0))]
    ppermute x3, waiting for transfers between devices: 19.7 us -> 13.2 us  [shards(): summed = mine + lax.ppermute(away, 'dp', swap)]
    all_to_all x3, starting transfers between devices: 22.7 us -> 19.5 us  [exchange(): return lax.all_to_all(x, axis, 0, 0, tiled=True, **kw)]
    unnamed x65 -> x67, local copies, waits for them, and re-layouts: 5.24 us -> 2.34 us
    ppermute x4, starting transfers between devices: 3.32 us -> 5.71 us  [shards(): lax.ppermute(own_acts, 'dp', swap)]
  transfers between devices with their start and end apart: 31 -> 31, of which waited for: 19 -> 19; matrix products, arithmetic and copies ran while one was open for 1% -> 2% of each run, Pallas kernels for 8% -> 8%
where the time goes in v5:
time: 211 us
  waiting for transfers between devices  81.1 us (38%)
  starting transfers between devices  55.2 us (26%)
  Pallas kernels  34.3 us (16%)
  blocking collectives  27.5 us (13%)
  other arithmetic  7.03 us (3%)
  local copies, waits for them, and re-layouts  3.98 us (2%)
    all_to_all x2, blocking collectives, exchange(): return lax.all_to_all(x, axis, 0, 0, tiled=True, **kw)  27.5 us
    ppermute x4, waiting for transfers between devices, shards(): lax.ppermute(own_acts, 'dp', swap)  19.9 us
    all_to_all x3, starting transfers between devices, exchange(): return lax.all_to_all(x, axis, 0, 0, tiled=True, **kw)  19.5 us
    pallas_call x1, Pallas kernels, score_blocks(): pl.pallas_call(score_kernel, out_shape=jax.ShapeDtypeStruct((GROUPS, 128)...  17.5 us
    pallas_call x2, Pallas kernels, turn(): pl.pallas_call(functools.partial(turn_kernel, len(blocks)), grid_spec=plt...  16.5 us
    ppermute x5, waiting for transfers between devices, over(): return lax.ppermute(x, 'dp', dp_shift(0, 1))  16.5 us
    ppermute x3, waiting for transfers between devices, shards(): summed = mine + lax.ppermute(away, 'dp', swap)  13.2 us
    ppermute x5, waiting for transfers between devices, down(): return lax.ppermute(x, 'dp', dp_shift(1, 0))  10.8 us
  transfers between devices with their start and end apart: 31, of which 19 were waited for; matrix products, arithmetic and copies ran while one was open for 2% of the time, Pallas kernels for 8%

profile of v5, /device:TPU:1, one launch (start us, length us, event | category | flops | bytes accessed | tf_op | source)
XLA Modules:
  0.0 210.6 jit_solution(9109898539065106714)
XLA Ops:
  1.7 3.3 %collective-permute-start.7 = (f32[896,256]{1,0:T(8,128)S(1)}, f32[896,256]{1,0:T(8,128)S(1)}, u32[]{:S(2)}, u32[]{:S(2)}) collective-permute-start(f32[896,256]{1,0:T(8,128)S(1)} %get-tuple-element.63), channel_id=1, source_target_pairs={{0,1},{1,0},{2,3},{3,2},{4,5},{5,4},{6,7},{7,6},{8,9},{9,8},{10,11... | collective-permute-start | bytes 2752520 | tf_op jit(solution)/shard_map/ppermute | solution.py:280
  5.0 3.9 %collective-permute-start = (bf16[64,1792]{1,0:T(8,128)(2,1)S(1)}, bf16[64,1792]{1,0:T(8,128)(2,1)S(1)}, u32[]{:S(2)}, u32[]{:S(2)}) collective-permute-start(bf16[64,1792]{1,0:T(8,128)(2,1)S(1)} %pad_maximum_fusion.2.refs_0_), channel_id=1, source_target_pairs={{0,224},{16,240},{32,0},{48,16},{64,32},{80,48},{96,64},{112,80},{... | collective-permute-start | bytes 688136 | tf_op jit(solution)/shard_map/ppermute | solution.py:87
  10.3 2.6 %collective-permute-start.6 = (bf16[64,256]{1,0:T(8,128)(2,1)S(1)}, bf16[64,256]{1,0:T(8,128)(2,1)S(1)}, u32[]{:S(2)}, u32[]{:S(2)}) collective-permute-start(bf16[64,256]{1,0:T(8,128)(2,1)S(1)} %pad_maximum_fusion.5), channel_id=1, source_target_pairs={{0,0},{1,16},{2,32},{3,48},{4,64},{5,80},{6,96},{7,112},{8,128},{9... | collective-permute-start | bytes 98312 | tf_op jit(solution)/shard_map/ppermute | solution.py:286
  14.0 3.1 %collective-permute-done.1.refs_2_ = bf16[64,1792]{1,0:T(8,128)(2,1)S(1)} collective-permute-done((bf16[64,1792]{1,0:T(8,128)(2,1)S(1)}, bf16[64,1792]{1,0:T(8,128)(2,1)S(1)}, u32[]{:S(2)}, u32[]{:S(2)}) %collective-permute-start.1) | collective-permute-done | bytes 229408 | tf_op jit(solution)/shard_map/ppermute | solution.py:91
  17.1 2.2 %collective-permute-start.3 = (bf16[64,1792]{1,0:T(8,128)(2,1)S(1)}, bf16[64,1792]{1,0:T(8,128)(2,1)S(1)}, u32[]{:S(2)}, u32[]{:S(2)}) collective-permute-start(bf16[64,1792]{1,0:T(8,128)(2,1)S(1)} %get-tuple-element.34.refs_0_), channel_id=1, source_target_pairs={{0,224},{16,240},{32,0},{48,16},{64,32},{80,48},{96,64},{112,80},{... | collective-permute-start | bytes 688136 | tf_op jit(solution)/shard_map/ppermute | solution.py:87
  20.1 4.2 %collective-permute-done.3.refs_2_ = bf16[64,1792]{1,0:T(8,128)(2,1)S(1)} collective-permute-done((bf16[64,1792]{1,0:T(8,128)(2,1)S(1)}, bf16[64,1792]{1,0:T(8,128)(2,1)S(1)}, u32[]{:S(2)}, u32[]{:S(2)}) %collective-permute-start.3) | collective-permute-done | bytes 229408 | tf_op jit(solution)/shard_map/ppermute | solution.py:87
  27.5 9.3 %all-to-all-start = ((bf16[16,64,256]{2,1,0:T(8,128)(2,1)}), bf16[16,64,256]{2,1,0:T(8,128)(2,1)S(1)}, u32[]{:S(2)}, u32[]{:S(2)}) async-start(bf16[16,64,256]{2,1,0:T(8,128)(2,1)} %tile.6), calls=%async_computation | async-start | bytes 1048576 | tf_op jit(solution)/shard_map/all_to_all | solution.py:63
  38.4 9.7 %collective-permute-done.10.refs_5_ = bf16[64,1792]{1,0:T(8,128)(2,1)S(1)} collective-permute-done((bf16[64,1792]{1,0:T(8,128)(2,1)S(1)}, bf16[64,1792]{1,0:T(8,128)(2,1)S(1)}, u32[]{:S(2)}, u32[]{:S(2)}) %collective-permute-start.10) | collective-permute-done | bytes 229408 | tf_op jit(solution)/shard_map/ppermute | solution.py:95
  49.7 2.0 collective-permute-start.14
  52.0 2.3 %collective-permute-done.11.refs_2_ = bf16[64,1792]{1,0:T(8,128)(2,1)S(1)} collective-permute-done((bf16[64,1792]{1,0:T(8,128)(2,1)S(1)}, bf16[64,1792]{1,0:T(8,128)(2,1)S(1)}, u32[]{:S(2)}, u32[]{:S(2)}) %collective-permute-start.11) | collective-permute-done | bytes 229408 | tf_op jit(solution)/shard_map/ppermute | solution.py:87
  55.6 4.9 %collective-permute-done.13.refs_4_ = bf16[64,1792]{1,0:T(8,128)(2,1)S(1)} collective-permute-done((bf16[64,1792]{1,0:T(8,128)(2,1)S(1)}, bf16[64,1792]{1,0:T(8,128)(2,1)S(1)}, u32[]{:S(2)}, u32[]{:S(2)}) %collective-permute-start.13) | collective-permute-done | bytes 229408 | tf_op jit(solution)/shard_map/ppermute | solution.py:91
  60.6 2.5 %collective-permute-start.18 = (bf16[512,256]{1,0:T(8,128)(2,1)S(1)}, bf16[512,256]{1,0:T(8,128)(2,1)S(1)}, u32[]{:S(2)}, u32[]{:S(2)}) collective-permute-start(bf16[512,256]{1,0:T(8,128)(2,1)S(1)} %get-tuple-element.56), channel_id=1, source_target_pairs={{0,16},{16,0},{32,48},{48,32},{64,80},{80,64},{96,112},{112,96},{1... | collective-permute-start | bytes 786440 | tf_op jit(solution)/shard_map/ppermute | solution.py:318
  63.1 8.2 %shard_map.95 = (bf16[512,896]{1,0:T(8,128)(2,1)}, f32[512,896]{1,0:T(8,128)}) custom-call(s32[1]{0:T(128)} %bitcast.core_ref, bf16[64,1792]{1,0:T(8,128)(2,1)} %copy-done.9, bf16[64,1792]{1,0:T(8,128)(2,1)} %copy-done.16, bf16[64,1792]{1,0:T(8,128)(2,1)} %copy-done.4, bf16[64,1792]{1,0:T(8,128)(2,1)} %copy-done.5, bf16[64,1792]{1,0:T(8,128)(2,1)} %copy-done.7, ...), custom_call_target="tpu_custom_call" | custom-call | flops 3288334336 | bytes 11010048 | tf_op jit(solution)/shard_map/pallas_call | solution.py:126
  71.4 1.8 collective-permute-start.15
  74.3 6.0 %collective-permute-done.16.refs_5_ = bf16[64,1792]{1,0:T(8,128)(2,1)S(1)} collective-permute-done((bf16[64,1792]{1,0:T(8,128)(2,1)S(1)}, bf16[64,1792]{1,0:T(8,128)(2,1)S(1)}, u32[]{:S(2)}, u32[]{:S(2)}) %collective-permute-start.16) | collective-permute-done | bytes 229408 | tf_op jit(solution)/shard_map/ppermute | solution.py:95
  81.1 8.3 %shard_map.96 = (bf16[512,896]{1,0:T(8,128)(2,1)}, f32[512,896]{1,0:T(8,128)}) custom-call(s32[1]{0:T(128)} %bitcast.core_ref, bf16[64,1792]{1,0:T(8,128)(2,1)} %copy-done.12, bf16[64,1792]{1,0:T(8,128)(2,1)} %copy-done.13, bf16[64,1792]{1,0:T(8,128)(2,1)} %copy-done.10, bf16[64,1792]{1,0:T(8,128)(2,1)} %copy-done.11, bf16[64,1792]{1,0:T(8,128)(2,1)} %copy-done.15, ...), custom_call_target="tpu_custom_call" | custom-call | flops 3288334336 | bytes 11010048 | tf_op jit(solution)/shard_map/pallas_call | solution.py:126
  90.4 2.1 %collective-permute-done.19 = bf16[512,896]{1,0:T(8,128)(2,1)S(1)} collective-permute-done((bf16[512,896]{1,0:T(8,128)(2,1)}, bf16[512,896]{1,0:T(8,128)(2,1)S(1)}, u32[]{:S(2)}, u32[]{:S(2)}) %collective-permute-start.19) | collective-permute-done | bytes 917536 | tf_op jit(solution)/shard_map/ppermute | solution.py:328
  94.1 6.5 %all-to-all-start.1 = ((bf16[8,128,896]{2,1,0:T(8,128)(2,1)}), bf16[8,128,896]{2,1,0:T(8,128)(2,1)S(1)}, u32[]{:S(2)}, u32[]{:S(2)}) async-start(bf16[8,128,896]{2,1,0:T(8,128)(2,1)} %bitcast.16), calls=%async_computation.1 | async-start | bytes 3670016 | tf_op jit(solution)/shard_map/all_to_all | solution.py:63
  100.7 1.8 collective-permute-start.20
  102.5 6.0 %collective-permute-done.20 = f32[256,256]{1,0:T(8,128)S(1)} collective-permute-done((f32[256,256]{1,0:T(8,128)S(1)}, f32[256,256]{1,0:T(8,128)S(1)}, u32[]{:S(2)}, u32[]{:S(2)}) %collective-permute-start.20) | collective-permute-done | bytes 262176 | tf_op jit(solution)/shard_map/ppermute | solution.py:322
  109.8 7.1 %collective-permute-done.21 = f32[128,256]{1,0:T(8,128)S(1)} collective-permute-done((f32[128,256]{1,0:T(8,128)S(1)}, f32[128,256]{1,0:T(8,128)S(1)}, u32[]{:S(2)}, u32[]{:S(2)}) %collective-permute-start.21) | collective-permute-done | bytes 131104 | tf_op jit(solution)/shard_map/ppermute | solution.py:322
  117.1 10.7 %all-to-all-done.1 = bf16[8,128,896]{2,1,0:T(8,128)(2,1)S(1)} async-done(((bf16[8,128,896]{2,1,0:T(8,128)(2,1)}), bf16[8,128,896]{2,1,0:T(8,128)(2,1)S(1)}, u32[]{:S(2)}, u32[]{:S(2)}) %all-to-all-start.1) | async-done | bytes 1835040 | tf_op jit(solution)/shard_map/all_to_all | solution.py:63
  129.3 3.6 %all-to-all-start.2 = ((bf16[8,128,896]{2,1,0:T(8,128)(2,1)}), bf16[8,128,896]{2,1,0:T(8,128)(2,1)S(1)}, u32[]{:S(2)}, u32[]{:S(2)}) async-start(bf16[8,128,896]{2,1,0:T(8,128)(2,1)} %bitcast.15), calls=%async_computation.2 | async-start | bytes 3670016 | tf_op jit(solution)/shard_map/all_to_all | solution.py:63
  133.0 2.3 %collective-permute-start.23 = (bf16[64,256]{1,0:T(8,128)(2,1)S(1)}, bf16[64,256]{1,0:T(8,128)(2,1)S(1)}, u32[]{:S(2)}, u32[]{:S(2)}) collective-permute-start(bf16[64,256]{1,0:T(8,128)(2,1)S(1)} %get-tuple-element.60), channel_id=1, source_target_pairs={{0,128},{16,144},{32,160},{48,176},{64,192},{80,208},{96,224},{112... | collective-permute-start | bytes 98312 | tf_op jit(solution)/shard_map/ppermute | solution.py:336
  135.3 4.5 %collective-permute-done.23 = bf16[64,256]{1,0:T(8,128)(2,1)S(1)} collective-permute-done((bf16[64,256]{1,0:T(8,128)(2,1)S(1)}, bf16[64,256]{1,0:T(8,128)(2,1)S(1)}, u32[]{:S(2)}, u32[]{:S(2)}) %collective-permute-start.23) | collective-permute-done | bytes 32800 | tf_op jit(solution)/shard_map/ppermute | solution.py:336
  141.4 2.8 %collective-permute-done.24 = bf16[128,256]{1,0:T(8,128)(2,1)S(1)} collective-permute-done((bf16[128,256]{1,0:T(8,128)(2,1)S(1)}, bf16[128,256]{1,0:T(8,128)(2,1)S(1)}, u32[]{:S(2)}, u32[]{:S(2)}) %collective-permute-start.24) | collective-permute-done | bytes 65568 | tf_op jit(solution)/shard_map/ppermute | solution.py:336
  145.9 2.7 %collective-permute-done.25 = bf16[256,256]{1,0:T(8,128)(2,1)S(1)} collective-permute-done((bf16[256,256]{1,0:T(8,128)(2,1)S(1)}, bf16[256,256]{1,0:T(8,128)(2,1)S(1)}, u32[]{:S(2)}, u32[]{:S(2)}) %collective-permute-start.25) | collective-permute-done | bytes 131104 | tf_op jit(solution)/shard_map/ppermute | solution.py:336
  148.7 9.9 %collective-permute-done.26 = bf16[512,256]{1,0:T(8,128)(2,1)S(1)} collective-permute-done((bf16[512,256]{1,0:T(8,128)(2,1)S(1)}, bf16[512,256]{1,0:T(8,128)(2,1)S(1)}, u32[]{:S(2)}, u32[]{:S(2)}) %collective-permute-start.26) | collective-permute-done | bytes 262176 | tf_op jit(solution)/shard_map/ppermute | solution.py:336
  158.7 2.5 %collective-permute-start.27 = (bf16[1024,256]{1,0:T(8,128)(2,1)S(1)}, bf16[1024,256]{1,0:T(8,128)(2,1)S(1)}, u32[]{:S(2)}, u32[]{:S(2)}) collective-permute-start(bf16[1024,256]{1,0:T(8,128)(2,1)S(1)} %constant_dynamic-update-slice_fusion.own_acts_ref), channel_id=1, source_target_pairs={{0,1},{1,0},{2,3},{3,2},{4,5},{5,4},{6,7},{7,6},{8,9},{9,8},{10,11... | collective-permute-start | bytes 1572872 | tf_op jit(solution)/shard_map/ppermute | solution.py:337
  164.2 17.5 %shard_map.98 = f32[16,128]{1,0:T(8,128)} custom-call(s32[16]{0:T(128)} %get-tuple-element.61.acts_at_ref, f32[16,16]{1,0:T(8,128)} %fusion.1.place_ref, bf16[1024,896]{1,0:T(8,128)(2,1)} %bitcast.18, bf16[1024,256]{1,0:T(8,128)(2,1)} %copy-done.26, bf16[1024,256]{1,0:T(8,128)(2,1)} %copy-done.29, f32[896,256]{1,0:T(8,128)} %copy-done.3, f32[896,256]{1,0:T(8,128)} %copy-done.2), custom_call_target="tpu_custom_call" | custom-call | flops 7985954816 | bytes 8388608 | tf_op jit(solution)/shard_map/pallas_call | solution.py:245
  182.5 14.1 %all_to_all.43 = f32[16,16,128]{2,1,0:T(8,128)S(1)} all-to-all(f32[16,16,128]{2,1,0:T(8,128)S(1)} %tile.7), channel_id=1, replica_groups=mesh['dp'=16,'mp'=16] {'mp'}, dimensions={0} | all-to-all | bytes 262144 | tf_op jit(solution)/shard_map/all_to_all | solution.py:63
  196.6 13.3 %all_to_all.44 = f32[16,16,128]{2,1,0:T(8,128)S(1)} all-to-all(f32[16,16,128]{2,1,0:T(8,128)S(1)} %tile.8), channel_id=1, replica_groups=mesh['dp'=16,'mp'=16] {'dp'}, dimensions={0} | all-to-all | bytes 262144 | tf_op jit(solution)/shard_map/all_to_all | solution.py:63
  (136 shorter events, 27.4 us)
Async XLA Ops:
  0.0 51.7 %copy-start = (bf16[256,256]{1,0:T(8,128)(2,1)S(1)}, bf16[256,256]{1,0:T(8,128)(2,1)}, u32[]{:S(2)}) copy-start(bf16[256,256]{1,0:T(8,128)(2,1)} %param.13) | copy-start | bytes 393220
  1.7 18.2 %collective-permute-start.7 = (f32[896,256]{1,0:T(8,128)S(1)}, f32[896,256]{1,0:T(8,128)S(1)}, u32[]{:S(2)}, u32[]{:S(2)}) collective-permute-start(f32[896,256]{1,0:T(8,128)S(1)} %get-tuple-element.63), channel_id=1, source_target_pairs={{0,1},{1,0},{2,3},{3,2},{4,5},{5,4},{6,7},{7,6},{8,9},{9,8},{10,11... | collective-permute-start | bytes 2752520 | tf_op jit(solution)/shard_map/ppermute | solution.py:280
  5.0 8.9 %collective-permute-start = (bf16[64,1792]{1,0:T(8,128)(2,1)S(1)}, bf16[64,1792]{1,0:T(8,128)(2,1)S(1)}, u32[]{:S(2)}, u32[]{:S(2)}) collective-permute-start(bf16[64,1792]{1,0:T(8,128)(2,1)S(1)} %pad_maximum_fusion.2.refs_0_), channel_id=1, source_target_pairs={{0,224},{16,240},{32,0},{48,16},{64,32},{80,48},{96,64},{112,80},{... | collective-permute-start | bytes 688136 | tf_op jit(solution)/shard_map/ppermute | solution.py:87
  9.0 8.1 %collective-permute-start.1 = (bf16[64,1792]{1,0:T(8,128)(2,1)S(1)}, bf16[64,1792]{1,0:T(8,128)(2,1)S(1)}, u32[]{:S(2)}, u32[]{:S(2)}) collective-permute-start(bf16[64,1792]{1,0:T(8,128)(2,1)S(1)} %pad_maximum_fusion.2.refs_0_), channel_id=1, source_target_pairs={{0,32},{16,48},{32,64},{48,80},{64,96},{80,112},{96,128},{112,144}... | collective-permute-start | bytes 688136 | tf_op jit(solution)/shard_map/ppermute | solution.py:91
  9.0 8.1 %collective-permute-start.2 = (bf16[64,1792]{1,0:T(8,128)(2,1)S(1)}, bf16[64,1792]{1,0:T(8,128)(2,1)S(1)}, u32[]{:S(2)}, u32[]{:S(2)}) collective-permute-start(bf16[64,1792]{1,0:T(8,128)(2,1)S(1)} %pad_maximum_fusion.2.refs_0_), channel_id=1, source_target_pairs={{0,16},{16,0},{32,48},{48,32},{64,80},{80,64},{96,112},{112,96},{1... | collective-permute-start | bytes 688136 | tf_op jit(solution)/shard_map/ppermute | solution.py:95
  10.3 9.8 %collective-permute-start.6 = (bf16[64,256]{1,0:T(8,128)(2,1)S(1)}, bf16[64,256]{1,0:T(8,128)(2,1)S(1)}, u32[]{:S(2)}, u32[]{:S(2)}) collective-permute-start(bf16[64,256]{1,0:T(8,128)(2,1)S(1)} %pad_maximum_fusion.5), channel_id=1, source_target_pairs={{0,0},{1,16},{2,32},{3,48},{4,64},{5,80},{6,96},{7,112},{8,128},{9... | collective-permute-start | bytes 98312 | tf_op jit(solution)/shard_map/ppermute | solution.py:286
  17.1 7.2 %collective-permute-start.3 = (bf16[64,1792]{1,0:T(8,128)(2,1)S(1)}, bf16[64,1792]{1,0:T(8,128)(2,1)S(1)}, u32[]{:S(2)}, u32[]{:S(2)}) collective-permute-start(bf16[64,1792]{1,0:T(8,128)(2,1)S(1)} %get-tuple-element.34.refs_0_), channel_id=1, source_target_pairs={{0,224},{16,240},{32,0},{48,16},{64,32},{80,48},{96,64},{112,80},{... | collective-permute-start | bytes 688136 | tf_op jit(solution)/shard_map/ppermute | solution.py:87
  19.3 5.7 %collective-permute-start.5 = (bf16[64,1792]{1,0:T(8,128)(2,1)S(1)}, bf16[64,1792]{1,0:T(8,128)(2,1)S(1)}, u32[]{:S(2)}, u32[]{:S(2)}) collective-permute-start(bf16[64,1792]{1,0:T(8,128)(2,1)S(1)} %get-tuple-element.34.refs_0_), channel_id=1, source_target_pairs={{0,16},{16,0},{32,48},{48,32},{64,80},{80,64},{96,112},{112,96},{1... | collective-permute-start | bytes 688136 | tf_op jit(solution)/shard_map/ppermute | solution.py:95
  19.5 7.0 %collective-permute-start.4 = (bf16[64,1792]{1,0:T(8,128)(2,1)S(1)}, bf16[64,1792]{1,0:T(8,128)(2,1)S(1)}, u32[]{:S(2)}, u32[]{:S(2)}) collective-permute-start(bf16[64,1792]{1,0:T(8,128)(2,1)S(1)} %get-tuple-element.35.refs_1_), channel_id=1, source_target_pairs={{0,32},{16,48},{32,64},{48,80},{64,96},{80,112},{96,128},{112,144}... | collective-permute-start | bytes 688136 | tf_op jit(solution)/shard_map/ppermute | solution.py:91
  27.5 24.2 %all-to-all-start = ((bf16[16,64,256]{2,1,0:T(8,128)(2,1)}), bf16[16,64,256]{2,1,0:T(8,128)(2,1)S(1)}, u32[]{:S(2)}, u32[]{:S(2)}) async-start(bf16[16,64,256]{2,1,0:T(8,128)(2,1)} %tile.6), calls=%async_computation | async-start | bytes 1048576 | tf_op jit(solution)/shard_map/all_to_all | solution.py:63
  36.8 11.2 %collective-permute-start.10 = (bf16[64,1792]{1,0:T(8,128)(2,1)S(1)}, bf16[64,1792]{1,0:T(8,128)(2,1)S(1)}, u32[]{:S(2)}, u32[]{:S(2)}) collective-permute-start(bf16[64,1792]{1,0:T(8,128)(2,1)S(1)} %get-tuple-element.37.refs_3_), channel_id=1, source_target_pairs={{0,16},{16,0},{32,48},{48,32},{64,80},{80,64},{96,112},{112,96},{1... | collective-permute-start | bytes 688136 | tf_op jit(solution)/shard_map/ppermute | solution.py:95
  36.8 11.2 %collective-permute-start.8 = (bf16[64,1792]{1,0:T(8,128)(2,1)S(1)}, bf16[64,1792]{1,0:T(8,128)(2,1)S(1)}, u32[]{:S(2)}, u32[]{:S(2)}) collective-permute-start(bf16[64,1792]{1,0:T(8,128)(2,1)S(1)} %get-tuple-element.38.refs_0_), channel_id=1, source_target_pairs={{0,224},{16,240},{32,0},{48,16},{64,32},{80,48},{96,64},{112,80},{... | collective-permute-start | bytes 688136 | tf_op jit(solution)/shard_map/ppermute | solution.py:87
  36.9 11.1 %collective-permute-start.9 = (bf16[64,1792]{1,0:T(8,128)(2,1)S(1)}, bf16[64,1792]{1,0:T(8,128)(2,1)S(1)}, u32[]{:S(2)}, u32[]{:S(2)}) collective-permute-start(bf16[64,1792]{1,0:T(8,128)(2,1)S(1)} %get-tuple-element.39.refs_1_), channel_id=1, source_target_pairs={{0,32},{16,48},{32,64},{48,80},{64,96},{80,112},{96,128},{112,144}... | collective-permute-start | bytes 688136 | tf_op jit(solution)/shard_map/ppermute | solution.py:91
  48.1 6.2 %collective-permute-start.11 = (bf16[64,1792]{1,0:T(8,128)(2,1)S(1)}, bf16[64,1792]{1,0:T(8,128)(2,1)S(1)}, u32[]{:S(2)}, u32[]{:S(2)}) collective-permute-start(bf16[64,1792]{1,0:T(8,128)(2,1)S(1)} %get-tuple-element.41.refs_4_), channel_id=1, source_target_pairs={{0,224},{16,240},{32,0},{48,16},{64,32},{80,48},{96,64},{112,80},{... | collective-permute-start | bytes 688136 | tf_op jit(solution)/shard_map/ppermute | solution.py:87
  48.2 7.4 %collective-permute-start.12 = (bf16[64,1792]{1,0:T(8,128)(2,1)S(1)}, bf16[64,1792]{1,0:T(8,128)(2,1)S(1)}, u32[]{:S(2)}, u32[]{:S(2)}) collective-permute-start(bf16[64,1792]{1,0:T(8,128)(2,1)S(1)} %get-tuple-element.42.refs_5_), channel_id=1, source_target_pairs={{0,32},{16,48},{32,64},{48,80},{64,96},{80,112},{96,128},{112,144}... | collective-permute-start | bytes 688136 | tf_op jit(solution)/shard_map/ppermute | solution.py:91
  49.7 10.9 %collective-permute-start.13 = (bf16[64,1792]{1,0:T(8,128)(2,1)S(1)}, bf16[64,1792]{1,0:T(8,128)(2,1)S(1)}, u32[]{:S(2)}, u32[]{:S(2)}) collective-permute-start(bf16[64,1792]{1,0:T(8,128)(2,1)S(1)} %get-tuple-element.46.refs_1_), channel_id=1, source_target_pairs={{0,32},{16,48},{32,64},{48,80},{64,96},{80,112},{96,128},{112,144}... | collective-permute-start | bytes 688136 | tf_op jit(solution)/shard_map/ppermute | solution.py:91
  49.7 10.8 %collective-permute-start.14 = (bf16[64,1792]{1,0:T(8,128)(2,1)S(1)}, bf16[64,1792]{1,0:T(8,128)(2,1)S(1)}, u32[]{:S(2)}, u32[]{:S(2)}) collective-permute-start(bf16[64,1792]{1,0:T(8,128)(2,1)S(1)} %get-tuple-element.45.refs_0_), channel_id=1, source_target_pairs={{0,16},{16,0},{32,48},{48,32},{64,80},{80,64},{96,112},{112,96},{1... | collective-permute-start | bytes 688136 | tf_op jit(solution)/shard_map/ppermute | solution.py:95
  60.6 12.8 %collective-permute-start.18 = (bf16[512,256]{1,0:T(8,128)(2,1)S(1)}, bf16[512,256]{1,0:T(8,128)(2,1)S(1)}, u32[]{:S(2)}, u32[]{:S(2)}) collective-permute-start(bf16[512,256]{1,0:T(8,128)(2,1)S(1)} %get-tuple-element.56), channel_id=1, source_target_pairs={{0,16},{16,0},{32,48},{48,32},{64,80},{80,64},{96,112},{112,96},{1... | collective-permute-start | bytes 786440 | tf_op jit(solution)/shard_map/ppermute | solution.py:318
  63.1 17.2 %collective-permute-start.17 = (bf16[64,1792]{1,0:T(8,128)(2,1)S(1)}, bf16[64,1792]{1,0:T(8,128)(2,1)S(1)}, u32[]{:S(2)}, u32[]{:S(2)}) collective-permute-start(bf16[64,1792]{1,0:T(8,128)(2,1)S(1)} %get-tuple-element.48.refs_9_.refs_4_), channel_id=1, source_target_pairs={{0,224},{16,240},{32,0},{48,16},{64,32},{80,48},{96,64},{112,80},{... | collective-permute-start | bytes 688136 | tf_op jit(solution)/shard_map/ppermute | solution.py:87
  71.4 18.9 %collective-permute-start.15 = (bf16[512,896]{1,0:T(8,128)(2,1)}, bf16[512,896]{1,0:T(8,128)(2,1)S(1)}, u32[]{:S(2)}, u32[]{:S(2)}) collective-permute-start(bf16[512,896]{1,0:T(8,128)(2,1)} %get-tuple-element.50), channel_id=1, source_target_pairs={{0,1},{1,0},{2,3},{3,2},{4,5},{5,4},{6,7},{7,6},{8,9},{9,8},{10,11... | collective-permute-start | bytes 2752520 | tf_op jit(solution)/shard_map/ppermute | solution.py:328
  73.2 7.2 %collective-permute-start.16 = (bf16[64,1792]{1,0:T(8,128)(2,1)S(1)}, bf16[64,1792]{1,0:T(8,128)(2,1)S(1)}, u32[]{:S(2)}, u32[]{:S(2)}) collective-permute-start(bf16[64,1792]{1,0:T(8,128)(2,1)S(1)} %get-tuple-element.54.refs_3_), channel_id=1, source_target_pairs={{0,16},{16,0},{32,48},{48,32},{64,80},{80,64},{96,112},{112,96},{1... | collective-permute-start | bytes 688136 | tf_op jit(solution)/shard_map/ppermute | solution.py:95
  89.4 3.2 %collective-permute-start.19 = (bf16[512,896]{1,0:T(8,128)(2,1)}, bf16[512,896]{1,0:T(8,128)(2,1)S(1)}, u32[]{:S(2)}, u32[]{:S(2)}) collective-permute-start(bf16[512,896]{1,0:T(8,128)(2,1)} %get-tuple-element.58), channel_id=1, source_target_pairs={{0,1},{1,0},{2,3},{3,2},{4,5},{5,4},{6,7},{7,6},{8,9},{9,8},{10,11... | collective-permute-start | bytes 2752520 | tf_op jit(solution)/shard_map/ppermute | solution.py:328
  94.1 33.7 %all-to-all-start.1 = ((bf16[8,128,896]{2,1,0:T(8,128)(2,1)}), bf16[8,128,896]{2,1,0:T(8,128)(2,1)S(1)}, u32[]{:S(2)}, u32[]{:S(2)}) async-start(bf16[8,128,896]{2,1,0:T(8,128)(2,1)} %bitcast.16), calls=%async_computation.1 | async-start | bytes 3670016 | tf_op jit(solution)/shard_map/all_to_all | solution.py:63
  100.7 7.9 %collective-permute-start.20 = (f32[256,256]{1,0:T(8,128)S(1)}, f32[256,256]{1,0:T(8,128)S(1)}, u32[]{:S(2)}, u32[]{:S(2)}) collective-permute-start(f32[256,256]{1,0:T(8,128)S(1)} %constant_dynamic-slice_fusion.2), channel_id=1, source_target_pairs={{0,32},{16,48},{32,0},{48,16},{64,96},{80,112},{96,64},{112,80},{1... | collective-permute-start | bytes 786440 | tf_op jit(solution)/shard_map/ppermute | solution.py:322
  108.6 8.3 %collective-permute-start.21 = (f32[128,256]{1,0:T(8,128)S(1)}, f32[128,256]{1,0:T(8,128)S(1)}, u32[]{:S(2)}, u32[]{:S(2)}) collective-permute-start(f32[128,256]{1,0:T(8,128)S(1)} %constant_dynamic-slice_fusion.1), channel_id=1, source_target_pairs={{0,64},{16,80},{32,96},{48,112},{64,0},{80,16},{96,32},{112,48},{1... | collective-permute-start | bytes 393224 | tf_op jit(solution)/shard_map/ppermute | solution.py:322
  117.0 16.0 %collective-permute-start.22 = (f32[64,256]{1,0:T(8,128)S(1)}, f32[64,256]{1,0:T(8,128)S(1)}, u32[]{:S(2)}, u32[]{:S(2)}) collective-permute-start(f32[64,256]{1,0:T(8,128)S(1)} %constant_dynamic-slice_fusion), channel_id=1, source_target_pairs={{0,128},{16,144},{32,160},{48,176},{64,192},{80,208},{96,224},{112... | collective-permute-start | bytes 196616 | tf_op jit(solution)/shard_map/ppermute | solution.py:322
  129.3 33.5 %all-to-all-start.2 = ((bf16[8,128,896]{2,1,0:T(8,128)(2,1)}), bf16[8,128,896]{2,1,0:T(8,128)(2,1)S(1)}, u32[]{:S(2)}, u32[]{:S(2)}) async-start(bf16[8,128,896]{2,1,0:T(8,128)(2,1)} %bitcast.15), calls=%async_computation.2 | async-start | bytes 3670016 | tf_op jit(solution)/shard_map/all_to_all | solution.py:63
  133.0 6.8 %collective-permute-start.23 = (bf16[64,256]{1,0:T(8,128)(2,1)S(1)}, bf16[64,256]{1,0:T(8,128)(2,1)S(1)}, u32[]{:S(2)}, u32[]{:S(2)}) collective-permute-start(bf16[64,256]{1,0:T(8,128)(2,1)S(1)} %get-tuple-element.60), channel_id=1, source_target_pairs={{0,128},{16,144},{32,160},{48,176},{64,192},{80,208},{96,224},{112... | collective-permute-start | bytes 98312 | tf_op jit(solution)/shard_map/ppermute | solution.py:336
  139.8 4.4 %collective-permute-start.24 = (bf16[128,256]{1,0:T(8,128)(2,1)S(1)}, bf16[128,256]{1,0:T(8,128)(2,1)S(1)}, u32[]{:S(2)}, u32[]{:S(2)}) collective-permute-start(bf16[128,256]{1,0:T(8,128)(2,1)S(1)} %pad_maximum_fusion.4), channel_id=1, source_target_pairs={{0,64},{16,80},{32,96},{48,112},{64,0},{80,16},{96,32},{112,48},{1... | collective-permute-start | bytes 196616 | tf_op jit(solution)/shard_map/ppermute | solution.py:336
  144.2 4.4 %collective-permute-start.25 = (bf16[256,256]{1,0:T(8,128)(2,1)S(1)}, bf16[256,256]{1,0:T(8,128)(2,1)S(1)}, u32[]{:S(2)}, u32[]{:S(2)}) collective-permute-start(bf16[256,256]{1,0:T(8,128)(2,1)S(1)} %pad_maximum_fusion.3), channel_id=1, source_target_pairs={{0,32},{16,48},{32,0},{48,16},{64,96},{80,112},{96,64},{112,80},{1... | collective-permute-start | bytes 393224 | tf_op jit(solution)/shard_map/ppermute | solution.py:336
  148.6 10.1 %collective-permute-start.26 = (bf16[512,256]{1,0:T(8,128)(2,1)S(1)}, bf16[512,256]{1,0:T(8,128)(2,1)S(1)}, u32[]{:S(2)}, u32[]{:S(2)}) collective-permute-start(bf16[512,256]{1,0:T(8,128)(2,1)S(1)} %pad_maximum_fusion.1), channel_id=1, source_target_pairs={{0,16},{16,0},{32,48},{48,32},{64,80},{80,64},{96,112},{112,96},{1... | collective-permute-start | bytes 786440 | tf_op jit(solution)/shard_map/ppermute | solution.py:336
  158.7 4.1 %collective-permute-start.27 = (bf16[1024,256]{1,0:T(8,128)(2,1)S(1)}, bf16[1024,256]{1,0:T(8,128)(2,1)S(1)}, u32[]{:S(2)}, u32[]{:S(2)}) collective-permute-start(bf16[1024,256]{1,0:T(8,128)(2,1)S(1)} %constant_dynamic-update-slice_fusion.own_acts_ref), channel_id=1, source_target_pairs={{0,1},{1,0},{2,3},{3,2},{4,5},{5,4},{6,7},{7,6},{8,9},{9,8},{10,11... | collective-permute-start | bytes 1572872 | tf_op jit(solution)/shard_map/ppermute | solution.py:337
  (31 other events, 324.2 us)

commit v6 on v3

--- a/solution.py
+++ b/solution.py
@@ -71,16 +71,16 @@
     del refs
 
 
-def fence(*arrays):
+def fence(*arrays, needs=()):
     anywhere = pl.BlockSpec(memory_space=pl.ANY)
     return pl.pallas_call(
         fence_kernel,
         out_shape=[jax.ShapeDtypeStruct(a.shape, a.dtype) for a in arrays],
-        in_specs=[anywhere] * len(arrays),
+        in_specs=[anywhere] * (len(arrays) + len(needs)),
         out_specs=[anywhere] * len(arrays),
         input_output_aliases={i: i for i in range(len(arrays))},
         compiler_params=pltpu.CompilerParams(vmem_limit_bytes=1024 * 1024),
-    )(*arrays)
+    )(*arrays, *needs)
 
 
 def up(x):
@@ -145,6 +145,58 @@
             transcendentals=0,
         ),
     )(core.reshape(1), *blocks, basis, *needs)
+
+
+def side_kernel(count, side_ref, *refs):
+    del side_ref
+    blocks, basis_ref = refs[:count], refs[count]
+    out_ref, tokens, total = refs[-3:]
+    rows = blocks[0].shape[0]
+    depth = basis_ref.shape[0]
+    step = pl.program_id(0)
+
+    @pl.when(step == 0)
+    def _():
+        for r, ref in enumerate(blocks):
+            tokens[r * rows : (r + 1) * rows, :] = ref[...]
+        total[...] = jnp.dot(
+            tokens[:, :depth], basis_ref[...], preferred_element_type=jnp.float32
+        )
+
+    @pl.when(step == 1)
+    def _():
+        out_ref[...] = (
+            total[...]
+            + jnp.dot(tokens[:, depth:], basis_ref[...], preferred_element_type=jnp.float32)
+        ).astype(out_ref.dtype)
+
+
+def turn_side(side, blocks, basis, kind, needs=()):
+    rows, features = blocks[0].shape
+    units = basis.shape[1] // 2
+    tokens = rows * len(blocks)
+    return pl.pallas_call(
+        functools.partial(side_kernel, len(blocks)),
+        grid_spec=pltpu.PrefetchScalarGridSpec(
+            num_scalar_prefetch=1,
+            grid=(2,),
+            in_specs=[pl.BlockSpec((rows, features), lambda i, side_ref: (0, 0))] * len(blocks)
+            + [pl.BlockSpec((features // 2, units), lambda i, side_ref: (i, side_ref[0]))]
+            + [pl.BlockSpec(memory_space=pl.ANY)] * len(needs),
+            out_specs=pl.BlockSpec((tokens, units), lambda i, side_ref: (0, 0)),
+            scratch_shapes=[
+                pltpu.VMEM((tokens, features), jnp.bfloat16),
+                pltpu.VMEM((tokens, units), jnp.float32),
+            ],
+        ),
+        out_shape=jax.ShapeDtypeStruct((tokens, units), kind),
+        compiler_params=pltpu.CompilerParams(vmem_limit_bytes=56 * 1024 * 1024),
+        cost_estimate=pl.CostEstimate(
+            flops=2 * tokens * features * units,
+            bytes_accessed=2 * tokens * (features + 2 * units) + 2 * features * units,
+            transcendentals=0,
+        ),
+    )(side.reshape(1), *blocks, basis, *needs)
 
 
 def after(x, y):
@@ -294,7 +346,7 @@
     (held[(2, 0)], held[(-2, 0)], held[(3, 0)], held[(-3, 0)], held[(1, 1)], held[(-1, 1)],
      moved) = fence(
         held[(2, 0)], held[(-2, 0)], up(held[(2, 0)]), down(held[(-2, 0)]), held[(1, 1)],
-        over(held[(-1, 0)]), moved,
+        over(held[(-1, 0)]), moved, needs=(own_inv, sib_inv),
     )
     every_acts = share(moved, GROUPS, "mp")
     held[(3, 0)], held[(-3, 0)], held[(2, 1)], held[(-2, 1)], held[(4, 0)], held[(3, 1)] = fence(
@@ -316,14 +368,15 @@
         sums.append(summed)
     own_acts = summed.astype(jnp.bfloat16)
 
-    pairs = []
-    for chunk, needs in zip(CHUNKS, ((held[(3, 1)],), (own_inv, sib_inv, first))):
-        sib_part, own_part = turn(core, [held[place] for place in chunk], basis_out, needs)
-        got = lax.ppermute(sib_part, "mp", CORE_SWAP).astype(jnp.float32)
-        if pairs:
-            got = after(got, sums[0])
-        pairs.append((own_part + got).astype(jnp.bfloat16))
-    pairs = jnp.concatenate(pairs, 0)
+    early, late = ([held[place] for place in chunk] for chunk in CHUNKS)
+    sib_part, own_part = turn(core, early, basis_out, (held[(3, 1)],))
+    got = lax.ppermute(sib_part, "mp", CORE_SWAP).astype(jnp.float32)
+    early = (own_part + got).astype(jnp.bfloat16)
+    sib_part = turn_side(1 - core, late, basis_out, jnp.bfloat16)
+    got = lax.ppermute(sib_part, "mp", CORE_SWAP).astype(jnp.float32)
+    own_part = turn_side(core, late, basis_out, jnp.float32, (first,))
+    late = (own_part + after(got, sums[0])).astype(jnp.bfloat16)
+    pairs = jnp.concatenate([early, late], 0)
     parts = exchange(pairs, "mp", axis_index_groups=SAME_CORE)
     copies = sum_and_copy(parts)
 

time: 206 us -> 200 us (0.971)
  waiting for transfers between devices: 63.7 us -> 52.2 us
  starting transfers between devices: 61.9 us -> 66.8 us
  other arithmetic: 12.4 us -> 8.74 us
  Pallas kernels: 34.2 us -> 37.2 us
    pallas_call x0 -> x2, Pallas kernels: none -> 11.2 us  [turn_side(): pl.pallas_call(functools.partial(side_kernel, len(blocks)), grid_spec=plt...]
    ppermute x4, waiting for transfers between devices: 21.1 us -> 12 us  [shards(): summed = mine + lax.ppermute(away, 'dp', swap).astype(jnp.float32)]
    ppermute x4, starting transfers between devices: 1.92 us -> 10.6 us  [shards(): lax.ppermute(own_acts, 'dp', swap)]
    pallas_call x2 -> x1, Pallas kernels: 16.4 us -> 8.16 us  [turn(): pl.pallas_call(functools.partial(turn_kernel, len(blocks)), grid_spec=plt...]
    ppermute x4, waiting for transfers between devices: 23 us -> 15.2 us  [shards(): lax.ppermute(own_acts, 'dp', swap)]
    ppermute x4, starting transfers between devices: 0.97 us -> 8.3 us  [shards(): summed = mine + lax.ppermute(away, 'dp', swap).astype(jnp.float32)]
    ppermute x5, waiting for transfers between devices: 0.01 us -> 7.31 us  [up(): return lax.ppermute(x, 'dp', dp_shift(-1, 0))]
    all_to_all x3, starting transfers between devices: 23.3 us -> 16.9 us  [exchange(): return lax.all_to_all(x, axis, 0, 0, tiled=True, **kw)]
  transfers between devices with their start and end apart: 31 -> 31, of which waited for: 12 -> 15; matrix products, arithmetic and copies ran while one was open for 6% -> 3% of each run, Pallas kernels for 8% -> 10%
where the time goes in v6:
time: 200 us
  starting transfers between devices  66.8 us (33%)
  waiting for transfers between devices  52.2 us (26%)
  Pallas kernels  37.2 us (19%)
  blocking collectives  27.5 us (14%)
  other arithmetic  8.74 us (4%)
  local copies, waits for them, and re-layouts  5.29 us (3%)
    all_to_all x2, blocking collectives, exchange(): return lax.all_to_all(x, axis, 0, 0, tiled=True, **kw)  27.5 us
    pallas_call x1, Pallas kernels, score_blocks(): pl.pallas_call(score_kernel, out_shape=jax.ShapeDtypeStruct((GROUPS, 128)...  17.5 us
    all_to_all x3, starting transfers between devices, exchange(): return lax.all_to_all(x, axis, 0, 0, tiled=True, **kw)  16.9 us
    ppermute x4, waiting for transfers between devices, shards(): lax.ppermute(own_acts, 'dp', swap)  15.2 us
    ppermute x4, waiting for transfers between devices, shards(): summed = mine + lax.ppermute(away, 'dp', swap).astype(jnp.float32)  12 us
    ppermute x5, starting transfers between devices, up(): return lax.ppermute(x, 'dp', dp_shift(-1, 0))  11.7 us
    pallas_call x2, Pallas kernels, turn_side(): pl.pallas_call(functools.partial(side_kernel, len(blocks)), grid_spec=plt...  11.2 us
    ppermute x4, starting transfers between devices, shards(): lax.ppermute(own_acts, 'dp', swap)  10.6 us
  transfers between devices with their start and end apart: 31, of which 15 were waited for; matrix products, arithmetic and copies ran while one was open for 3% of the time, Pallas kernels for 10%

profile of v6, /device:TPU:1, one launch (start us, length us, event | category | flops | bytes accessed | tf_op | source)
XLA Modules:
  0.0 199.8 jit_solution(106399158482990417)
XLA Ops:
  0.0 1.7 constant_dynamic-slice_fusion.3
  1.7 3.3 %collective-permute-start.10 = (f32[896,256]{1,0:T(8,128)S(1)}, f32[896,256]{1,0:T(8,128)S(1)}, u32[]{:S(2)}, u32[]{:S(2)}) collective-permute-start(f32[896,256]{1,0:T(8,128)S(1)} %get-tuple-element.57), channel_id=1, source_target_pairs={{0,1},{1,0},{2,3},{3,2},{4,5},{5,4},{6,7},{7,6},{8,9},{9,8},{10,11... | collective-permute-start | bytes 2752520 | tf_op jit(solution)/shard_map/ppermute | solution.py:332
  5.0 3.9 %collective-permute-start = (bf16[64,1792]{1,0:T(8,128)(2,1)S(1)}, bf16[64,1792]{1,0:T(8,128)(2,1)S(1)}, u32[]{:S(2)}, u32[]{:S(2)}) collective-permute-start(bf16[64,1792]{1,0:T(8,128)(2,1)S(1)} %pad_maximum_fusion.2.refs_0_), channel_id=1, source_target_pairs={{0,224},{16,240},{32,0},{48,16},{64,32},{80,48},{96,64},{112,80},{... | collective-permute-start | bytes 688136 | tf_op jit(solution)/shard_map/ppermute | solution.py:87
  10.3 3.7 %collective-permute-done.refs_1_ = bf16[64,1792]{1,0:T(8,128)(2,1)S(1)} collective-permute-done((bf16[64,1792]{1,0:T(8,128)(2,1)S(1)}, bf16[64,1792]{1,0:T(8,128)(2,1)S(1)}, u32[]{:S(2)}, u32[]{:S(2)}) %collective-permute-start) | collective-permute-done | bytes 229408 | tf_op jit(solution)/shard_map/ppermute | solution.py:87
  14.0 3.1 %collective-permute-done.1.refs_2_ = bf16[64,1792]{1,0:T(8,128)(2,1)S(1)} collective-permute-done((bf16[64,1792]{1,0:T(8,128)(2,1)S(1)}, bf16[64,1792]{1,0:T(8,128)(2,1)S(1)}, u32[]{:S(2)}, u32[]{:S(2)}) %collective-permute-start.1) | collective-permute-done | bytes 229408 | tf_op jit(solution)/shard_map/ppermute | solution.py:91
  19.9 3.9 %collective-permute-start.9 = (bf16[64,256]{1,0:T(8,128)(2,1)S(1)}, bf16[64,256]{1,0:T(8,128)(2,1)S(1)}, u32[]{:S(2)}, u32[]{:S(2)}) collective-permute-start(bf16[64,256]{1,0:T(8,128)(2,1)S(1)} %pad_maximum_fusion.5), channel_id=1, source_target_pairs={{0,0},{1,16},{2,32},{3,48},{4,64},{5,80},{6,96},{7,112},{8,128},{9... | collective-permute-start | bytes 98312 | tf_op jit(solution)/shard_map/ppermute | solution.py:338
  23.9 1.7 collective-permute-done.4.refs_3_
  26.3 4.6 %collective-permute-start.6 = (bf16[64,1792]{1,0:T(8,128)(2,1)S(1)}, bf16[64,1792]{1,0:T(8,128)(2,1)S(1)}, u32[]{:S(2)}, u32[]{:S(2)}) collective-permute-start(bf16[64,1792]{1,0:T(8,128)(2,1)S(1)} %get-tuple-element.35.refs_0_), channel_id=1, source_target_pairs={{0,224},{16,240},{32,0},{48,16},{64,32},{80,48},{96,64},{112,80},{... | collective-permute-start | bytes 688136 | tf_op jit(solution)/shard_map/ppermute | solution.py:87
  31.1 3.6 %collective-permute-done.6.refs_2_ = bf16[64,1792]{1,0:T(8,128)(2,1)S(1)} collective-permute-done((bf16[64,1792]{1,0:T(8,128)(2,1)S(1)}, bf16[64,1792]{1,0:T(8,128)(2,1)S(1)}, u32[]{:S(2)}, u32[]{:S(2)}) %collective-permute-start.6) | collective-permute-done | bytes 229408 | tf_op jit(solution)/shard_map/ppermute | solution.py:87
  34.7 3.8 %collective-permute-done.7.refs_3_ = bf16[64,1792]{1,0:T(8,128)(2,1)S(1)} collective-permute-done((bf16[64,1792]{1,0:T(8,128)(2,1)S(1)}, bf16[64,1792]{1,0:T(8,128)(2,1)S(1)}, u32[]{:S(2)}, u32[]{:S(2)}) %collective-permute-start.7) | collective-permute-done | bytes 229408 | tf_op jit(solution)/shard_map/ppermute | solution.py:91
  41.0 7.3 %all-to-all-start = ((bf16[16,64,256]{2,1,0:T(8,128)(2,1)}), bf16[16,64,256]{2,1,0:T(8,128)(2,1)S(1)}, u32[]{:S(2)}, u32[]{:S(2)}) async-start(bf16[16,64,256]{2,1,0:T(8,128)(2,1)} %tile.6), calls=%async_computation | async-start | bytes 1048576 | tf_op jit(solution)/shard_map/all_to_all | solution.py:63
  51.9 8.2 %shard_map.95 = (bf16[512,896]{1,0:T(8,128)(2,1)}, f32[512,896]{1,0:T(8,128)}) custom-call(s32[1]{0:T(128)} %bitcast.core_ref.side_ref, bf16[64,1792]{1,0:T(8,128)(2,1)} %copy-done.13, bf16[64,1792]{1,0:T(8,128)(2,1)} %copy-done.16, bf16[64,1792]{1,0:T(8,128)(2,1)} %copy-done.14, bf16[64,1792]{1,0:T(8,128)(2,1)} %copy-done.15, bf16[64,1792]{1,0:T(8,128)(2,1)} %copy-done.11, ...), custom_call_target="tpu_custom_call" | custom-call | flops 3288334336 | bytes 11010048 | tf_op jit(solution)/shard_map/pallas_call | solution.py:126
  60.1 2.6 %collective-permute-start.15 = (bf16[512,896]{1,0:T(8,128)(2,1)}, bf16[512,896]{1,0:T(8,128)(2,1)}, u32[]{:S(2)}, u32[]{:S(2)}) collective-permute-start(bf16[512,896]{1,0:T(8,128)(2,1)} %get-tuple-element.46), channel_id=1, source_target_pairs={{0,1},{1,0},{2,3},{3,2},{4,5},{5,4},{6,7},{7,6},{8,9},{9,8},{10,11... | collective-permute-start | bytes 2752520 | tf_op jit(solution)/shard_map/ppermute | solution.py:373
  63.4 5.4 %shard_map.97 = bf16[512,896]{1,0:T(8,128)(2,1)} custom-call(s32[1]{0:T(128)} %bitcast.6.side_ref, bf16[64,1792]{1,0:T(8,128)(2,1)} %copy-done.6, bf16[64,1792]{1,0:T(8,128)(2,1)} %copy-done.7, bf16[64,1792]{1,0:T(8,128)(2,1)} %copy-done.4, bf16[64,1792]{1,0:T(8,128)(2,1)} %copy-done.5, bf16[64,1792]{1,0:T(8,128)(2,1)} %copy-done.9, ...), custom_call_target="tpu_custom_call" | custom-call | flops 1644167168 | bytes 6881280 | tf_op jit(solution)/shard_map/pallas_call | solution.py:178
  70.5 5.8 %shard_map.96 = f32[512,896]{1,0:T(8,128)} custom-call(s32[1]{0:T(128)} %bitcast.core_ref.side_ref, bf16[64,1792]{1,0:T(8,128)(2,1)} %copy-done.6, bf16[64,1792]{1,0:T(8,128)(2,1)} %copy-done.7, bf16[64,1792]{1,0:T(8,128)(2,1)} %copy-done.4, bf16[64,1792]{1,0:T(8,128)(2,1)} %copy-done.5, bf16[64,1792]{1,0:T(8,128)(2,1)} %copy-done.9, ...), custom_call_target="tpu_custom_call" | custom-call | flops 1644167168 | bytes 6881280 | tf_op jit(solution)/shard_map/pallas_call | solution.py:178
  82.5 6.0 %all-to-all-start.1 = ((bf16[8,128,896]{2,1,0:T(8,128)(2,1)}), bf16[8,128,896]{2,1,0:T(8,128)(2,1)S(1)}, u32[]{:S(2)}, u32[]{:S(2)}) async-start(bf16[8,128,896]{2,1,0:T(8,128)(2,1)} %bitcast.18), calls=%async_computation.1 | async-start | bytes 3670016 | tf_op jit(solution)/shard_map/all_to_all | solution.py:63
  88.5 3.1 %collective-permute-start.20 = (f32[256,256]{1,0:T(8,128)S(1)}, f32[256,256]{1,0:T(8,128)S(1)}, u32[]{:S(2)}, u32[]{:S(2)}) collective-permute-start(f32[256,256]{1,0:T(8,128)S(1)} %constant_dynamic-slice_fusion.2), channel_id=1, source_target_pairs={{0,32},{16,48},{32,0},{48,16},{64,96},{80,112},{96,64},{112,80},{1... | collective-permute-start | bytes 786440 | tf_op jit(solution)/shard_map/ppermute | solution.py:367
  91.6 5.6 %collective-permute-done.20 = f32[256,256]{1,0:T(8,128)S(1)} collective-permute-done((f32[256,256]{1,0:T(8,128)S(1)}, f32[256,256]{1,0:T(8,128)S(1)}, u32[]{:S(2)}, u32[]{:S(2)}) %collective-permute-start.20) | collective-permute-done | bytes 262176 | tf_op jit(solution)/shard_map/ppermute | solution.py:367
  97.3 3.8 %collective-permute-start.21 = (f32[128,256]{1,0:T(8,128)S(1)}, f32[128,256]{1,0:T(8,128)S(1)}, u32[]{:S(2)}, u32[]{:S(2)}) collective-permute-start(f32[128,256]{1,0:T(8,128)S(1)} %constant_dynamic-slice_fusion.1), channel_id=1, source_target_pairs={{0,64},{16,80},{32,96},{48,112},{64,0},{80,16},{96,32},{112,48},{1... | collective-permute-start | bytes 393224 | tf_op jit(solution)/shard_map/ppermute | solution.py:367
  101.1 6.0 %collective-permute-done.21 = f32[128,256]{1,0:T(8,128)S(1)} collective-permute-done((f32[128,256]{1,0:T(8,128)S(1)}, f32[128,256]{1,0:T(8,128)S(1)}, u32[]{:S(2)}, u32[]{:S(2)}) %collective-permute-start.21) | collective-permute-done | bytes 131104 | tf_op jit(solution)/shard_map/ppermute | solution.py:367
  107.2 7.3 %all-to-all-done.1 = bf16[8,128,896]{2,1,0:T(8,128)(2,1)S(1)} async-done(((bf16[8,128,896]{2,1,0:T(8,128)(2,1)}), bf16[8,128,896]{2,1,0:T(8,128)(2,1)S(1)}, u32[]{:S(2)}, u32[]{:S(2)}) %all-to-all-start.1) | async-done | bytes 1835040 | tf_op jit(solution)/shard_map/all_to_all | solution.py:63
  116.0 3.6 %all-to-all-start.2 = ((bf16[8,128,896]{2,1,0:T(8,128)(2,1)}), bf16[8,128,896]{2,1,0:T(8,128)(2,1)S(1)}, u32[]{:S(2)}, u32[]{:S(2)}) async-start(bf16[8,128,896]{2,1,0:T(8,128)(2,1)} %bitcast.17), calls=%async_computation.2 | async-start | bytes 3670016 | tf_op jit(solution)/shard_map/all_to_all | solution.py:63
  119.7 4.3 %collective-permute-start.23 = (bf16[64,256]{1,0:T(8,128)(2,1)S(1)}, bf16[64,256]{1,0:T(8,128)(2,1)S(1)}, u32[]{:S(2)}, u32[]{:S(2)}) collective-permute-start(bf16[64,256]{1,0:T(8,128)(2,1)S(1)} %get-tuple-element.54), channel_id=1, source_target_pairs={{0,128},{16,144},{32,160},{48,176},{64,192},{80,208},{96,224},{112... | collective-permute-start | bytes 98312 | tf_op jit(solution)/shard_map/ppermute | solution.py:385
  124.0 2.5 %collective-permute-done.23 = bf16[64,256]{1,0:T(8,128)(2,1)S(1)} collective-permute-done((bf16[64,256]{1,0:T(8,128)(2,1)S(1)}, bf16[64,256]{1,0:T(8,128)(2,1)S(1)}, u32[]{:S(2)}, u32[]{:S(2)}) %collective-permute-start.23) | collective-permute-done | bytes 32800 | tf_op jit(solution)/shard_map/ppermute | solution.py:385
  126.5 6.1 %collective-permute-start.24 = (bf16[128,256]{1,0:T(8,128)(2,1)S(1)}, bf16[128,256]{1,0:T(8,128)(2,1)S(1)}, u32[]{:S(2)}, u32[]{:S(2)}) collective-permute-start(bf16[128,256]{1,0:T(8,128)(2,1)S(1)} %pad_maximum_fusion.4), channel_id=1, source_target_pairs={{0,64},{16,80},{32,96},{48,112},{64,0},{80,16},{96,32},{112,48},{1... | collective-permute-start | bytes 196616 | tf_op jit(solution)/shard_map/ppermute | solution.py:385
  132.6 2.4 %collective-permute-done.24 = bf16[128,256]{1,0:T(8,128)(2,1)S(1)} collective-permute-done((bf16[128,256]{1,0:T(8,128)(2,1)S(1)}, bf16[128,256]{1,0:T(8,128)(2,1)S(1)}, u32[]{:S(2)}, u32[]{:S(2)}) %collective-permute-start.24) | collective-permute-done | bytes 65568 | tf_op jit(solution)/shard_map/ppermute | solution.py:385
  135.1 4.6 %collective-permute-done.25 = bf16[256,256]{1,0:T(8,128)(2,1)S(1)} collective-permute-done((bf16[256,256]{1,0:T(8,128)(2,1)S(1)}, bf16[256,256]{1,0:T(8,128)(2,1)S(1)}, u32[]{:S(2)}, u32[]{:S(2)}) %collective-permute-start.25) | collective-permute-done | bytes 131104 | tf_op jit(solution)/shard_map/ppermute | solution.py:385
  139.8 5.8 %collective-permute-done.26 = bf16[512,256]{1,0:T(8,128)(2,1)S(1)} collective-permute-done((bf16[512,256]{1,0:T(8,128)(2,1)S(1)}, bf16[512,256]{1,0:T(8,128)(2,1)S(1)}, u32[]{:S(2)}, u32[]{:S(2)}) %collective-permute-start.26) | collective-permute-done | bytes 262176 | tf_op jit(solution)/shard_map/ppermute | solution.py:385
  145.6 4.8 %collective-permute-start.27 = (bf16[1024,256]{1,0:T(8,128)(2,1)S(1)}, bf16[1024,256]{1,0:T(8,128)(2,1)S(1)}, u32[]{:S(2)}, u32[]{:S(2)}) collective-permute-start(bf16[1024,256]{1,0:T(8,128)(2,1)S(1)} %constant_dynamic-update-slice_fusion.own_acts_ref), channel_id=1, source_target_pairs={{0,1},{1,0},{2,3},{3,2},{4,5},{5,4},{6,7},{7,6},{8,9},{9,8},{10,11... | collective-permute-start | bytes 1572872 | tf_op jit(solution)/shard_map/ppermute | solution.py:386
  153.4 17.5 %shard_map.99 = f32[16,128]{1,0:T(8,128)} custom-call(s32[16]{0:T(128)} %get-tuple-element.55.acts_at_ref, f32[16,16]{1,0:T(8,128)} %fusion.1.place_ref, bf16[1024,896]{1,0:T(8,128)(2,1)} %bitcast.20, bf16[1024,256]{1,0:T(8,128)(2,1)} %copy-done.27, bf16[1024,256]{1,0:T(8,128)(2,1)} %copy-done.30, f32[896,256]{1,0:T(8,128)} %copy-done.3, f32[896,256]{1,0:T(8,128)} %copy-done.2), custom_call_target="tpu_custom_call" | custom-call | flops 7985954816 | bytes 8388608 | tf_op jit(solution)/shard_map/pallas_call | solution.py:297
  171.6 14.9 %all_to_all.43 = f32[16,16,128]{2,1,0:T(8,128)S(1)} all-to-all(f32[16,16,128]{2,1,0:T(8,128)S(1)} %tile.7), channel_id=1, replica_groups=mesh['dp'=16,'mp'=16] {'mp'}, dimensions={0} | all-to-all | bytes 262144 | tf_op jit(solution)/shard_map/all_to_all | solution.py:63
  186.5 12.6 %all_to_all.44 = f32[16,16,128]{2,1,0:T(8,128)S(1)} all-to-all(f32[16,16,128]{2,1,0:T(8,128)S(1)} %tile.8), channel_id=1, replica_groups=mesh['dp'=16,'mp'=16] {'dp'}, dimensions={0} | all-to-all | bytes 262144 | tf_op jit(solution)/shard_map/all_to_all | solution.py:63
  (136 shorter events, 24.4 us)
Async XLA Ops:
  0.0 68.8 %copy-start = (bf16[256,256]{1,0:T(8,128)(2,1)S(1)}, bf16[256,256]{1,0:T(8,128)(2,1)}, u32[]{:S(2)}) copy-start(bf16[256,256]{1,0:T(8,128)(2,1)} %param.13) | copy-start | bytes 393220
  1.7 29.2 %collective-permute-start.10 = (f32[896,256]{1,0:T(8,128)S(1)}, f32[896,256]{1,0:T(8,128)S(1)}, u32[]{:S(2)}, u32[]{:S(2)}) collective-permute-start(f32[896,256]{1,0:T(8,128)S(1)} %get-tuple-element.57), channel_id=1, source_target_pairs={{0,1},{1,0},{2,3},{3,2},{4,5},{5,4},{6,7},{7,6},{8,9},{9,8},{10,11... | collective-permute-start | bytes 2752520 | tf_op jit(solution)/shard_map/ppermute | solution.py:332
  5.0 8.9 %collective-permute-start = (bf16[64,1792]{1,0:T(8,128)(2,1)S(1)}, bf16[64,1792]{1,0:T(8,128)(2,1)S(1)}, u32[]{:S(2)}, u32[]{:S(2)}) collective-permute-start(bf16[64,1792]{1,0:T(8,128)(2,1)S(1)} %pad_maximum_fusion.2.refs_0_), channel_id=1, source_target_pairs={{0,224},{16,240},{32,0},{48,16},{64,32},{80,48},{96,64},{112,80},{... | collective-permute-start | bytes 688136 | tf_op jit(solution)/shard_map/ppermute | solution.py:87
  9.0 8.1 %collective-permute-start.1 = (bf16[64,1792]{1,0:T(8,128)(2,1)S(1)}, bf16[64,1792]{1,0:T(8,128)(2,1)S(1)}, u32[]{:S(2)}, u32[]{:S(2)}) collective-permute-start(bf16[64,1792]{1,0:T(8,128)(2,1)S(1)} %pad_maximum_fusion.2.refs_0_), channel_id=1, source_target_pairs={{0,32},{16,48},{32,64},{48,80},{64,96},{80,112},{96,128},{112,144}... | collective-permute-start | bytes 688136 | tf_op jit(solution)/shard_map/ppermute | solution.py:91
  9.0 8.1 %collective-permute-start.2 = (bf16[64,1792]{1,0:T(8,128)(2,1)S(1)}, bf16[64,1792]{1,0:T(8,128)(2,1)S(1)}, u32[]{:S(2)}, u32[]{:S(2)}) collective-permute-start(bf16[64,1792]{1,0:T(8,128)(2,1)S(1)} %pad_maximum_fusion.2.refs_0_), channel_id=1, source_target_pairs={{0,16},{16,0},{32,48},{48,32},{64,80},{80,64},{96,112},{112,96},{1... | collective-permute-start | bytes 688136 | tf_op jit(solution)/shard_map/ppermute | solution.py:95
  17.1 6.8 %collective-permute-start.3 = (bf16[64,1792]{1,0:T(8,128)(2,1)S(1)}, bf16[64,1792]{1,0:T(8,128)(2,1)S(1)}, u32[]{:S(2)}, u32[]{:S(2)}) collective-permute-start(bf16[64,1792]{1,0:T(8,128)(2,1)S(1)} %get-tuple-element.31.refs_0_), channel_id=1, source_target_pairs={{0,224},{16,240},{32,0},{48,16},{64,32},{80,48},{96,64},{112,80},{... | collective-permute-start | bytes 688136 | tf_op jit(solution)/shard_map/ppermute | solution.py:87
  18.2 5.7 %collective-permute-start.5 = (bf16[64,1792]{1,0:T(8,128)(2,1)S(1)}, bf16[64,1792]{1,0:T(8,128)(2,1)S(1)}, u32[]{:S(2)}, u32[]{:S(2)}) collective-permute-start(bf16[64,1792]{1,0:T(8,128)(2,1)S(1)} %get-tuple-element.31.refs_0_), channel_id=1, source_target_pairs={{0,16},{16,0},{32,48},{48,32},{64,80},{80,64},{96,112},{112,96},{1... | collective-permute-start | bytes 688136 | tf_op jit(solution)/shard_map/ppermute | solution.py:95
  19.5 6.1 %collective-permute-start.4 = (bf16[64,1792]{1,0:T(8,128)(2,1)S(1)}, bf16[64,1792]{1,0:T(8,128)(2,1)S(1)}, u32[]{:S(2)}, u32[]{:S(2)}) collective-permute-start(bf16[64,1792]{1,0:T(8,128)(2,1)S(1)} %get-tuple-element.32.refs_1_), channel_id=1, source_target_pairs={{0,32},{16,48},{32,64},{48,80},{64,96},{80,112},{96,128},{112,144}... | collective-permute-start | bytes 688136 | tf_op jit(solution)/shard_map/ppermute | solution.py:91
  19.9 11.2 %collective-permute-start.9 = (bf16[64,256]{1,0:T(8,128)(2,1)S(1)}, bf16[64,256]{1,0:T(8,128)(2,1)S(1)}, u32[]{:S(2)}, u32[]{:S(2)}) collective-permute-start(bf16[64,256]{1,0:T(8,128)(2,1)S(1)} %pad_maximum_fusion.5), channel_id=1, source_target_pairs={{0,0},{1,16},{2,32},{3,48},{4,64},{5,80},{6,96},{7,112},{8,128},{9... | collective-permute-start | bytes 98312 | tf_op jit(solution)/shard_map/ppermute | solution.py:338
  26.3 8.4 %collective-permute-start.6 = (bf16[64,1792]{1,0:T(8,128)(2,1)S(1)}, bf16[64,1792]{1,0:T(8,128)(2,1)S(1)}, u32[]{:S(2)}, u32[]{:S(2)}) collective-permute-start(bf16[64,1792]{1,0:T(8,128)(2,1)S(1)} %get-tuple-element.35.refs_0_), channel_id=1, source_target_pairs={{0,224},{16,240},{32,0},{48,16},{64,32},{80,48},{96,64},{112,80},{... | collective-permute-start | bytes 688136 | tf_op jit(solution)/shard_map/ppermute | solution.py:87
  30.9 7.6 %collective-permute-start.7 = (bf16[64,1792]{1,0:T(8,128)(2,1)S(1)}, bf16[64,1792]{1,0:T(8,128)(2,1)S(1)}, u32[]{:S(2)}, u32[]{:S(2)}) collective-permute-start(bf16[64,1792]{1,0:T(8,128)(2,1)S(1)} %get-tuple-element.36.refs_1_), channel_id=1, source_target_pairs={{0,32},{16,48},{32,64},{48,80},{64,96},{80,112},{96,128},{112,144}... | collective-permute-start | bytes 688136 | tf_op jit(solution)/shard_map/ppermute | solution.py:91
  30.9 7.6 %collective-permute-start.8 = (bf16[64,1792]{1,0:T(8,128)(2,1)S(1)}, bf16[64,1792]{1,0:T(8,128)(2,1)}, u32[]{:S(2)}, u32[]{:S(2)}) collective-permute-start(bf16[64,1792]{1,0:T(8,128)(2,1)S(1)} %get-tuple-element.34.refs_3_), channel_id=1, source_target_pairs={{0,16},{16,0},{32,48},{48,32},{64,80},{80,64},{96,112},{112,96},{1... | collective-permute-start | bytes 688136 | tf_op jit(solution)/shard_map/ppermute | solution.py:95
  38.6 9.8 %collective-permute-start.11 = (bf16[64,1792]{1,0:T(8,128)(2,1)S(1)}, bf16[64,1792]{1,0:T(8,128)(2,1)S(1)}, u32[]{:S(2)}, u32[]{:S(2)}) collective-permute-start(bf16[64,1792]{1,0:T(8,128)(2,1)S(1)} %get-tuple-element.38.refs_4_), channel_id=1, source_target_pairs={{0,224},{16,240},{32,0},{48,16},{64,32},{80,48},{96,64},{112,80},{... | collective-permute-start | bytes 688136 | tf_op jit(solution)/shard_map/ppermute | solution.py:87
  39.3 9.1 %collective-permute-start.12 = (bf16[64,1792]{1,0:T(8,128)(2,1)}, bf16[64,1792]{1,0:T(8,128)(2,1)S(1)}, u32[]{:S(2)}, u32[]{:S(2)}) collective-permute-start(bf16[64,1792]{1,0:T(8,128)(2,1)} %get-tuple-element.39.refs_5_), channel_id=1, source_target_pairs={{0,32},{16,48},{32,64},{48,80},{64,96},{80,112},{96,128},{112,144}... | collective-permute-start | bytes 688136 | tf_op jit(solution)/shard_map/ppermute | solution.py:91
  40.1 9.7 %collective-permute-start.13 = (bf16[64,1792]{1,0:T(8,128)(2,1)S(1)}, bf16[64,1792]{1,0:T(8,128)(2,1)S(1)}, u32[]{:S(2)}, u32[]{:S(2)}) collective-permute-start(bf16[64,1792]{1,0:T(8,128)(2,1)S(1)} %get-tuple-element.43.refs_1_), channel_id=1, source_target_pairs={{0,32},{16,48},{32,64},{48,80},{64,96},{80,112},{96,128},{112,144}... | collective-permute-start | bytes 688136 | tf_op jit(solution)/shard_map/ppermute | solution.py:91
  40.2 9.7 %collective-permute-start.14 = (bf16[64,1792]{1,0:T(8,128)(2,1)S(1)}, bf16[64,1792]{1,0:T(8,128)(2,1)S(1)}, u32[]{:S(2)}, u32[]{:S(2)}) collective-permute-start(bf16[64,1792]{1,0:T(8,128)(2,1)S(1)} %get-tuple-element.42.refs_0_), channel_id=1, source_target_pairs={{0,16},{16,0},{32,48},{48,32},{64,80},{80,64},{96,112},{112,96},{1... | collective-permute-start | bytes 688136 | tf_op jit(solution)/shard_map/ppermute | solution.py:95
  41.0 27.8 %all-to-all-start = ((bf16[16,64,256]{2,1,0:T(8,128)(2,1)}), bf16[16,64,256]{2,1,0:T(8,128)(2,1)S(1)}, u32[]{:S(2)}, u32[]{:S(2)}) async-start(bf16[16,64,256]{2,1,0:T(8,128)(2,1)} %tile.6), calls=%async_computation | async-start | bytes 1048576 | tf_op jit(solution)/shard_map/all_to_all | solution.py:63
  49.9 12.8 %collective-permute-start.16 = (bf16[64,1792]{1,0:T(8,128)(2,1)S(1)}, bf16[64,1792]{1,0:T(8,128)(2,1)S(1)}, u32[]{:S(2)}, u32[]{:S(2)}) collective-permute-start(bf16[64,1792]{1,0:T(8,128)(2,1)S(1)} %get-tuple-element.50.refs_3_), channel_id=1, source_target_pairs={{0,16},{16,0},{32,48},{48,32},{64,80},{80,64},{96,112},{112,96},{1... | collective-permute-start | bytes 688136 | tf_op jit(solution)/shard_map/ppermute | solution.py:95
  50.5 12.1 %collective-permute-start.17 = (bf16[64,1792]{1,0:T(8,128)(2,1)S(1)}, bf16[64,1792]{1,0:T(8,128)(2,1)S(1)}, u32[]{:S(2)}, u32[]{:S(2)}) collective-permute-start(bf16[64,1792]{1,0:T(8,128)(2,1)S(1)} %get-tuple-element.44.refs_9_.refs_4_), channel_id=1, source_target_pairs={{0,224},{16,240},{32,0},{48,16},{64,32},{80,48},{96,64},{112,80},{... | collective-permute-start | bytes 688136 | tf_op jit(solution)/shard_map/ppermute | solution.py:87
  60.1 17.8 %collective-permute-start.15 = (bf16[512,896]{1,0:T(8,128)(2,1)}, bf16[512,896]{1,0:T(8,128)(2,1)}, u32[]{:S(2)}, u32[]{:S(2)}) collective-permute-start(bf16[512,896]{1,0:T(8,128)(2,1)} %get-tuple-element.46), channel_id=1, source_target_pairs={{0,1},{1,0},{2,3},{3,2},{4,5},{5,4},{6,7},{7,6},{8,9},{9,8},{10,11... | collective-permute-start | bytes 2752520 | tf_op jit(solution)/shard_map/ppermute | solution.py:373
  68.8 10.6 %collective-permute-start.18 = (bf16[512,896]{1,0:T(8,128)(2,1)}, bf16[512,896]{1,0:T(8,128)(2,1)}, u32[]{:S(2)}, u32[]{:S(2)}) collective-permute-start(bf16[512,896]{1,0:T(8,128)(2,1)} %shard_map.97), channel_id=1, source_target_pairs={{0,1},{1,0},{2,3},{3,2},{4,5},{5,4},{6,7},{7,6},{8,9},{9,8},{10,11... | collective-permute-start | bytes 2752520 | tf_op jit(solution)/shard_map/ppermute | solution.py:376
  69.2 7.5 %collective-permute-start.19 = (bf16[512,256]{1,0:T(8,128)(2,1)S(1)}, bf16[512,256]{1,0:T(8,128)(2,1)S(1)}, u32[]{:S(2)}, u32[]{:S(2)}) collective-permute-start(bf16[512,256]{1,0:T(8,128)(2,1)S(1)} %dynamic-slice_convert_fusion.refs_9_), channel_id=1, source_target_pairs={{0,16},{16,0},{32,48},{48,32},{64,80},{80,64},{96,112},{112,96},{1... | collective-permute-start | bytes 786440 | tf_op jit(solution)/shard_map/ppermute | solution.py:367
  82.5 32.0 %all-to-all-start.1 = ((bf16[8,128,896]{2,1,0:T(8,128)(2,1)}), bf16[8,128,896]{2,1,0:T(8,128)(2,1)S(1)}, u32[]{:S(2)}, u32[]{:S(2)}) async-start(bf16[8,128,896]{2,1,0:T(8,128)(2,1)} %bitcast.18), calls=%async_computation.1 | async-start | bytes 3670016 | tf_op jit(solution)/shard_map/all_to_all | solution.py:63
  88.5 8.7 %collective-permute-start.20 = (f32[256,256]{1,0:T(8,128)S(1)}, f32[256,256]{1,0:T(8,128)S(1)}, u32[]{:S(2)}, u32[]{:S(2)}) collective-permute-start(f32[256,256]{1,0:T(8,128)S(1)} %constant_dynamic-slice_fusion.2), channel_id=1, source_target_pairs={{0,32},{16,48},{32,0},{48,16},{64,96},{80,112},{96,64},{112,80},{1... | collective-permute-start | bytes 786440 | tf_op jit(solution)/shard_map/ppermute | solution.py:367
  97.3 9.8 %collective-permute-start.21 = (f32[128,256]{1,0:T(8,128)S(1)}, f32[128,256]{1,0:T(8,128)S(1)}, u32[]{:S(2)}, u32[]{:S(2)}) collective-permute-start(f32[128,256]{1,0:T(8,128)S(1)} %constant_dynamic-slice_fusion.1), channel_id=1, source_target_pairs={{0,64},{16,80},{32,96},{48,112},{64,0},{80,16},{96,32},{112,48},{1... | collective-permute-start | bytes 393224 | tf_op jit(solution)/shard_map/ppermute | solution.py:367
  107.1 12.6 %collective-permute-start.22 = (f32[64,256]{1,0:T(8,128)S(1)}, f32[64,256]{1,0:T(8,128)S(1)}, u32[]{:S(2)}, u32[]{:S(2)}) collective-permute-start(f32[64,256]{1,0:T(8,128)S(1)} %constant_dynamic-slice_fusion), channel_id=1, source_target_pairs={{0,128},{16,144},{32,160},{48,176},{64,192},{80,208},{96,224},{112... | collective-permute-start | bytes 196616 | tf_op jit(solution)/shard_map/ppermute | solution.py:367
  116.0 36.0 %all-to-all-start.2 = ((bf16[8,128,896]{2,1,0:T(8,128)(2,1)}), bf16[8,128,896]{2,1,0:T(8,128)(2,1)S(1)}, u32[]{:S(2)}, u32[]{:S(2)}) async-start(bf16[8,128,896]{2,1,0:T(8,128)(2,1)} %bitcast.17), calls=%async_computation.2 | async-start | bytes 3670016 | tf_op jit(solution)/shard_map/all_to_all | solution.py:63
  119.7 6.8 %collective-permute-start.23 = (bf16[64,256]{1,0:T(8,128)(2,1)S(1)}, bf16[64,256]{1,0:T(8,128)(2,1)S(1)}, u32[]{:S(2)}, u32[]{:S(2)}) collective-permute-start(bf16[64,256]{1,0:T(8,128)(2,1)S(1)} %get-tuple-element.54), channel_id=1, source_target_pairs={{0,128},{16,144},{32,160},{48,176},{64,192},{80,208},{96,224},{112... | collective-permute-start | bytes 98312 | tf_op jit(solution)/shard_map/ppermute | solution.py:385
  126.5 8.5 %collective-permute-start.24 = (bf16[128,256]{1,0:T(8,128)(2,1)S(1)}, bf16[128,256]{1,0:T(8,128)(2,1)S(1)}, u32[]{:S(2)}, u32[]{:S(2)}) collective-permute-start(bf16[128,256]{1,0:T(8,128)(2,1)S(1)} %pad_maximum_fusion.4), channel_id=1, source_target_pairs={{0,64},{16,80},{32,96},{48,112},{64,0},{80,16},{96,32},{112,48},{1... | collective-permute-start | bytes 196616 | tf_op jit(solution)/shard_map/ppermute | solution.py:385
  135.0 4.7 %collective-permute-start.25 = (bf16[256,256]{1,0:T(8,128)(2,1)S(1)}, bf16[256,256]{1,0:T(8,128)(2,1)S(1)}, u32[]{:S(2)}, u32[]{:S(2)}) collective-permute-start(bf16[256,256]{1,0:T(8,128)(2,1)S(1)} %pad_maximum_fusion.3), channel_id=1, source_target_pairs={{0,32},{16,48},{32,0},{48,16},{64,96},{80,112},{96,64},{112,80},{1... | collective-permute-start | bytes 393224 | tf_op jit(solution)/shard_map/ppermute | solution.py:385
  139.7 5.9 %collective-permute-start.26 = (bf16[512,256]{1,0:T(8,128)(2,1)S(1)}, bf16[512,256]{1,0:T(8,128)(2,1)S(1)}, u32[]{:S(2)}, u32[]{:S(2)}) collective-permute-start(bf16[512,256]{1,0:T(8,128)(2,1)S(1)} %pad_maximum_fusion.1), channel_id=1, source_target_pairs={{0,16},{16,0},{32,48},{48,32},{64,80},{80,64},{96,112},{112,96},{1... | collective-permute-start | bytes 786440 | tf_op jit(solution)/shard_map/ppermute | solution.py:385
  145.6 6.3 %collective-permute-start.27 = (bf16[1024,256]{1,0:T(8,128)(2,1)S(1)}, bf16[1024,256]{1,0:T(8,128)(2,1)S(1)}, u32[]{:S(2)}, u32[]{:S(2)}) collective-permute-start(bf16[1024,256]{1,0:T(8,128)(2,1)S(1)} %constant_dynamic-update-slice_fusion.own_acts_ref), channel_id=1, source_target_pairs={{0,1},{1,0},{2,3},{3,2},{4,5},{5,4},{6,7},{7,6},{8,9},{9,8},{10,11... | collective-permute-start | bytes 1572872 | tf_op jit(solution)/shard_map/ppermute | solution.py:386
  (30 other events, 321.2 us)
